TPU v7x, 256 devices: a whole 4x4x8 slice. The times are simulated.
256 devices in a mesh: row: 16 (over x, z_hi, core), col: 16 (over y, z_lo).
Axes of the slice: x: 4, y: 4, z: 8 (z_hi: 2, z_lo: 4; z = z_hi * 4 + z_lo), core: 2. Of those that a mesh axis runs over, the one named last changes fastest.
Arguments:
- feats_one: bfloat16 [32768, 1536], P(('row', 'col')), may hold values from -4 to 4
- feats_two: bfloat16 [32768, 1536], P(('col', 'row')), may hold values from -4 to 4
- w_first: bfloat16 [1536, 512], replicated, may hold values from -0.15625 to 0.15625
- w_second: bfloat16 [512, 128], replicated, may hold values from -0.25 to 0.25
Outputs:
- mapped: float32 [32768, 128], P(('row', 'col'))
All inputs are finite; a program needn't handle non-finite values.
Results may differ from a plain program's by a relative error of at most 0.0022.
Values may be sent and summed in bfloat16 or wider, within the bound.
No kernel may reach another device: no remote copies, remote signals or barrier semaphores. Data moves between devices by JAX's collectives and lax.ppermute only.
A program may use at most 64 MiB of HBM per device.

v0:
```python
import jax
import jax.numpy as jnp
from jax import lax
from jax.sharding import PartitionSpec as P

SWEEPS = 3


def first_layer(feats, w_first):
    return jax.nn.relu(jnp.dot(feats, w_first, preferred_element_type=jnp.float32)).astype(
        jnp.bfloat16
    )


def second_layer(hidden, w_second):
    plain = jnp.dot(hidden, w_second, preferred_element_type=jnp.float32).astype(jnp.bfloat16)
    wide = plain.astype(jnp.float32)
    unit = (wide / jnp.sqrt(jnp.sum(wide * wide, axis=1, keepdims=True) + 1e-06)).astype(
        jnp.bfloat16
    )
    return (plain, unit)


def on_device(feats_one, feats_two, w_first, w_second):
    plain_one, unit_one = second_layer(first_layer(feats_one, w_first), w_second)
    units_left = lax.all_gather(unit_one, "col", axis=0, tiled=True)
    plain_two, unit_two = second_layer(first_layer(feats_two, w_first), w_second)
    plain_right, units_right = (
        lax.all_gather(plain_two, "row", axis=0, tiled=True),
        lax.all_gather(unit_two, "row", axis=0, tiled=True),
    )
    stored = jnp.exp(20.0 * jnp.dot(units_left, units_right.T, preferred_element_type=jnp.float32))

    def tile():
        return stored

    col_scale = jnp.ones((units_right.shape[0],), jnp.float32)
    row_scale = jnp.ones((units_left.shape[0],), jnp.float32)
    for sweep in range(SWEEPS):
        partial_rows = jnp.dot(tile(), col_scale, precision=lax.Precision.HIGHEST)
        row_scale = 1.0 / lax.psum(partial_rows, "col")
        partial_cols = jnp.dot(row_scale, tile(), precision=lax.Precision.HIGHEST)
        col_scale = 1.0 / lax.psum(partial_cols, "row")
    kernel = tile()
    scaled = (kernel * col_scale[None, :]).astype(jnp.bfloat16)
    rows_here = units_left.shape[0] // lax.axis_size("col")
    partial_maps = jnp.dot(scaled, plain_right, preferred_element_type=jnp.float32)
    summed = lax.psum(partial_maps, "col")
    weighted = row_scale[:, None] * summed
    return lax.dynamic_slice_in_dim(weighted, lax.axis_index("col") * rows_here, rows_here, 0)


def solution(mesh):
    in_specs = (P(("row", "col"), None), P(("col", "row"), None), P(), P())
    out_specs = P(("row", "col"), None)
    return jax.shard_map(
        on_device, mesh=mesh, in_specs=in_specs, out_specs=out_specs, check_vma=False
    )
```

profile of v0, /device:TPU:2, one launch (start us, length us, event | category | flops | bytes accessed | tf_op | source)
XLA Modules:
  0.0 650.1 jit_solution(12145773088619303128)
XLA Ops:
  6.5 0.0 copy-start
  6.5 0.0 all-reduce.2.cloned.1.call-start
  6.5 1.4 copy-done
  7.9 1.6 fusion.11
  9.6 33.6 %all_gather.11 = bf16[2048,128]{0,1:T(8,128)(2,1)S(1)} all-gather(bf16[128,128]{0,1:T(8,128)(2,1)S(1)} %get-tuple-element.8), channel_id=1, replica_groups=mesh['row'=16,'col'=16] {'row'}, dimensions={0}, use_global_device_ids=true | all-gather | bytes 557056 | tf_op jit(solution)/shard_map/all_gather | solution.py:29
  43.2 1.6 multiply_reduce_fusion
  44.8 46.0 %all_gather.9 = bf16[2048,128]{0,1:T(8,128)(2,1)S(1)} all-gather(bf16[128,128]{0,1:T(8,128)(2,1)S(1)} %divide_convert_fusion), channel_id=1, replica_groups=mesh['row'=16,'col'=16] {'col'}, dimensions={0}, use_global_device_ids=true | all-gather | bytes 557056 | tf_op jit(solution)/shard_map/all_gather | solution.py:26
  90.8 29.0 %all_gather.10 = bf16[2048,128]{0,1:T(8,128)(2,1)S(1)} all-gather(bf16[128,128]{0,1:T(8,128)(2,1)S(1)} %fusion.12), channel_id=1, replica_groups=mesh['row'=16,'col'=16] {'row'}, dimensions={0}, use_global_device_ids=true | all-gather | bytes 557056 | tf_op jit(solution)/shard_map/all_gather | solution.py:30
  119.8 2.4 multiply_exponential_fusion
  122.2 0.0 copy-start.1
  122.2 5.7 copy-done.1
  127.9 25.5 %fusion.13 = f32[1,2048]{1,0:T(1,128)S(1)} fusion(f32[2048,2048]{1,0:T(8,128)S(1)} %multiply_exponential_fusion), kind=kOutput, calls=%fused_computation.22 | convolution fusion | flops 50331648 | bytes 16785408 | tf_op jit(solution)/shard_map/dot_general | solution.py:40
  153.5 40.0 %psum.49 = f32[2048]{0:T(1024)S(1)} all-reduce(f32[2048]{0:T(1024)S(1)} %bitcast.33), channel_id=1, replica_groups=mesh['row'=16,'col'=16] {'col'}, use_global_device_ids=true, to_apply=%region_2.3 | all-reduce | flops 2048 | bytes 16384 | tf_op jit(solution)/shard_map/psum | solution.py:41
  193.5 11.5 %fusion.18 = f32[1,2048]{1,0:T(1,128)S(1)} fusion(f32[2048,1]{0,1:T(1,128)S(1)} %bitcast.35, f32[2048,2048]{1,0:T(8,128)} %copy-done.1), kind=kOutput, calls=%fused_computation.35 | convolution fusion | flops 50331648 | bytes 16793600 | tf_op jit(solution)/shard_map/dot_general | solution.py:42
  205.0 38.4 %psum.50 = f32[2048]{0:T(1024)S(1)} all-reduce(f32[2048]{0:T(1024)S(1)} %bitcast.36), channel_id=1, replica_groups=mesh['row'=16,'col'=16] {'row'}, use_global_device_ids=true, to_apply=%region_3.4 | all-reduce | flops 2048 | bytes 16384 | tf_op jit(solution)/shard_map/psum | solution.py:43
  243.4 17.5 %fusion.19 = f32[1,2048]{1,0:T(1,128)S(1)} fusion(f32[2048,2048]{1,0:T(8,128)} %copy-done.1, f32[2048,1]{0,1:T(1,128)S(1)} %bitcast.37), kind=kOutput, calls=%fused_computation.36 | convolution fusion | flops 50331648 | bytes 16793600 | tf_op jit(solution)/shard_map/dot_general | solution.py:40
  261.0 39.4 %psum.51 = f32[2048]{0:T(1024)S(1)} all-reduce(f32[2048]{0:T(1024)S(1)} %bitcast.31), channel_id=1, replica_groups=mesh['row'=16,'col'=16] {'col'}, use_global_device_ids=true, to_apply=%region_4.5 | all-reduce | flops 2048 | bytes 16384 | tf_op jit(solution)/shard_map/psum | solution.py:41
  300.4 11.5 %fusion.20 = f32[1,2048]{1,0:T(1,128)S(1)} fusion(f32[2048,1]{0,1:T(1,128)S(1)} %bitcast.38, f32[2048,2048]{1,0:T(8,128)} %copy-done.1), kind=kOutput, calls=%fused_computation.37 | convolution fusion | flops 50331648 | bytes 16793600 | tf_op jit(solution)/shard_map/dot_general | solution.py:42
  311.9 40.4 %psum.52 = f32[2048]{0:T(1024)S(1)} all-reduce(f32[2048]{0:T(1024)S(1)} %bitcast.39), channel_id=1, replica_groups=mesh['row'=16,'col'=16] {'row'}, use_global_device_ids=true, to_apply=%region_5.6 | all-reduce | flops 2048 | bytes 16384 | tf_op jit(solution)/shard_map/psum | solution.py:43
  352.3 17.5 %fusion.21 = f32[1,2048]{1,0:T(1,128)S(1)} fusion(f32[2048,2048]{1,0:T(8,128)} %copy-done.1, f32[2048,1]{0,1:T(1,128)S(1)} %bitcast.40), kind=kOutput, calls=%fused_computation.38 | convolution fusion | flops 50331648 | bytes 16793600 | tf_op jit(solution)/shard_map/dot_general | solution.py:40
  369.8 39.6 %psum.53 = f32[2048]{0:T(1024)S(1)} all-reduce(f32[2048]{0:T(1024)S(1)} %bitcast.32), channel_id=1, replica_groups=mesh['row'=16,'col'=16] {'col'}, use_global_device_ids=true, to_apply=%region_6.7 | all-reduce | flops 2048 | bytes 16384 | tf_op jit(solution)/shard_map/psum | solution.py:41
  409.4 11.5 %fusion.22 = f32[1,2048]{1,0:T(1,128)S(1)} fusion(f32[2048,1]{0,1:T(1,128)S(1)} %bitcast.34, f32[2048,2048]{1,0:T(8,128)} %copy-done.1), kind=kOutput, calls=%fused_computation.39 | convolution fusion | flops 50331648 | bytes 16793600 | tf_op jit(solution)/shard_map/dot_general | solution.py:42
  420.9 43.6 %psum.54 = f32[2048]{0:T(1024)S(1)} all-reduce(f32[2048]{0:T(1024)S(1)} %bitcast.41), channel_id=1, replica_groups=mesh['row'=16,'col'=16] {'row'}, use_global_device_ids=true, to_apply=%region_7.8 | all-reduce | flops 2048 | bytes 16384 | tf_op jit(solution)/shard_map/psum | solution.py:43
  464.5 9.1 %fusion = f32[2048,128]{1,0:T(8,128)} fusion(bf16[2048,128]{0,1:T(8,128)(2,1)S(1)} %all_gather.11, f32[2048,2048]{1,0:T(8,128)} %copy-done.1, f32[2048]{0:T(1024)S(1)} %broadcast_divide_fusion.5), kind=kOutput, calls=%fused_computation.2 | convolution fusion | flops 1082130432 | bytes 18358272 | tf_op jit(solution)/shard_map/dot_general | solution.py:47
  473.7 0.0 all-reduce.2.cloned.1.call-update
  473.7 0.1 dynamic-slice
  473.8 167.5 %all-reduce.2.cloned.1.call-done = f32[2048,128]{1,0:T(8,128)} async-done(((f32[2048,128]{1,0:T(8,128)}), f32[2048,128]{1,0:T(8,128)}) %all-reduce.2.cloned.1.call-update) | async-done | bytes 1048592 | tf_op jit(solution)/shard_map/psum | solution.py:48
  641.3 1.6 dynamic-slice_multiply_fusion
  (10 shorter events, 0.1 us)
Async XLA Ops:
  6.5 1.4 copy-start
  6.5 634.7 %all-reduce.2.cloned.1.call-start = ((), (), s32[]{:S(2)}) async-start(), calls=%async_computation | async-start | bytes 2097152 | tf_op jit(solution)/shard_map/psum | solution.py:48
  122.2 5.7 copy-start.1
Sparse Core Ops, SparseCore 0:
  473.8 167.4 all-reduce.1
where the time goes:
time: 660 us; the launch traced here: 650 us
  blocking collectives  350 us (53%)
  waiting for transfers between devices  168 us (25%)
  matrix products  110 us (17%)
  between operations  14 us (2%)
  local copies, waits for them, and re-layouts  7.19 us (1%)
    psum x1, waiting for transfers between devices, on_device(): summed = lax.psum(partial_maps, 'col')  168 us
    psum x3, blocking collectives, on_device(): col_scale = 1.0 / lax.psum(partial_cols, 'row')  122 us
    psum x3, blocking collectives, on_device(): row_scale = 1.0 / lax.psum(partial_rows, 'col')  119 us
    dot_general x3, matrix products, on_device(): partial_rows = jnp.dot(tile(), col_scale, precision=lax.Precision.HIGHEST)  60.6 us
    all_gather x1, blocking collectives, on_device(): units_left = lax.all_gather(unit_one, 'col', axis=0, tiled=True)  46 us
    dot_general x3, matrix products, on_device(): partial_cols = jnp.dot(row_scale, tile(), precision=lax.Precision.HIGHEST)  34.4 us
    all_gather x1, blocking collectives, on_device(): lax.all_gather(plain_two, 'row', axis=0, tiled=True)  33.6 us
    all_gather x1, blocking collectives, on_device(): lax.all_gather(unit_two, 'row', axis=0, tiled=True)  29 us
  transfers between devices with their start and end apart: 1, of which 1 were waited for; matrix products, arithmetic and copies ran while one was open for 0% of the time, Pallas kernels for 0%

commit v1 on v0

v1 whole, which is shorter than its diff:
```python
import math

import jax
import jax.numpy as jnp
from jax import lax
from jax.experimental import pallas as pl
from jax.experimental.pallas import tpu as pltpu
from jax.sharding import Mesh
from jax.sharding import PartitionSpec as P

SWEEPS = 3
PEERS = 16
LANES = 128
SIDE = PEERS * LANES
EXPONENT = 20.0 * math.log2(math.e)
AXES = ("xh", "xl", "zh", "c", "yh", "yl", "zm", "zl")
SAME_ROWS = ("xh", "xl", "yl", "c")
SAME_COLS = ("yh", "zh", "zm", "zl")
F32, BF16 = jnp.float32, jnp.bfloat16
VMEM_LIMIT = 40 * 2**20


def unit_of(plain):
    wide = plain.astype(F32)
    return (wide / jnp.sqrt(jnp.sum(wide * wide, axis=1, keepdims=True) + 1e-06)).astype(BF16)


def embed_kernel(one_ref, two_ref, first_ref, second_ref, unit_ref, plain_ref):
    feats = jnp.concatenate([one_ref[...], two_ref[...]], axis=0)
    hidden = jnp.maximum(jnp.dot(feats, first_ref[...], preferred_element_type=F32), 0.0).astype(BF16)
    plain = jnp.dot(hidden, second_ref[...], preferred_element_type=F32).astype(BF16)
    unit = unit_of(plain[:LANES])
    for peer in range(PEERS):
        unit_ref[peer] = unit
        plain_ref[peer] = plain[LANES:]


def row_totals(parts):
    return jnp.sum(parts.T, axis=0, keepdims=True)


def fill(out_ref, lines_ref):
    lines = lines_ref[...]
    for peer in range(PEERS):
        out_ref[peer] = lines


def tile_kernel(left_ref, plain_ref, tile_ref, sums_ref, units_ref, lines_ref):
    units_ref[...] = unit_of(plain_ref[...].reshape(SIDE, LANES))

    @pl.loop(0, PEERS // 2)
    def _(step):
        left = left_ref[pl.ds(2 * step, 2)].reshape(2 * LANES, LANES)
        rows = pl.ds(pl.multiple_of(step * 2 * LANES, 2 * LANES), 2 * LANES)
        parts = jnp.zeros((2 * LANES, LANES), F32)
        for chunk in range(PEERS // 2):
            right = units_ref[chunk * 2 * LANES : (chunk + 1) * 2 * LANES]
            dots = lax.dot_general(left, right, (((1,), (1,)), ((), ())), preferred_element_type=F32)
            block = jnp.exp2(dots * EXPONENT)
            tile_ref[rows, chunk * 2 * LANES : (chunk + 1) * 2 * LANES] = block
            parts += block[:, :LANES] + block[:, LANES:]
        lines_ref[pl.ds(2 * step, 1)] = row_totals(parts[:LANES])
        lines_ref[pl.ds(2 * step + 1, 1)] = row_totals(parts[LANES:])

    fill(sums_ref, lines_ref)


def scale_of(got_ref):
    total = got_ref[0]
    for peer in range(1, PEERS):
        total += got_ref[peer]
    return 1.0 / total


def cols_kernel(got_ref, tile_ref, sums_ref, scale_ref, lines_ref):
    scale_ref[...] = scale_of(got_ref)
    zero = tuple(jnp.zeros((8, LANES), F32) for _ in range(PEERS))

    def step(block, parts):
        rows = pl.ds(pl.multiple_of(block * LANES, LANES), LANES)
        factor = jnp.broadcast_to(scale_ref[pl.ds(block, 1)], (LANES, LANES)).T
        out = []
        for chunk in range(PEERS):
            product = tile_ref[rows, chunk * LANES : (chunk + 1) * LANES] * factor
            out.append(parts[chunk] + jnp.sum(product.reshape(LANES // 8, 8, LANES), axis=0))
        return tuple(out)

    parts = lax.fori_loop(0, PEERS, step, zero)
    for chunk in range(PEERS):
        lines_ref[chunk : chunk + 1] = jnp.sum(parts[chunk], axis=0, keepdims=True)
    fill(sums_ref, lines_ref)


def rows_kernel(got_ref, tile_ref, sums_ref, lines_ref):
    scale = scale_of(got_ref)

    @pl.loop(0, PEERS)
    def _(block):
        rows = pl.ds(pl.multiple_of(block * LANES, LANES), LANES)
        parts = tile_ref[rows, :LANES] * scale[:1]
        for chunk in range(1, PEERS):
            parts += tile_ref[rows, chunk * LANES : (chunk + 1) * LANES] * scale[chunk : chunk + 1]
        lines_ref[pl.ds(block, 1)] = row_totals(parts)

    fill(sums_ref, lines_ref)


def map_kernel(got_ref, tile_ref, plain_ref, out_ref):
    scale = scale_of(got_ref)
    wide = jnp.concatenate([scale[chunk : chunk + 1] for chunk in range(PEERS)], axis=1)
    plain = plain_ref[...].reshape(SIDE, LANES)

    @pl.loop(0, PEERS // 2)
    def _(step):
        rows = pl.ds(pl.multiple_of(step * 2 * LANES, 2 * LANES), 2 * LANES)
        scaled = (tile_ref[rows, :] * wide).astype(BF16)
        part = jnp.dot(scaled, plain, preferred_element_type=F32)
        out_ref[pl.ds(2 * step, 2)] = part.reshape(2, LANES, LANES)


def finish_kernel(got_ref, scale_ref, out_ref):
    total = got_ref[0].astype(F32)
    for peer in range(1, PEERS):
        total += got_ref[peer].astype(F32)
    out_ref[...] = total * jnp.broadcast_to(scale_ref[...], (LANES, LANES)).T


def call(kernel, outs, *args, scratch=(), flops=0, exps=0):
    moved = sum(math.prod(a.shape) * a.dtype.itemsize for a in args)
    return pl.pallas_call(
        kernel,
        out_shape=outs,
        scratch_shapes=scratch,
        compiler_params=pltpu.CompilerParams(vmem_limit_bytes=VMEM_LIMIT),
        cost_estimate=pl.CostEstimate(flops=flops, bytes_accessed=moved, transcendentals=exps),
    )(*args)


def near(array):
    return pltpu.with_memory_space_constraint(array, pltpu.VMEM)


def exchange(array, axes):
    return lax.all_to_all(array, axes, 0, 0)


def on_device(feats_one, feats_two, w_first, w_second):
    spread = jax.ShapeDtypeStruct((PEERS, LANES, LANES), BF16)
    vectors = jax.ShapeDtypeStruct((PEERS, PEERS, LANES), F32)
    lines = pltpu.VMEM((PEERS, LANES), F32)
    unit_one, plain_two = call(embed_kernel, (spread, spread), feats_one, feats_two, w_first, w_second)
    plains = exchange(plain_two, SAME_COLS)
    units = exchange(unit_one, SAME_ROWS)
    tile, sums = call(
        tile_kernel,
        (pltpu.VMEM((SIDE, SIDE), F32), vectors),
        units,
        plains,
        scratch=(pltpu.VMEM((SIDE, LANES), BF16), lines),
    )
    tile = near(tile)
    for sweep in range(SWEEPS):
        if sweep:
            sums = call(rows_kernel, vectors, sums, tile, scratch=(lines,))
        sums = exchange(sums, SAME_ROWS)
        sums, row_scale = call(
            cols_kernel,
            (vectors, jax.ShapeDtypeStruct((PEERS, LANES), F32)),
            sums,
            tile,
            scratch=(lines,),
        )
        sums = exchange(sums, SAME_COLS)
    parts = call(map_kernel, jax.ShapeDtypeStruct((PEERS, LANES, LANES), F32), sums, tile, plains)
    parts = exchange(parts, SAME_ROWS)
    own = lax.dynamic_slice_in_dim(row_scale, lax.axis_index(SAME_ROWS), 1, 0)
    return call(finish_kernel, jax.ShapeDtypeStruct((LANES, LANES), F32), parts, own)


def solution(mesh):
    fine = Mesh(mesh.devices.reshape((2,) * 8), AXES)
    row, col = AXES[:4], AXES[4:]
    return jax.shard_map(
        on_device,
        mesh=fine,
        in_specs=(P(row + col, None), P(col + row, None), P(), P()),
        out_specs=P(row + col, None),
        check_vma=False,
    )
```

time: 660 us -> 179 us (0.27)
  the two profiles are of different devices: /device:TPU:2 before, /device:TPU:1 now
where the time goes in v1:
time: 179 us; the launch traced here: 178 us
  blocking collectives  119 us (66%)
  Pallas kernels  33.5 us (19%)
  waiting for transfers between devices  15.1 us (8%)
  starting transfers between devices  5.17 us (3%)
  local copies, waits for them, and re-layouts  4.99 us (3%)
    all_to_all x8, blocking collectives, exchange(): return lax.all_to_all(array, axes, 0, 0)  119 us
    pallas_call x9, Pallas kernels, call(): pl.pallas_call(kernel, out_shape=outs, scratch_shapes=scratch, compiler_p...  33.5 us
    all_to_all x1, waiting for transfers between devices, exchange(): return lax.all_to_all(array, axes, 0, 0)  15.1 us
    all_to_all x1, starting transfers between devices, exchange(): return lax.all_to_all(array, axes, 0, 0)  5.17 us
    unnamed x8, local copies, waits for them, and re-layouts  4.3 us
  transfers between devices with their start and end apart: 1, of which 1 were waited for; matrix products, arithmetic and copies ran while one was open for 0% of the time, Pallas kernels for 0%

profile of v1, /device:TPU:1, one launch (start us, length us, event | category | flops | bytes accessed | tf_op | source)
XLA Modules:
  0.0 177.7 jit_solution(133779880320628226)
XLA Ops:
  0.0 0.0 copy-start
  0.0 1.4 copy-done
  1.4 0.0 copy-start.1
  1.4 1.0 copy-done.1
  2.4 0.0 copy-start.2
  2.4 1.0 copy-done.2
  3.4 0.0 copy-start.3
  3.4 0.9 copy-done.3
  4.3 0.8 shard_map.46
  5.1 16.4 %all_to_all.45.left_ref = bf16[16,128,128]{2,1,0:T(8,128)(2,1)} all-to-all(bf16[16,128,128]{2,1,0:T(8,128)(2,1)S(1)} %get-tuple-element.13), channel_id=1, replica_groups=mesh['xh'=2,'xl'=2,'zh'=2,'c'=2,'yh'=2,'yl'=2,'zm'=2,'zl'=2] {'xh','xl',..., dimensions={0} | all-to-all | bytes 1048576 | tf_op jit(solution)/shard_map/all_to_all | solution.py:144
  21.5 25.1 %all_to_all.46.plain_ref = bf16[16,128,128]{2,1,0:T(8,128)(2,1)} all-to-all(bf16[16,128,128]{2,1,0:T(8,128)(2,1)S(1)} %get-tuple-element.14), channel_id=1, replica_groups=mesh['xh'=2,'xl'=2,'zh'=2,'c'=2,'yh'=2,'yl'=2,'zm'=2,'zl'=2] {'yh','zh',..., dimensions={0} | all-to-all | bytes 1048576 | tf_op jit(solution)/shard_map/all_to_all | solution.py:144
  46.6 6.6 %shard_map.47 = (f32[2048,2048]{1,0:T(8,128)S(1)}, f32[16,16,128]{2,1,0:T(8,128)}) custom-call(bf16[16,128,128]{2,1,0:T(8,128)(2,1)} %all_to_all.45.left_ref, bf16[16,128,128]{2,1,0:T(8,128)(2,1)} %all_to_all.46.plain_ref), custom_call_target="tpu_custom_call" | custom-call | bytes 1048576 | tf_op jit(solution)/shard_map/pallas_call | solution.py:130
  53.2 13.2 %all_to_all.47.got_ref = f32[16,16,128]{2,1,0:T(8,128)} all-to-all(f32[16,16,128]{2,1,0:T(8,128)} %get-tuple-element.15), channel_id=1, replica_groups=mesh['xh'=2,'xl'=2,'zh'=2,'c'=2,'yh'=2,'yl'=2,'zm'=2,'zl'=2] {'xh','xl',..., dimensions={0} | all-to-all | bytes 262144 | tf_op jit(solution)/shard_map/all_to_all | solution.py:144
  66.3 4.0 %shard_map.48 = (f32[16,16,128]{2,1,0:T(8,128)}, f32[16,128]{1,0:T(8,128)}) custom-call(f32[16,16,128]{2,1,0:T(8,128)} %all_to_all.47.got_ref, f32[2048,2048]{1,0:T(8,128)S(1)} %get-tuple-element.16.tile_ref), custom_call_target="tpu_custom_call" | custom-call | bytes 16908288 | tf_op jit(solution)/shard_map/pallas_call | solution.py:130
  70.3 13.9 %all_to_all.48.got_ref = f32[16,16,128]{2,1,0:T(8,128)} all-to-all(f32[16,16,128]{2,1,0:T(8,128)} %get-tuple-element.17), channel_id=1, replica_groups=mesh['xh'=2,'xl'=2,'zh'=2,'c'=2,'yh'=2,'yl'=2,'zm'=2,'zl'=2] {'yh','zh',..., dimensions={0} | all-to-all | bytes 262144 | tf_op jit(solution)/shard_map/all_to_all | solution.py:144
  84.2 4.0 %shard_map.49 = f32[16,16,128]{2,1,0:T(8,128)} custom-call(f32[16,16,128]{2,1,0:T(8,128)} %all_to_all.48.got_ref, f32[2048,2048]{1,0:T(8,128)S(1)} %get-tuple-element.16.tile_ref), custom_call_target="tpu_custom_call" | custom-call | bytes 16908288 | tf_op jit(solution)/shard_map/pallas_call | solution.py:130
  88.2 12.3 %all_to_all.49.got_ref = f32[16,16,128]{2,1,0:T(8,128)} all-to-all(f32[16,16,128]{2,1,0:T(8,128)} %shard_map.49), channel_id=1, replica_groups=mesh['xh'=2,'xl'=2,'zh'=2,'c'=2,'yh'=2,'yl'=2,'zm'=2,'zl'=2] {'xh','xl',..., dimensions={0} | all-to-all | bytes 262144 | tf_op jit(solution)/shard_map/all_to_all | solution.py:144
  100.5 3.9 %shard_map.50 = (f32[16,16,128]{2,1,0:T(8,128)}, f32[16,128]{1,0:T(8,128)}) custom-call(f32[16,16,128]{2,1,0:T(8,128)} %all_to_all.49.got_ref, f32[2048,2048]{1,0:T(8,128)S(1)} %get-tuple-element.16.tile_ref), custom_call_target="tpu_custom_call" | custom-call | bytes 16908288 | tf_op jit(solution)/shard_map/pallas_call | solution.py:130
  104.4 13.1 %all_to_all.50.got_ref = f32[16,16,128]{2,1,0:T(8,128)} all-to-all(f32[16,16,128]{2,1,0:T(8,128)} %get-tuple-element.18), channel_id=1, replica_groups=mesh['xh'=2,'xl'=2,'zh'=2,'c'=2,'yh'=2,'yl'=2,'zm'=2,'zl'=2] {'yh','zh',..., dimensions={0} | all-to-all | bytes 262144 | tf_op jit(solution)/shard_map/all_to_all | solution.py:144
  117.5 4.0 %shard_map.51 = f32[16,16,128]{2,1,0:T(8,128)} custom-call(f32[16,16,128]{2,1,0:T(8,128)} %all_to_all.50.got_ref, f32[2048,2048]{1,0:T(8,128)S(1)} %get-tuple-element.16.tile_ref), custom_call_target="tpu_custom_call" | custom-call | bytes 16908288 | tf_op jit(solution)/shard_map/pallas_call | solution.py:130
  121.5 11.9 %all_to_all.51.got_ref = f32[16,16,128]{2,1,0:T(8,128)} all-to-all(f32[16,16,128]{2,1,0:T(8,128)} %shard_map.51), channel_id=1, replica_groups=mesh['xh'=2,'xl'=2,'zh'=2,'c'=2,'yh'=2,'yl'=2,'zm'=2,'zl'=2] {'xh','xl',..., dimensions={0} | all-to-all | bytes 262144 | tf_op jit(solution)/shard_map/all_to_all | solution.py:144
  133.4 3.9 %shard_map.52 = (f32[16,16,128]{2,1,0:T(8,128)}, f32[16,128]{1,0:T(8,128)}) custom-call(f32[16,16,128]{2,1,0:T(8,128)} %all_to_all.51.got_ref, f32[2048,2048]{1,0:T(8,128)S(1)} %get-tuple-element.16.tile_ref), custom_call_target="tpu_custom_call" | custom-call | bytes 16908288 | tf_op jit(solution)/shard_map/pallas_call | solution.py:130
  137.4 13.1 %all_to_all.52.got_ref = f32[16,16,128]{2,1,0:T(8,128)} all-to-all(f32[16,16,128]{2,1,0:T(8,128)} %get-tuple-element.19), channel_id=1, replica_groups=mesh['xh'=2,'xl'=2,'zh'=2,'c'=2,'yh'=2,'yl'=2,'zm'=2,'zl'=2] {'yh','zh',..., dimensions={0} | all-to-all | bytes 262144 | tf_op jit(solution)/shard_map/all_to_all | solution.py:144
  150.4 5.6 %shard_map.53 = f32[16,128,128]{2,1,0:T(8,128)} custom-call(f32[16,16,128]{2,1,0:T(8,128)} %all_to_all.52.got_ref, f32[2048,2048]{1,0:T(8,128)S(1)} %get-tuple-element.16.tile_ref, bf16[16,128,128]{2,1,0:T(8,128)(2,1)} %all_to_all.46.plain_ref), custom_call_target="tpu_custom_call" | custom-call | bytes 17432576 | tf_op jit(solution)/shard_map/pallas_call | solution.py:130
  156.0 5.2 %all-to-all-start.8 = ((f32[16,128,128]{2,1,0:T(8,128)}), f32[16,128,128]{2,1,0:T(8,128)S(1)}, u32[]{:S(2)}, u32[]{:S(2)}) async-start(f32[16,128,128]{2,1,0:T(8,128)} %shard_map.53), calls=%async_computation.8 | async-start | bytes 2097152 | tf_op jit(solution)/shard_map/all_to_all | solution.py:144
  161.2 0.7 constant_dynamic-slice_fusion.scale_ref
  161.9 15.1 %all-to-all-done.8.got_ref = f32[16,128,128]{2,1,0:T(8,128)S(1)} async-done(((f32[16,128,128]{2,1,0:T(8,128)}), f32[16,128,128]{2,1,0:T(8,128)S(1)}, u32[]{:S(2)}, u32[]{:S(2)}) %all-to-all-start.8) | async-done | bytes 1048608 | tf_op jit(solution)/shard_map/all_to_all | solution.py:144
  177.0 0.7 shard_map.54
Async XLA Ops:
  0.0 1.4 copy-start
  1.4 1.0 copy-start.1
  2.4 1.0 copy-start.2
  3.4 0.9 copy-start.3
  156.0 21.0 %all-to-all-start.8 = ((f32[16,128,128]{2,1,0:T(8,128)}), f32[16,128,128]{2,1,0:T(8,128)S(1)}, u32[]{:S(2)}, u32[]{:S(2)}) async-start(f32[16,128,128]{2,1,0:T(8,128)} %shard_map.53), calls=%async_computation.8 | async-start | bytes 2097152 | tf_op jit(solution)/shard_map/all_to_all | solution.py:144

commit v2 on v1

--- a/solution.py
+++ b/solution.py
@@ -14,10 +14,10 @@
 SIDE = PEERS * LANES
 EXPONENT = 20.0 * math.log2(math.e)
 AXES = ("xh", "xl", "zh", "c", "yh", "yl", "zm", "zl")
-SAME_ROWS = ("xh", "xl", "yl", "c")
-SAME_COLS = ("yh", "zh", "zm", "zl")
+SAME_ROWS = ("xh", "xl", "yh", "yl")
+SAME_COLS = ("zh", "zm", "zl", "c")
 F32, BF16 = jnp.float32, jnp.bfloat16
-VMEM_LIMIT = 40 * 2**20
+VMEM_LIMIT = 16 * 2**20
 
 
 def unit_of(plain):
@@ -25,9 +25,19 @@
     return (wide / jnp.sqrt(jnp.sum(wide * wide, axis=1, keepdims=True) + 1e-06)).astype(BF16)
 
 
-def embed_kernel(one_ref, two_ref, first_ref, second_ref, unit_ref, plain_ref):
-    feats = jnp.concatenate([one_ref[...], two_ref[...]], axis=0)
-    hidden = jnp.maximum(jnp.dot(feats, first_ref[...], preferred_element_type=F32), 0.0).astype(BF16)
+def embed_kernel(one_hbm, two_hbm, first_hbm, second_hbm, unit_ref, plain_ref, feats_ref, first_ref, second_ref, sems):
+    copies = [
+        pltpu.make_async_copy(first_hbm, first_ref, sems.at[0]),
+        pltpu.make_async_copy(one_hbm, feats_ref.at[pl.ds(0, LANES)], sems.at[1]),
+        pltpu.make_async_copy(two_hbm, feats_ref.at[pl.ds(LANES, LANES)], sems.at[2]),
+        pltpu.make_async_copy(second_hbm, second_ref, sems.at[3]),
+    ]
+    for copy in copies:
+        copy.start()
+    for copy in copies:
+        copy.wait()
+    hidden = jnp.dot(feats_ref[...], first_ref[...], preferred_element_type=F32)
+    hidden = jnp.maximum(hidden, 0.0).astype(BF16)
     plain = jnp.dot(hidden, second_ref[...], preferred_element_type=F32).astype(BF16)
     unit = unit_of(plain[:LANES])
     for peer in range(PEERS):
@@ -125,13 +135,14 @@
     out_ref[...] = total * jnp.broadcast_to(scale_ref[...], (LANES, LANES)).T
 
 
-def call(kernel, outs, *args, scratch=(), flops=0, exps=0):
+def call(kernel, outs, *args, scratch=(), flops=0, exps=0, limit=VMEM_LIMIT, **specs):
     moved = sum(math.prod(a.shape) * a.dtype.itemsize for a in args)
     return pl.pallas_call(
         kernel,
         out_shape=outs,
+        **specs,
         scratch_shapes=scratch,
-        compiler_params=pltpu.CompilerParams(vmem_limit_bytes=VMEM_LIMIT),
+        compiler_params=pltpu.CompilerParams(vmem_limit_bytes=limit),
         cost_estimate=pl.CostEstimate(flops=flops, bytes_accessed=moved, transcendentals=exps),
     )(*args)
 
@@ -145,12 +156,28 @@
 
 
 def on_device(feats_one, feats_two, w_first, w_second):
-    spread = jax.ShapeDtypeStruct((PEERS, LANES, LANES), BF16)
-    vectors = jax.ShapeDtypeStruct((PEERS, PEERS, LANES), F32)
+    spread = pltpu.VMEM((PEERS, LANES, LANES), BF16)
+    vectors = pltpu.VMEM((PEERS, PEERS, LANES), F32)
     lines = pltpu.VMEM((PEERS, LANES), F32)
-    unit_one, plain_two = call(embed_kernel, (spread, spread), feats_one, feats_two, w_first, w_second)
-    plains = exchange(plain_two, SAME_COLS)
-    units = exchange(unit_one, SAME_ROWS)
+    rows = feats_one.shape[0] + feats_two.shape[0]
+    unit_one, plain_two = call(
+        embed_kernel,
+        (spread, spread),
+        feats_one,
+        feats_two,
+        w_first,
+        w_second,
+        in_specs=[pl.BlockSpec(memory_space=pltpu.HBM)] * 4,
+        limit=60 * 2**20,
+        scratch=(
+            pltpu.VMEM((rows, feats_one.shape[1]), BF16),
+            pltpu.VMEM(w_first.shape, BF16),
+            pltpu.VMEM(w_second.shape, BF16),
+            pltpu.SemaphoreType.DMA((4,)),
+        ),
+    )
+    plains = near(exchange(plain_two, SAME_COLS))
+    units = near(exchange(unit_one, SAME_ROWS))
     tile, sums = call(
         tile_kernel,
         (pltpu.VMEM((SIDE, SIDE), F32), vectors),
@@ -162,17 +189,11 @@
     for sweep in range(SWEEPS):
         if sweep:
             sums = call(rows_kernel, vectors, sums, tile, scratch=(lines,))
-        sums = exchange(sums, SAME_ROWS)
-        sums, row_scale = call(
-            cols_kernel,
-            (vectors, jax.ShapeDtypeStruct((PEERS, LANES), F32)),
-            sums,
-            tile,
-            scratch=(lines,),
-        )
-        sums = exchange(sums, SAME_COLS)
-    parts = call(map_kernel, jax.ShapeDtypeStruct((PEERS, LANES, LANES), F32), sums, tile, plains)
-    parts = exchange(parts, SAME_ROWS)
+        sums = near(exchange(sums, SAME_ROWS))
+        sums, row_scale = call(cols_kernel, (vectors, lines), sums, tile, scratch=(lines,))
+        sums = near(exchange(sums, SAME_COLS))
+    parts = call(map_kernel, pltpu.VMEM((PEERS, LANES, LANES), F32), sums, tile, plains)
+    parts = near(exchange(parts, SAME_ROWS))
     own = lax.dynamic_slice_in_dim(row_scale, lax.axis_index(SAME_ROWS), 1, 0)
     return call(finish_kernel, jax.ShapeDtypeStruct((LANES, LANES), F32), parts, own)
 

time: 179 us -> 162 us (0.905)
  Pallas kernels: 33.5 us -> 25.3 us
  blocking collectives: 119 us -> 114 us
  local copies, waits for them, and re-layouts: 4.99 us -> 0.01 us
  waiting for transfers between devices: 15.1 us -> 18.5 us
    pallas_call x9, Pallas kernels: 33.5 us -> 25.3 us  [call(): pl.pallas_call(kernel, out_shape=outs, **specs, scratch_shapes=scratch, c...]
    all_to_all x8, blocking collectives: 119 us -> 114 us  [exchange(): return lax.all_to_all(array, axes, 0, 0)]
    unnamed x8 -> x0, local copies, waits for them, and re-layouts: 4.3 us -> none
    all_to_all x1, waiting for transfers between devices: 15.1 us -> 18.5 us  [exchange(): return lax.all_to_all(array, axes, 0, 0)]
where the time goes in v2:
time: 162 us
  blocking collectives  114 us (70%)
  Pallas kernels  25.3 us (16%)
  waiting for transfers between devices  18.5 us (11%)
  starting transfers between devices  3.65 us (2%)
    all_to_all x8, blocking collectives, exchange(): return lax.all_to_all(array, axes, 0, 0)  114 us
    pallas_call x9, Pallas kernels, call(): pl.pallas_call(kernel, out_shape=outs, **specs, scratch_shapes=scratch, c...  25.3 us
    all_to_all x1, waiting for transfers between devices, exchange(): return lax.all_to_all(array, axes, 0, 0)  18.5 us
    all_to_all x1, starting transfers between devices, exchange(): return lax.all_to_all(array, axes, 0, 0)  3.65 us
  transfers between devices with their start and end apart: 1, of which 1 were waited for; matrix products, arithmetic and copies ran while one was open for 0% of the time, Pallas kernels for 0%

profile of v2, /device:TPU:1, one launch (start us, length us, event | category | flops | bytes accessed | tf_op | source)
XLA Modules:
  0.0 161.6 jit_solution(3723655623053832645)
XLA Ops:
  0.0 2.4 %shard_map.46 = (bf16[16,128,128]{2,1,0:T(8,128)(2,1)S(1)}, bf16[16,128,128]{2,1,0:T(8,128)(2,1)S(1)}) custom-call(bf16[128,1536]{1,0:T(8,128)(2,1)} %one_hbm.1, bf16[128,1536]{1,0:T(8,128)(2,1)} %two_hbm.1, bf16[1536,512]{1,0:T(8,128)(2,1)} %first_hbm.1, bf16[512,128]{1,0:T(8,128)(2,1)} %second_hbm.1), custom_call_target="tpu_custom_call" | custom-call | bytes 2490368 | tf_op jit(solution)/shard_map/pallas_call | solution.py:140
  2.5 17.7 %all_to_all.45.left_ref = bf16[16,128,128]{2,1,0:T(8,128)(2,1)S(1)} all-to-all(bf16[16,128,128]{2,1,0:T(8,128)(2,1)S(1)} %get-tuple-element.13), channel_id=1, replica_groups=mesh['xh'=2,'xl'=2,'zh'=2,'c'=2,'yh'=2,'yl'=2,'zm'=2,'zl'=2] {'xh','xl',..., dimensions={0} | all-to-all | bytes 1048576 | tf_op jit(solution)/shard_map/all_to_all | solution.py:155
  20.1 27.7 %all_to_all.46.plain_ref = bf16[16,128,128]{2,1,0:T(8,128)(2,1)S(1)} all-to-all(bf16[16,128,128]{2,1,0:T(8,128)(2,1)S(1)} %get-tuple-element.14), channel_id=1, replica_groups=mesh['xh'=2,'xl'=2,'zh'=2,'c'=2,'yh'=2,'yl'=2,'zm'=2,'zl'=2] {'zh','zm',..., dimensions={0} | all-to-all | bytes 1048576 | tf_op jit(solution)/shard_map/all_to_all | solution.py:155
  47.9 4.7 %shard_map.47 = (f32[2048,2048]{1,0:T(8,128)S(1)}, f32[16,16,128]{2,1,0:T(8,128)S(1)}) custom-call(bf16[16,128,128]{2,1,0:T(8,128)(2,1)S(1)} %all_to_all.45.left_ref, bf16[16,128,128]{2,1,0:T(8,128)(2,1)S(1)} %all_to_all.46.plain_ref), custom_call_target="tpu_custom_call" | custom-call | bytes 1048576 | tf_op jit(solution)/shard_map/pallas_call | solution.py:140
  52.6 10.0 %all_to_all.47.got_ref = f32[16,16,128]{2,1,0:T(8,128)S(1)} all-to-all(f32[16,16,128]{2,1,0:T(8,128)S(1)} %get-tuple-element.15), channel_id=1, replica_groups=mesh['xh'=2,'xl'=2,'zh'=2,'c'=2,'yh'=2,'yl'=2,'zm'=2,'zl'=2] {'xh','xl',..., dimensions={0} | all-to-all | bytes 262144 | tf_op jit(solution)/shard_map/all_to_all | solution.py:155
  62.6 2.8 %shard_map.48 = (f32[16,16,128]{2,1,0:T(8,128)S(1)}, f32[16,128]{1,0:T(8,128)}) custom-call(f32[16,16,128]{2,1,0:T(8,128)S(1)} %all_to_all.47.got_ref, f32[2048,2048]{1,0:T(8,128)S(1)} %get-tuple-element.16.tile_ref), custom_call_target="tpu_custom_call" | custom-call | bytes 16908288 | tf_op jit(solution)/shard_map/pallas_call | solution.py:140
  65.4 13.0 %all_to_all.48.got_ref = f32[16,16,128]{2,1,0:T(8,128)S(1)} all-to-all(f32[16,16,128]{2,1,0:T(8,128)S(1)} %get-tuple-element.17), channel_id=1, replica_groups=mesh['xh'=2,'xl'=2,'zh'=2,'c'=2,'yh'=2,'yl'=2,'zm'=2,'zl'=2] {'zh','zm',..., dimensions={0} | all-to-all | bytes 262144 | tf_op jit(solution)/shard_map/all_to_all | solution.py:155
  78.4 2.5 %shard_map.49 = f32[16,16,128]{2,1,0:T(8,128)S(1)} custom-call(f32[16,16,128]{2,1,0:T(8,128)S(1)} %all_to_all.48.got_ref, f32[2048,2048]{1,0:T(8,128)S(1)} %get-tuple-element.16.tile_ref), custom_call_target="tpu_custom_call" | custom-call | bytes 16908288 | tf_op jit(solution)/shard_map/pallas_call | solution.py:140
  80.8 10.3 %all_to_all.49.got_ref = f32[16,16,128]{2,1,0:T(8,128)S(1)} all-to-all(f32[16,16,128]{2,1,0:T(8,128)S(1)} %shard_map.49), channel_id=1, replica_groups=mesh['xh'=2,'xl'=2,'zh'=2,'c'=2,'yh'=2,'yl'=2,'zm'=2,'zl'=2] {'xh','xl',..., dimensions={0} | all-to-all | bytes 262144 | tf_op jit(solution)/shard_map/all_to_all | solution.py:155
  91.1 2.8 %shard_map.50 = (f32[16,16,128]{2,1,0:T(8,128)S(1)}, f32[16,128]{1,0:T(8,128)}) custom-call(f32[16,16,128]{2,1,0:T(8,128)S(1)} %all_to_all.49.got_ref, f32[2048,2048]{1,0:T(8,128)S(1)} %get-tuple-element.16.tile_ref), custom_call_target="tpu_custom_call" | custom-call | bytes 16908288 | tf_op jit(solution)/shard_map/pallas_call | solution.py:140
  93.9 12.6 %all_to_all.50.got_ref = f32[16,16,128]{2,1,0:T(8,128)S(1)} all-to-all(f32[16,16,128]{2,1,0:T(8,128)S(1)} %get-tuple-element.18), channel_id=1, replica_groups=mesh['xh'=2,'xl'=2,'zh'=2,'c'=2,'yh'=2,'yl'=2,'zm'=2,'zl'=2] {'zh','zm',..., dimensions={0} | all-to-all | bytes 262144 | tf_op jit(solution)/shard_map/all_to_all | solution.py:155
  106.5 2.5 %shard_map.51 = f32[16,16,128]{2,1,0:T(8,128)S(1)} custom-call(f32[16,16,128]{2,1,0:T(8,128)S(1)} %all_to_all.50.got_ref, f32[2048,2048]{1,0:T(8,128)S(1)} %get-tuple-element.16.tile_ref), custom_call_target="tpu_custom_call" | custom-call | bytes 16908288 | tf_op jit(solution)/shard_map/pallas_call | solution.py:140
  109.0 10.2 %all_to_all.51.got_ref = f32[16,16,128]{2,1,0:T(8,128)S(1)} all-to-all(f32[16,16,128]{2,1,0:T(8,128)S(1)} %shard_map.51), channel_id=1, replica_groups=mesh['xh'=2,'xl'=2,'zh'=2,'c'=2,'yh'=2,'yl'=2,'zm'=2,'zl'=2] {'xh','xl',..., dimensions={0} | all-to-all | bytes 262144 | tf_op jit(solution)/shard_map/all_to_all | solution.py:155
  119.2 2.4 %shard_map.52 = (f32[16,16,128]{2,1,0:T(8,128)S(1)}, f32[16,128]{1,0:T(8,128)S(1)}) custom-call(f32[16,16,128]{2,1,0:T(8,128)S(1)} %all_to_all.51.got_ref, f32[2048,2048]{1,0:T(8,128)S(1)} %get-tuple-element.16.tile_ref), custom_call_target="tpu_custom_call" | custom-call | bytes 16908288 | tf_op jit(solution)/shard_map/pallas_call | solution.py:140
  121.6 12.6 %all_to_all.52.got_ref = f32[16,16,128]{2,1,0:T(8,128)S(1)} all-to-all(f32[16,16,128]{2,1,0:T(8,128)S(1)} %get-tuple-element.19), channel_id=1, replica_groups=mesh['xh'=2,'xl'=2,'zh'=2,'c'=2,'yh'=2,'yl'=2,'zm'=2,'zl'=2] {'zh','zm',..., dimensions={0} | all-to-all | bytes 262144 | tf_op jit(solution)/shard_map/all_to_all | solution.py:155
  134.2 4.5 %shard_map.53 = f32[16,128,128]{2,1,0:T(8,128)} custom-call(f32[16,16,128]{2,1,0:T(8,128)S(1)} %all_to_all.52.got_ref, f32[2048,2048]{1,0:T(8,128)S(1)} %get-tuple-element.16.tile_ref, bf16[16,128,128]{2,1,0:T(8,128)(2,1)S(1)} %all_to_all.46.plain_ref), custom_call_target="tpu_custom_call" | custom-call | bytes 17432576 | tf_op jit(solution)/shard_map/pallas_call | solution.py:140
  138.7 3.7 %all-to-all-start.8 = ((f32[16,128,128]{2,1,0:T(8,128)}), f32[16,128,128]{2,1,0:T(8,128)S(1)}, u32[]{:S(2)}, u32[]{:S(2)}) async-start(f32[16,128,128]{2,1,0:T(8,128)} %shard_map.53), calls=%async_computation.8 | async-start | bytes 2097152 | tf_op jit(solution)/shard_map/all_to_all | solution.py:155
  142.4 18.5 %all-to-all-done.8.got_ref = f32[16,128,128]{2,1,0:T(8,128)S(1)} async-done(((f32[16,128,128]{2,1,0:T(8,128)}), f32[16,128,128]{2,1,0:T(8,128)S(1)}, u32[]{:S(2)}, u32[]{:S(2)}) %all-to-all-start.8) | async-done | bytes 1048608 | tf_op jit(solution)/shard_map/all_to_all | solution.py:155
  160.8 0.7 shard_map.54
  (1 shorter events, 0.0 us)
Async XLA Ops:
  138.7 22.2 %all-to-all-start.8 = ((f32[16,128,128]{2,1,0:T(8,128)}), f32[16,128,128]{2,1,0:T(8,128)S(1)}, u32[]{:S(2)}, u32[]{:S(2)}) async-start(f32[16,128,128]{2,1,0:T(8,128)} %shard_map.53), calls=%async_computation.8 | async-start | bytes 2097152 | tf_op jit(solution)/shard_map/all_to_all | solution.py:155

commit v3 on v2

--- a/solution.py
+++ b/solution.py
@@ -16,6 +16,9 @@
 AXES = ("xh", "xl", "zh", "c", "yh", "yl", "zm", "zl")
 SAME_ROWS = ("xh", "xl", "yh", "yl")
 SAME_COLS = ("zh", "zm", "zl", "c")
+RING = SAME_COLS[:3]
+HALF = SIDE // 2
+SWAP = [(0, 1), (1, 0)]
 F32, BF16 = jnp.float32, jnp.bfloat16
 VMEM_LIMIT = 16 * 2**20
 
@@ -42,6 +45,7 @@
     unit = unit_of(plain[:LANES])
     for peer in range(PEERS):
         unit_ref[peer] = unit
+    for peer in range(PEERS // 2):
         plain_ref[peer] = plain[LANES:]
 
 
@@ -55,8 +59,13 @@
         out_ref[peer] = lines
 
 
-def tile_kernel(left_ref, plain_ref, tile_ref, sums_ref, units_ref, lines_ref):
-    units_ref[...] = unit_of(plain_ref[...].reshape(SIDE, LANES))
+def tile_kernel(left_ref, mine_ref, other_ref, tile_ref, sums_ref, plain_ref, units_ref, lines_ref):
+    core = lax.axis_index("c")
+    for half, got_ref in ((core, mine_ref), (1 - core, other_ref)):
+        place = pl.ds(pl.multiple_of(half * HALF, HALF), HALF)
+        plain = got_ref[...].reshape(HALF, LANES)
+        plain_ref[place, :] = plain
+        units_ref[place, :] = unit_of(plain)
 
     @pl.loop(0, PEERS // 2)
     def _(step):
@@ -118,21 +127,22 @@
 def map_kernel(got_ref, tile_ref, plain_ref, out_ref):
     scale = scale_of(got_ref)
     wide = jnp.concatenate([scale[chunk : chunk + 1] for chunk in range(PEERS)], axis=1)
-    plain = plain_ref[...].reshape(SIDE, LANES)
+    plain = plain_ref[...]
 
     @pl.loop(0, PEERS // 2)
     def _(step):
         rows = pl.ds(pl.multiple_of(step * 2 * LANES, 2 * LANES), 2 * LANES)
         scaled = (tile_ref[rows, :] * wide).astype(BF16)
         part = jnp.dot(scaled, plain, preferred_element_type=F32)
-        out_ref[pl.ds(2 * step, 2)] = part.reshape(2, LANES, LANES)
+        out_ref[pl.ds(2 * step, 2)] = part.reshape(2, LANES, LANES).astype(BF16)
 
 
 def finish_kernel(got_ref, scale_ref, out_ref):
     total = got_ref[0].astype(F32)
     for peer in range(1, PEERS):
         total += got_ref[peer].astype(F32)
-    out_ref[...] = total * jnp.broadcast_to(scale_ref[...], (LANES, LANES)).T
+    scale = scale_ref[pl.ds(lax.axis_index(SAME_ROWS), 1)]
+    out_ref[...] = total * jnp.broadcast_to(scale, (LANES, LANES)).T
 
 
 def call(kernel, outs, *args, scratch=(), flops=0, exps=0, limit=VMEM_LIMIT, **specs):
@@ -162,7 +172,7 @@
     rows = feats_one.shape[0] + feats_two.shape[0]
     unit_one, plain_two = call(
         embed_kernel,
-        (spread, spread),
+        (spread, pltpu.VMEM((PEERS // 2, LANES, LANES), BF16)),
         feats_one,
         feats_two,
         w_first,
@@ -176,13 +186,16 @@
             pltpu.SemaphoreType.DMA((4,)),
         ),
     )
-    plains = near(exchange(plain_two, SAME_COLS))
-    units = near(exchange(unit_one, SAME_ROWS))
-    tile, sums = call(
+    mine = exchange(plain_two, RING)
+    other = lax.ppermute(mine, "c", SWAP)
+    mine, unit_one = lax.optimization_barrier((mine, unit_one))
+    units = exchange(unit_one, SAME_ROWS)
+    tile, sums, plains = call(
         tile_kernel,
-        (pltpu.VMEM((SIDE, SIDE), F32), vectors),
-        units,
-        plains,
+        (pltpu.VMEM((SIDE, SIDE), F32), vectors, pltpu.VMEM((SIDE, LANES), BF16)),
+        near(units),
+        near(mine),
+        near(other),
         scratch=(pltpu.VMEM((SIDE, LANES), BF16), lines),
     )
     tile = near(tile)
@@ -192,10 +205,9 @@
         sums = near(exchange(sums, SAME_ROWS))
         sums, row_scale = call(cols_kernel, (vectors, lines), sums, tile, scratch=(lines,))
         sums = near(exchange(sums, SAME_COLS))
-    parts = call(map_kernel, pltpu.VMEM((PEERS, LANES, LANES), F32), sums, tile, plains)
+    parts = call(map_kernel, spread, sums, tile, near(plains))
     parts = near(exchange(parts, SAME_ROWS))
-    own = lax.dynamic_slice_in_dim(row_scale, lax.axis_index(SAME_ROWS), 1, 0)
-    return call(finish_kernel, jax.ShapeDtypeStruct((LANES, LANES), F32), parts, own)
+    return call(finish_kernel, jax.ShapeDtypeStruct((LANES, LANES), F32), parts, row_scale)
 
 
 def solution(mesh):

time: 162 us -> 147 us (0.907)
  waiting for transfers between devices: 18.5 us -> 6.27 us
  blocking collectives: 114 us -> 106 us
  starting transfers between devices: 3.65 us -> 9.58 us
    all_to_all x1, waiting for transfers between devices: 18.5 us -> 5.11 us  [exchange(): return lax.all_to_all(array, axes, 0, 0)]
    all_to_all x8, blocking collectives: 114 us -> 106 us  [exchange(): return lax.all_to_all(array, axes, 0, 0)]
    all_to_all x1, starting transfers between devices: 3.65 us -> 6.76 us  [exchange(): return lax.all_to_all(array, axes, 0, 0)]
    ppermute x0 -> x1, starting transfers between devices: none -> 2.82 us  [on_device(): other = lax.ppermute(mine, 'c', SWAP)]
  transfers between devices with their start and end apart: 1 -> 2, of which waited for: 1 -> 2; matrix products, arithmetic and copies ran while one was open for 0% -> 0% of each run, Pallas kernels for 0% -> 0%
where the time goes in v3:
time: 147 us
  blocking collectives  106 us (72%)
  Pallas kernels  25.1 us (17%)
  starting transfers between devices  9.58 us (7%)
  waiting for transfers between devices  6.27 us (4%)
    all_to_all x8, blocking collectives, exchange(): return lax.all_to_all(array, axes, 0, 0)  106 us
    pallas_call x9, Pallas kernels, call(): pl.pallas_call(kernel, out_shape=outs, **specs, scratch_shapes=scratch, c...  25.1 us
    all_to_all x1, starting transfers between devices, exchange(): return lax.all_to_all(array, axes, 0, 0)  6.76 us
    all_to_all x1, waiting for transfers between devices, exchange(): return lax.all_to_all(array, axes, 0, 0)  5.11 us
  transfers between devices with their start and end apart: 2, of which 2 were waited for; matrix products, arithmetic and copies ran while one was open for 0% of the time, Pallas kernels for 0%

profile of v3, /device:TPU:1, one launch (start us, length us, event | category | flops | bytes accessed | tf_op | source)
XLA Modules:
  0.0 147.0 jit_solution(17189354590994569108)
XLA Ops:
  0.0 3.2 %shard_map.46 = (bf16[16,128,128]{2,1,0:T(8,128)(2,1)}, bf16[8,128,128]{2,1,0:T(8,128)(2,1)S(1)}) custom-call(bf16[128,1536]{1,0:T(8,128)(2,1)} %one_hbm.1, bf16[128,1536]{1,0:T(8,128)(2,1)} %two_hbm.1, bf16[1536,512]{1,0:T(8,128)(2,1)} %first_hbm.1, bf16[512,128]{1,0:T(8,128)(2,1)} %second_hbm.1), custom_call_target="tpu_custom_call" | custom-call | bytes 2490368 | tf_op jit(solution)/shard_map/pallas_call | solution.py:150
  3.2 19.2 %all_to_all.45.mine_ref = bf16[8,128,128]{2,1,0:T(8,128)(2,1)S(1)} all-to-all(bf16[8,128,128]{2,1,0:T(8,128)(2,1)S(1)} %get-tuple-element.16), channel_id=1, replica_groups=mesh['xh'=2,'xl'=2,'zh'=2,'c'=2,'yh'=2,'yl'=2,'zm'=2,'zl'=2] {'zh','zm',..., dimensions={0} | all-to-all | bytes 524288 | tf_op jit(solution)/shard_map/all_to_all | solution.py:165
  22.4 6.8 %all-to-all-start.1 = ((bf16[16,128,128]{2,1,0:T(8,128)(2,1)}), bf16[16,128,128]{2,1,0:T(8,128)(2,1)S(1)}, u32[]{:S(2)}, u32[]{:S(2)}) async-start(bf16[16,128,128]{2,1,0:T(8,128)(2,1)} %get-tuple-element.18), calls=%async_computation.1 | async-start | bytes 1048576 | tf_op jit(solution)/shard_map/all_to_all | solution.py:165
  29.2 2.8 %collective-permute-start = (bf16[8,128,128]{2,1,0:T(8,128)(2,1)S(1)}, bf16[8,128,128]{2,1,0:T(8,128)(2,1)S(1)}, u32[]{:S(2)}, u32[]{:S(2)}) collective-permute-start(bf16[8,128,128]{2,1,0:T(8,128)(2,1)S(1)} %all_to_all.45.mine_ref), channel_id=1, source_target_pairs={{0,16},{16,0},{1,17},{17,1},{2,18},{18,2},{3,19},{19,3},{4,20},{20... | collective-permute-start | bytes 786440 | tf_op jit(solution)/shard_map/ppermute | solution.py:190
  32.0 1.2 collective-permute-done.other_ref
  33.2 5.1 %all-to-all-done.1.left_ref = bf16[16,128,128]{2,1,0:T(8,128)(2,1)S(1)} async-done(((bf16[16,128,128]{2,1,0:T(8,128)(2,1)}), bf16[16,128,128]{2,1,0:T(8,128)(2,1)S(1)}, u32[]{:S(2)}, u32[]{:S(2)}) %all-to-all-start.1) | async-done | bytes 524320 | tf_op jit(solution)/shard_map/all_to_all | solution.py:165
  38.3 4.8 %shard_map.47 = (f32[2048,2048]{1,0:T(8,128)S(1)}, f32[16,16,128]{2,1,0:T(8,128)S(1)}, bf16[2048,128]{1,0:T(8,128)(2,1)S(1)}) custom-call(bf16[16,128,128]{2,1,0:T(8,128)(2,1)S(1)} %all-to-all-done.1.left_ref, bf16[8,128,128]{2,1,0:T(8,128)(2,1)S(1)} %all_to_all.45.mine_ref, bf16[8,128,128]{2,1,0:T(8,128)(2,1)S(1)} %collective-permute-done.other_ref), custom_call_target="tpu_custom_call" | custom-call | bytes 1048576 | tf_op jit(solution)/shard_map/pallas_call | solution.py:150
  43.1 9.8 %all_to_all.46.got_ref = f32[16,16,128]{2,1,0:T(8,128)S(1)} all-to-all(f32[16,16,128]{2,1,0:T(8,128)S(1)} %get-tuple-element.20), channel_id=1, replica_groups=mesh['xh'=2,'xl'=2,'zh'=2,'c'=2,'yh'=2,'yl'=2,'zm'=2,'zl'=2] {'xh','xl',..., dimensions={0} | all-to-all | bytes 262144 | tf_op jit(solution)/shard_map/all_to_all | solution.py:165
  52.9 2.8 %shard_map.48 = (f32[16,16,128]{2,1,0:T(8,128)S(1)}, f32[16,128]{1,0:T(8,128)}) custom-call(f32[16,16,128]{2,1,0:T(8,128)S(1)} %all_to_all.46.got_ref, f32[2048,2048]{1,0:T(8,128)S(1)} %get-tuple-element.21.tile_ref), custom_call_target="tpu_custom_call" | custom-call | bytes 16908288 | tf_op jit(solution)/shard_map/pallas_call | solution.py:150
  55.7 16.6 %all_to_all.47.got_ref = f32[16,16,128]{2,1,0:T(8,128)S(1)} all-to-all(f32[16,16,128]{2,1,0:T(8,128)S(1)} %get-tuple-element.22), channel_id=1, replica_groups=mesh['xh'=2,'xl'=2,'zh'=2,'c'=2,'yh'=2,'yl'=2,'zm'=2,'zl'=2] {'zh','zm',..., dimensions={0} | all-to-all | bytes 262144 | tf_op jit(solution)/shard_map/all_to_all | solution.py:165
  72.3 2.5 %shard_map.49 = f32[16,16,128]{2,1,0:T(8,128)S(1)} custom-call(f32[16,16,128]{2,1,0:T(8,128)S(1)} %all_to_all.47.got_ref, f32[2048,2048]{1,0:T(8,128)S(1)} %get-tuple-element.21.tile_ref), custom_call_target="tpu_custom_call" | custom-call | bytes 16908288 | tf_op jit(solution)/shard_map/pallas_call | solution.py:150
  74.8 10.3 %all_to_all.48.got_ref = f32[16,16,128]{2,1,0:T(8,128)S(1)} all-to-all(f32[16,16,128]{2,1,0:T(8,128)S(1)} %shard_map.49), channel_id=1, replica_groups=mesh['xh'=2,'xl'=2,'zh'=2,'c'=2,'yh'=2,'yl'=2,'zm'=2,'zl'=2] {'xh','xl',..., dimensions={0} | all-to-all | bytes 262144 | tf_op jit(solution)/shard_map/all_to_all | solution.py:165
  85.0 2.8 %shard_map.50 = (f32[16,16,128]{2,1,0:T(8,128)S(1)}, f32[16,128]{1,0:T(8,128)}) custom-call(f32[16,16,128]{2,1,0:T(8,128)S(1)} %all_to_all.48.got_ref, f32[2048,2048]{1,0:T(8,128)S(1)} %get-tuple-element.21.tile_ref), custom_call_target="tpu_custom_call" | custom-call | bytes 16908288 | tf_op jit(solution)/shard_map/pallas_call | solution.py:150
  87.9 12.6 %all_to_all.49.got_ref = f32[16,16,128]{2,1,0:T(8,128)S(1)} all-to-all(f32[16,16,128]{2,1,0:T(8,128)S(1)} %get-tuple-element.23), channel_id=1, replica_groups=mesh['xh'=2,'xl'=2,'zh'=2,'c'=2,'yh'=2,'yl'=2,'zm'=2,'zl'=2] {'zh','zm',..., dimensions={0} | all-to-all | bytes 262144 | tf_op jit(solution)/shard_map/all_to_all | solution.py:165
  100.5 2.5 %shard_map.51 = f32[16,16,128]{2,1,0:T(8,128)S(1)} custom-call(f32[16,16,128]{2,1,0:T(8,128)S(1)} %all_to_all.49.got_ref, f32[2048,2048]{1,0:T(8,128)S(1)} %get-tuple-element.21.tile_ref), custom_call_target="tpu_custom_call" | custom-call | bytes 16908288 | tf_op jit(solution)/shard_map/pallas_call | solution.py:150
  102.9 10.2 %all_to_all.50.got_ref = f32[16,16,128]{2,1,0:T(8,128)S(1)} all-to-all(f32[16,16,128]{2,1,0:T(8,128)S(1)} %shard_map.51), channel_id=1, replica_groups=mesh['xh'=2,'xl'=2,'zh'=2,'c'=2,'yh'=2,'yl'=2,'zm'=2,'zl'=2] {'xh','xl',..., dimensions={0} | all-to-all | bytes 262144 | tf_op jit(solution)/shard_map/all_to_all | solution.py:165
  113.1 2.4 %shard_map.52 = (f32[16,16,128]{2,1,0:T(8,128)S(1)}, f32[16,128]{1,0:T(8,128)S(1)}) custom-call(f32[16,16,128]{2,1,0:T(8,128)S(1)} %all_to_all.50.got_ref, f32[2048,2048]{1,0:T(8,128)S(1)} %get-tuple-element.21.tile_ref), custom_call_target="tpu_custom_call" | custom-call | bytes 16908288 | tf_op jit(solution)/shard_map/pallas_call | solution.py:150
  115.5 12.6 %all_to_all.51.got_ref = f32[16,16,128]{2,1,0:T(8,128)S(1)} all-to-all(f32[16,16,128]{2,1,0:T(8,128)S(1)} %get-tuple-element.24), channel_id=1, replica_groups=mesh['xh'=2,'xl'=2,'zh'=2,'c'=2,'yh'=2,'yl'=2,'zm'=2,'zl'=2] {'zh','zm',..., dimensions={0} | all-to-all | bytes 262144 | tf_op jit(solution)/shard_map/all_to_all | solution.py:165
  128.1 3.5 %shard_map.53 = bf16[16,128,128]{2,1,0:T(8,128)(2,1)S(1)} custom-call(f32[16,16,128]{2,1,0:T(8,128)S(1)} %all_to_all.51.got_ref, f32[2048,2048]{1,0:T(8,128)S(1)} %get-tuple-element.21.tile_ref, bf16[2048,128]{1,0:T(8,128)(2,1)S(1)} %get-tuple-element.25.plain_ref), custom_call_target="tpu_custom_call" | custom-call | bytes 17432576 | tf_op jit(solution)/shard_map/pallas_call | solution.py:150
  131.6 14.6 %all_to_all.52.got_ref = bf16[16,128,128]{2,1,0:T(8,128)(2,1)S(1)} all-to-all(bf16[16,128,128]{2,1,0:T(8,128)(2,1)S(1)} %shard_map.53), channel_id=1, replica_groups=mesh['xh'=2,'xl'=2,'zh'=2,'c'=2,'yh'=2,'yl'=2,'zm'=2,'zl'=2] {'xh','xl',..., dimensions={0} | all-to-all | bytes 1048576 | tf_op jit(solution)/shard_map/all_to_all | solution.py:165
  146.2 0.7 shard_map.54
Async XLA Ops:
  22.4 15.9 %all-to-all-start.1 = ((bf16[16,128,128]{2,1,0:T(8,128)(2,1)}), bf16[16,128,128]{2,1,0:T(8,128)(2,1)S(1)}, u32[]{:S(2)}, u32[]{:S(2)}) async-start(bf16[16,128,128]{2,1,0:T(8,128)(2,1)} %get-tuple-element.18), calls=%async_computation.1 | async-start | bytes 1048576 | tf_op jit(solution)/shard_map/all_to_all | solution.py:165
  29.2 4.0 %collective-permute-start = (bf16[8,128,128]{2,1,0:T(8,128)(2,1)S(1)}, bf16[8,128,128]{2,1,0:T(8,128)(2,1)S(1)}, u32[]{:S(2)}, u32[]{:S(2)}) collective-permute-start(bf16[8,128,128]{2,1,0:T(8,128)(2,1)S(1)} %all_to_all.45.mine_ref), channel_id=1, source_target_pairs={{0,16},{16,0},{1,17},{17,1},{2,18},{18,2},{3,19},{19,3},{4,20},{20... | collective-permute-start | bytes 786440 | tf_op jit(solution)/shard_map/ppermute | solution.py:190

commit v4 on v3

v4 whole, which is shorter than its diff:
```python
import functools
import math

import jax
import jax.numpy as jnp
from jax import lax
from jax.experimental import pallas as pl
from jax.experimental.pallas import tpu as pltpu
from jax.sharding import Mesh
from jax.sharding import PartitionSpec as P

SWEEPS = 3
PIECES = 3
PEERS = 16
LANES = 128
SIDE = PEERS * LANES
EXPONENT = 20.0 * math.log2(math.e)
AXES = ("xh", "xl", "zh", "c", "yh", "yl", "zm", "zl")
SAME_ROWS = ("xh", "xl", "yh", "yl")
SAME_COLS = ("zh", "zm", "zl", "c")
RING = SAME_COLS[:3]
HALF = SIDE // 2
SWAP = [(0, 1), (1, 0)]
F32, BF16 = jnp.float32, jnp.bfloat16
VMEM_LIMIT = 16 * 2**20


def unit_of(plain):
    wide = plain.astype(F32)
    return (wide / jnp.sqrt(jnp.sum(wide * wide, axis=1, keepdims=True) + 1e-06)).astype(BF16)


def embed_kernel(feats_hbm, first_hbm, second_hbm, out_ref, feats_ref, first_ref, second_ref, sems, *, unit):
    depth = first_hbm.shape[0] // PIECES
    copies = [pltpu.make_async_copy(feats_hbm, feats_ref, sems.at[PIECES])]
    for piece in range(PIECES):
        place = pl.ds(piece * depth, depth)
        copies.append(pltpu.make_async_copy(first_hbm.at[place], first_ref.at[place], sems.at[piece]))
    copies.append(pltpu.make_async_copy(second_hbm, second_ref, sems.at[PIECES + 1]))
    for copy in copies:
        copy.start()
    copies[0].wait()
    hidden = jnp.zeros((LANES, first_hbm.shape[1]), F32)
    for piece in range(PIECES):
        copies[1 + piece].wait()
        place = slice(piece * depth, (piece + 1) * depth)
        hidden += jnp.dot(feats_ref[:, place], first_ref[place], preferred_element_type=F32)
    hidden = jnp.maximum(hidden, 0.0).astype(BF16)
    copies[-1].wait()
    out = jnp.dot(hidden, second_ref[...], preferred_element_type=F32).astype(BF16)
    if unit:
        out = unit_of(out)
    for peer in range(out_ref.shape[0]):
        out_ref[peer] = out


def unit_kernel(mine_ref, other_ref, plain_ref, unit_ref):
    core = lax.axis_index("c")
    for half, got_ref in ((core, mine_ref), (1 - core, other_ref)):
        place = pl.ds(pl.multiple_of(half * HALF, HALF), HALF)
        plain = got_ref[...].reshape(HALF, LANES)
        plain_ref[place, :] = plain
        unit_ref[place, :] = unit_of(plain)


def row_totals(parts):
    return jnp.sum(parts.T, axis=0, keepdims=True)


def fill(out_ref, lines_ref):
    lines = lines_ref[...]
    for peer in range(PEERS):
        out_ref[peer] = lines


def tile_kernel(left_ref, right_ref, tile_ref, sums_ref, lines_ref):
    for step in range(PEERS // 2):
        left = left_ref[2 * step : 2 * step + 2].reshape(2 * LANES, LANES)
        rows = slice(step * 2 * LANES, (step + 1) * 2 * LANES)
        parts = jnp.zeros((2 * LANES, LANES), F32)
        for chunk in range(PEERS // 2):
            cols = slice(chunk * 2 * LANES, (chunk + 1) * 2 * LANES)
            dots = lax.dot_general(left, right_ref[cols], (((1,), (1,)), ((), ())), preferred_element_type=F32)
            block = jnp.exp2(dots * EXPONENT)
            tile_ref[rows, cols] = block
            parts += block[:, :LANES] + block[:, LANES:]
        lines_ref[2 * step : 2 * step + 1] = row_totals(parts[:LANES])
        lines_ref[2 * step + 1 : 2 * step + 2] = row_totals(parts[LANES:])
    fill(sums_ref, lines_ref)


def scale_of(got_ref):
    total = got_ref[0]
    for peer in range(1, PEERS):
        total += got_ref[peer]
    return 1.0 / total


def cols_kernel(got_ref, tile_ref, sums_ref, scale_ref, lines_ref):
    scale = scale_of(got_ref)
    scale_ref[...] = scale
    parts = [jnp.zeros((8, LANES), F32) for _ in range(PEERS)]
    for block in range(PEERS):
        rows = slice(block * LANES, (block + 1) * LANES)
        factor = jnp.broadcast_to(scale[block : block + 1], (LANES, LANES)).T
        for chunk in range(PEERS):
            product = tile_ref[rows, chunk * LANES : (chunk + 1) * LANES] * factor
            parts[chunk] += jnp.sum(product.reshape(LANES // 8, 8, LANES), axis=0)
    for chunk in range(PEERS):
        lines_ref[chunk : chunk + 1] = jnp.sum(parts[chunk], axis=0, keepdims=True)
    fill(sums_ref, lines_ref)


def rows_kernel(got_ref, tile_ref, sums_ref, lines_ref):
    scale = scale_of(got_ref)
    for block in range(PEERS):
        rows = slice(block * LANES, (block + 1) * LANES)
        parts = tile_ref[rows, :LANES] * scale[:1]
        for chunk in range(1, PEERS):
            parts += tile_ref[rows, chunk * LANES : (chunk + 1) * LANES] * scale[chunk : chunk + 1]
        lines_ref[block : block + 1] = row_totals(parts)
    fill(sums_ref, lines_ref)


def map_kernel(got_ref, tile_ref, plain_ref, out_ref):
    scale = scale_of(got_ref)
    wide = jnp.concatenate([scale[chunk : chunk + 1] for chunk in range(PEERS)], axis=1)
    scaled = (tile_ref[...] * wide).astype(BF16)
    part = jnp.dot(scaled, plain_ref[...], preferred_element_type=F32)
    out_ref[...] = part.reshape(PEERS, LANES, LANES).astype(BF16)


def finish_kernel(got_ref, scale_ref, out_ref):
    total = got_ref[0].astype(F32)
    for peer in range(1, PEERS):
        total += got_ref[peer].astype(F32)
    scale = scale_ref[pl.ds(lax.axis_index(SAME_ROWS), 1)]
    out_ref[...] = total * jnp.broadcast_to(scale, (LANES, LANES)).T


def call(kernel, outs, *args, scratch=(), flops=0, exps=0, limit=VMEM_LIMIT, **specs):
    moved = sum(math.prod(a.shape) * a.dtype.itemsize for a in args)
    return pl.pallas_call(
        kernel,
        out_shape=outs,
        **specs,
        scratch_shapes=scratch,
        compiler_params=pltpu.CompilerParams(vmem_limit_bytes=limit),
        cost_estimate=pl.CostEstimate(flops=flops, bytes_accessed=moved, transcendentals=exps),
    )(*args)


def near(array):
    return pltpu.with_memory_space_constraint(array, pltpu.VMEM)


def exchange(array, axes):
    return lax.all_to_all(array, axes, 0, 0)


def embed(feats, w_first, w_second, copies, unit):
    flops = 2 * feats.shape[0] * w_first.shape[0] * w_first.shape[1]
    return call(
        functools.partial(embed_kernel, unit=unit),
        pltpu.VMEM((copies, LANES, LANES), BF16),
        feats,
        w_first,
        w_second,
        in_specs=[pl.BlockSpec(memory_space=pltpu.HBM)] * 3,
        limit=60 * 2**20,
        scratch=(
            pltpu.VMEM(feats.shape, BF16),
            pltpu.VMEM(w_first.shape, BF16),
            pltpu.VMEM(w_second.shape, BF16),
            pltpu.SemaphoreType.DMA((PIECES + 2,)),
        ),
        flops=flops,
    )


def on_device(feats_one, feats_two, w_first, w_second):
    vectors = pltpu.VMEM((PEERS, PEERS, LANES), F32)
    lines = pltpu.VMEM((PEERS, LANES), F32)
    block = pltpu.VMEM((SIDE, LANES), BF16)
    plain_two = embed(feats_two, w_first, w_second, PEERS // 2, False)
    mine = exchange(plain_two, RING)
    unit_one = embed(feats_one, w_first, w_second, PEERS, True)
    mine, unit_one = lax.optimization_barrier((mine, unit_one))
    other = lax.ppermute(mine, "c", SWAP)
    units_left = exchange(unit_one, SAME_ROWS)
    plains, units_right = call(unit_kernel, (block, block), near(mine), near(other), flops=SIDE * LANES * 8)
    tile, sums = call(
        tile_kernel,
        (pltpu.VMEM((SIDE, SIDE), F32), vectors),
        near(units_left),
        near(units_right),
        scratch=(lines,),
        flops=2 * SIDE * SIDE * LANES,
        exps=SIDE * SIDE,
    )
    tile = near(tile)
    for sweep in range(SWEEPS):
        if sweep:
            sums = call(rows_kernel, vectors, sums, tile, scratch=(lines,))
        sums = near(exchange(sums, SAME_ROWS))
        sums, row_scale = call(cols_kernel, (vectors, lines), sums, tile, scratch=(lines,))
        sums = near(exchange(sums, SAME_COLS))
    parts = call(map_kernel, pltpu.VMEM((PEERS, LANES, LANES), BF16), sums, tile, near(plains))
    parts = near(exchange(parts, SAME_ROWS))
    return call(finish_kernel, jax.ShapeDtypeStruct((LANES, LANES), F32), parts, row_scale)


def solution(mesh):
    fine = Mesh(mesh.devices.reshape((2,) * 8), AXES)
    row, col = AXES[:4], AXES[4:]
    return jax.shard_map(
        on_device,
        mesh=fine,
        in_specs=(P(row + col, None), P(col + row, None), P(), P()),
        out_specs=P(row + col, None),
        check_vma=False,
    )
```

time: 147 us -> 137 us (0.932)
  blocking collectives: 106 us -> 86.4 us
  starting transfers between devices: 9.58 us -> 18.6 us
  Pallas kernels: 25.1 us -> 17.8 us
  waiting for transfers between devices: 6.27 us -> 13.1 us
    all_to_all x8 -> x7, blocking collectives: 106 us -> 86.4 us  [exchange(): return lax.all_to_all(array, axes, 0, 0)]
    all_to_all x1 -> x2, starting transfers between devices: 6.76 us -> 15.8 us  [exchange(): return lax.all_to_all(array, axes, 0, 0)]
    pallas_call x9 -> x11, Pallas kernels: 25.1 us -> 17.8 us  [call(): pl.pallas_call(kernel, out_shape=outs, **specs, scratch_shapes=scratch, c...]
    all_to_all x1 -> x2, waiting for transfers between devices: 5.11 us -> 11.9 us  [exchange(): return lax.all_to_all(array, axes, 0, 0)]
  transfers between devices with their start and end apart: 2 -> 3, of which waited for: 2 -> 3; matrix products, arithmetic and copies ran while one was open for 0% -> 0% of each run, Pallas kernels for 0% -> 3%
where the time goes in v4:
time: 137 us; the launch traced here: 136 us
  blocking collectives  86.4 us (63%)
  starting transfers between devices  18.6 us (14%)
  Pallas kernels  17.8 us (13%)
  waiting for transfers between devices  13.1 us (10%)
    all_to_all x7, blocking collectives, exchange(): return lax.all_to_all(array, axes, 0, 0)  86.4 us
    pallas_call x11, Pallas kernels, call(): pl.pallas_call(kernel, out_shape=outs, **specs, scratch_shapes=scratch, c...  17.8 us
    all_to_all x2, starting transfers between devices, exchange(): return lax.all_to_all(array, axes, 0, 0)  15.8 us
    all_to_all x2, waiting for transfers between devices, exchange(): return lax.all_to_all(array, axes, 0, 0)  11.9 us
    ppermute x1, starting transfers between devices, on_device(): other = lax.ppermute(mine, 'c', SWAP)  2.84 us
  transfers between devices with their start and end apart: 3, of which 3 were waited for; matrix products, arithmetic and copies ran while one was open for 0% of the time, Pallas kernels for 3%

profile of v4, /device:TPU:1, one launch (start us, length us, event | category | flops | bytes accessed | tf_op | source)
XLA Modules:
  0.0 135.9 jit_solution(17929052908190601089)
XLA Ops:
  0.0 2.7 %shard_map.46 = bf16[8,128,128]{2,1,0:T(8,128)(2,1)} custom-call(bf16[128,1536]{1,0:T(8,128)(2,1)} %feats_hbm.2, bf16[1536,512]{1,0:T(8,128)(2,1)} %first_hbm.3, bf16[512,128]{1,0:T(8,128)(2,1)} %second_hbm.3), custom_call_target="tpu_custom_call" | custom-call | flops 201326592 | bytes 2097152 | tf_op jit(solution)/shard_map/pallas_call | solution.py:143
  2.7 9.0 %all-to-all-start = ((bf16[8,128,128]{2,1,0:T(8,128)(2,1)}), bf16[8,128,128]{2,1,0:T(8,128)(2,1)S(1)}, u32[]{:S(2)}, u32[]{:S(2)}) async-start(bf16[8,128,128]{2,1,0:T(8,128)(2,1)} %shard_map.46), calls=%async_computation | async-start | bytes 524288 | tf_op jit(solution)/shard_map/all_to_all | solution.py:158
  11.7 2.9 %shard_map.47 = bf16[16,128,128]{2,1,0:T(8,128)(2,1)} custom-call(bf16[128,1536]{1,0:T(8,128)(2,1)} %feats_hbm.3, bf16[1536,512]{1,0:T(8,128)(2,1)} %first_hbm.3, bf16[512,128]{1,0:T(8,128)(2,1)} %second_hbm.3), custom_call_target="tpu_custom_call" | custom-call | flops 201326592 | bytes 2097152 | tf_op jit(solution)/shard_map/pallas_call | solution.py:143
  14.6 7.5 %all-to-all-done.mine_ref = bf16[8,128,128]{2,1,0:T(8,128)(2,1)S(1)} async-done(((bf16[8,128,128]{2,1,0:T(8,128)(2,1)}), bf16[8,128,128]{2,1,0:T(8,128)(2,1)S(1)}, u32[]{:S(2)}, u32[]{:S(2)}) %all-to-all-start) | async-done | bytes 262176 | tf_op jit(solution)/shard_map/all_to_all | solution.py:158
  22.1 6.7 %all-to-all-start.1 = ((bf16[16,128,128]{2,1,0:T(8,128)(2,1)}), bf16[16,128,128]{2,1,0:T(8,128)(2,1)S(1)}, u32[]{:S(2)}, u32[]{:S(2)}) async-start(bf16[16,128,128]{2,1,0:T(8,128)(2,1)} %shard_map.47), calls=%async_computation.1 | async-start | bytes 1048576 | tf_op jit(solution)/shard_map/all_to_all | solution.py:158
  28.8 2.8 %collective-permute-start = (bf16[8,128,128]{2,1,0:T(8,128)(2,1)S(1)}, bf16[8,128,128]{2,1,0:T(8,128)(2,1)S(1)}, u32[]{:S(2)}, u32[]{:S(2)}) collective-permute-start(bf16[8,128,128]{2,1,0:T(8,128)(2,1)S(1)} %all-to-all-done.mine_ref), channel_id=1, source_target_pairs={{0,16},{16,0},{1,17},{17,1},{2,18},{18,2},{3,19},{19,3},{4,20},{20... | collective-permute-start | bytes 786440 | tf_op jit(solution)/shard_map/ppermute | solution.py:189
  31.7 1.2 collective-permute-done.other_ref
  32.8 0.6 shard_map.48
  33.4 4.4 %all-to-all-done.1.left_ref = bf16[16,128,128]{2,1,0:T(8,128)(2,1)S(1)} async-done(((bf16[16,128,128]{2,1,0:T(8,128)(2,1)}), bf16[16,128,128]{2,1,0:T(8,128)(2,1)S(1)}, u32[]{:S(2)}, u32[]{:S(2)}) %all-to-all-start.1) | async-done | bytes 524320 | tf_op jit(solution)/shard_map/all_to_all | solution.py:158
  37.9 2.5 %shard_map.49 = (f32[2048,2048]{1,0:T(8,128)S(1)}, f32[16,16,128]{2,1,0:T(8,128)S(1)}) custom-call(bf16[16,128,128]{2,1,0:T(8,128)(2,1)S(1)} %all-to-all-done.1.left_ref, bf16[2048,128]{1,0:T(8,128)(2,1)S(1)} %get-tuple-element.17.right_ref), custom_call_target="tpu_custom_call" | custom-call | flops 1073741824 | bytes 1048576 | tf_op jit(solution)/shard_map/pallas_call | solution.py:143
  40.3 9.9 %all_to_all.45.got_ref = f32[16,16,128]{2,1,0:T(8,128)S(1)} all-to-all(f32[16,16,128]{2,1,0:T(8,128)S(1)} %get-tuple-element.18), channel_id=1, replica_groups=mesh['xh'=2,'xl'=2,'zh'=2,'c'=2,'yh'=2,'yl'=2,'zm'=2,'zl'=2] {'xh','xl',..., dimensions={0} | all-to-all | bytes 262144 | tf_op jit(solution)/shard_map/all_to_all | solution.py:158
  50.2 1.2 shard_map.50
  51.4 16.7 %all_to_all.46.got_ref = f32[16,16,128]{2,1,0:T(8,128)S(1)} all-to-all(f32[16,16,128]{2,1,0:T(8,128)S(1)} %get-tuple-element.20), channel_id=1, replica_groups=mesh['xh'=2,'xl'=2,'zh'=2,'c'=2,'yh'=2,'yl'=2,'zm'=2,'zl'=2] {'zh','zm',..., dimensions={0} | all-to-all | bytes 262144 | tf_op jit(solution)/shard_map/all_to_all | solution.py:158
  68.1 1.2 shard_map.51
  69.3 10.3 %all_to_all.47.got_ref = f32[16,16,128]{2,1,0:T(8,128)S(1)} all-to-all(f32[16,16,128]{2,1,0:T(8,128)S(1)} %shard_map.51), channel_id=1, replica_groups=mesh['xh'=2,'xl'=2,'zh'=2,'c'=2,'yh'=2,'yl'=2,'zm'=2,'zl'=2] {'xh','xl',..., dimensions={0} | all-to-all | bytes 262144 | tf_op jit(solution)/shard_map/all_to_all | solution.py:158
  79.5 1.2 shard_map.52
  80.8 12.6 %all_to_all.48.got_ref = f32[16,16,128]{2,1,0:T(8,128)S(1)} all-to-all(f32[16,16,128]{2,1,0:T(8,128)S(1)} %get-tuple-element.21), channel_id=1, replica_groups=mesh['xh'=2,'xl'=2,'zh'=2,'c'=2,'yh'=2,'yl'=2,'zm'=2,'zl'=2] {'zh','zm',..., dimensions={0} | all-to-all | bytes 262144 | tf_op jit(solution)/shard_map/all_to_all | solution.py:158
  93.4 1.2 shard_map.53
  94.6 10.2 %all_to_all.49.got_ref = f32[16,16,128]{2,1,0:T(8,128)S(1)} all-to-all(f32[16,16,128]{2,1,0:T(8,128)S(1)} %shard_map.53), channel_id=1, replica_groups=mesh['xh'=2,'xl'=2,'zh'=2,'c'=2,'yh'=2,'yl'=2,'zm'=2,'zl'=2] {'xh','xl',..., dimensions={0} | all-to-all | bytes 262144 | tf_op jit(solution)/shard_map/all_to_all | solution.py:158
  104.8 1.2 shard_map.54
  106.0 12.6 %all_to_all.50.got_ref = f32[16,16,128]{2,1,0:T(8,128)S(1)} all-to-all(f32[16,16,128]{2,1,0:T(8,128)S(1)} %get-tuple-element.22), channel_id=1, replica_groups=mesh['xh'=2,'xl'=2,'zh'=2,'c'=2,'yh'=2,'yl'=2,'zm'=2,'zl'=2] {'zh','zm',..., dimensions={0} | all-to-all | bytes 262144 | tf_op jit(solution)/shard_map/all_to_all | solution.py:158
  118.7 2.4 %shard_map.55 = bf16[16,128,128]{2,1,0:T(8,128)(2,1)S(1)} custom-call(f32[16,16,128]{2,1,0:T(8,128)S(1)} %all_to_all.50.got_ref, f32[2048,2048]{1,0:T(8,128)S(1)} %get-tuple-element.19.tile_ref, bf16[2048,128]{1,0:T(8,128)(2,1)S(1)} %get-tuple-element.23.plain_ref), custom_call_target="tpu_custom_call" | custom-call | bytes 17432576 | tf_op jit(solution)/shard_map/pallas_call | solution.py:143
  121.0 14.2 %all_to_all.51.got_ref = bf16[16,128,128]{2,1,0:T(8,128)(2,1)S(1)} all-to-all(bf16[16,128,128]{2,1,0:T(8,128)(2,1)S(1)} %shard_map.55), channel_id=1, replica_groups=mesh['xh'=2,'xl'=2,'zh'=2,'c'=2,'yh'=2,'yl'=2,'zm'=2,'zl'=2] {'xh','xl',..., dimensions={0} | all-to-all | bytes 1048576 | tf_op jit(solution)/shard_map/all_to_all | solution.py:158
  135.2 0.7 shard_map.56
Async XLA Ops:
  2.7 19.4 %all-to-all-start = ((bf16[8,128,128]{2,1,0:T(8,128)(2,1)}), bf16[8,128,128]{2,1,0:T(8,128)(2,1)S(1)}, u32[]{:S(2)}, u32[]{:S(2)}) async-start(bf16[8,128,128]{2,1,0:T(8,128)(2,1)} %shard_map.46), calls=%async_computation | async-start | bytes 524288 | tf_op jit(solution)/shard_map/all_to_all | solution.py:158
  22.1 15.8 %all-to-all-start.1 = ((bf16[16,128,128]{2,1,0:T(8,128)(2,1)}), bf16[16,128,128]{2,1,0:T(8,128)(2,1)S(1)}, u32[]{:S(2)}, u32[]{:S(2)}) async-start(bf16[16,128,128]{2,1,0:T(8,128)(2,1)} %shard_map.47), calls=%async_computation.1 | async-start | bytes 1048576 | tf_op jit(solution)/shard_map/all_to_all | solution.py:158
  28.8 4.0 %collective-permute-start = (bf16[8,128,128]{2,1,0:T(8,128)(2,1)S(1)}, bf16[8,128,128]{2,1,0:T(8,128)(2,1)S(1)}, u32[]{:S(2)}, u32[]{:S(2)}) collective-permute-start(bf16[8,128,128]{2,1,0:T(8,128)(2,1)S(1)} %all-to-all-done.mine_ref), channel_id=1, source_target_pairs={{0,16},{16,0},{1,17},{17,1},{2,18},{18,2},{3,19},{19,3},{4,20},{20... | collective-permute-start | bytes 786440 | tf_op jit(solution)/shard_map/ppermute | solution.py:189

commit v5 on v4

--- a/solution.py
+++ b/solution.py
@@ -1,4 +1,3 @@
-import functools
 import math
 
 import jax
@@ -10,13 +9,15 @@
 from jax.sharding import PartitionSpec as P
 
 SWEEPS = 3
-PIECES = 3
+PIECES = 6
 PEERS = 16
 LANES = 128
 SIDE = PEERS * LANES
 EXPONENT = 20.0 * math.log2(math.e)
 AXES = ("xh", "xl", "zh", "c", "yh", "yl", "zm", "zl")
 SAME_ROWS = ("xh", "xl", "yh", "yl")
+ALONG_X, ALONG_Y = SAME_ROWS[:2], SAME_ROWS[2:]
+SIDES = 4
 SAME_COLS = ("zh", "zm", "zl", "c")
 RING = SAME_COLS[:3]
 HALF = SIDE // 2
@@ -30,28 +31,32 @@
     return (wide / jnp.sqrt(jnp.sum(wide * wide, axis=1, keepdims=True) + 1e-06)).astype(BF16)
 
 
-def embed_kernel(feats_hbm, first_hbm, second_hbm, out_ref, feats_ref, first_ref, second_ref, sems, *, unit):
+def embed_kernel(one_hbm, two_hbm, first_hbm, second_hbm, unit_ref, plain_ref, feats_ref, first_ref, second_ref, sems):
     depth = first_hbm.shape[0] // PIECES
-    copies = [pltpu.make_async_copy(feats_hbm, feats_ref, sems.at[PIECES])]
+    copies = [
+        pltpu.make_async_copy(one_hbm, feats_ref.at[pl.ds(0, LANES)], sems.at[PIECES]),
+        pltpu.make_async_copy(two_hbm, feats_ref.at[pl.ds(LANES, LANES)], sems.at[PIECES + 1]),
+    ]
     for piece in range(PIECES):
         place = pl.ds(piece * depth, depth)
         copies.append(pltpu.make_async_copy(first_hbm.at[place], first_ref.at[place], sems.at[piece]))
-    copies.append(pltpu.make_async_copy(second_hbm, second_ref, sems.at[PIECES + 1]))
+    copies.append(pltpu.make_async_copy(second_hbm, second_ref, sems.at[PIECES + 2]))
     for copy in copies:
         copy.start()
     copies[0].wait()
-    hidden = jnp.zeros((LANES, first_hbm.shape[1]), F32)
+    copies[1].wait()
+    hidden = None
     for piece in range(PIECES):
-        copies[1 + piece].wait()
+        copies[2 + piece].wait()
         place = slice(piece * depth, (piece + 1) * depth)
-        hidden += jnp.dot(feats_ref[:, place], first_ref[place], preferred_element_type=F32)
+        part = jnp.dot(feats_ref[:, place], first_ref[place], preferred_element_type=F32)
+        hidden = part if hidden is None else hidden + part
     hidden = jnp.maximum(hidden, 0.0).astype(BF16)
     copies[-1].wait()
-    out = jnp.dot(hidden, second_ref[...], preferred_element_type=F32).astype(BF16)
-    if unit:
-        out = unit_of(out)
-    for peer in range(out_ref.shape[0]):
-        out_ref[peer] = out
+    plain = jnp.dot(hidden, second_ref[...], preferred_element_type=F32).astype(BF16)
+    unit_ref[...] = unit_of(plain[:LANES])
+    for peer in range(plain_ref.shape[0]):
+        plain_ref[peer] = plain[LANES:]
 
 
 def unit_kernel(mine_ref, other_ref, plain_ref, unit_ref):
@@ -68,14 +73,23 @@
 
 
 def fill(out_ref, lines_ref):
-    lines = lines_ref[...]
+    lines = lines_ref[...].astype(out_ref.dtype)
     for peer in range(PEERS):
         out_ref[peer] = lines
 
 
-def tile_kernel(left_ref, right_ref, tile_ref, sums_ref, lines_ref):
+def tile_kernel(*refs):
+    *got_refs, right_ref, tile_ref, sums_ref, left_ref, lines_ref = refs
+    for turn, got_ref in enumerate(got_refs):
+        left_ref[turn * SIDES : (turn + 1) * SIDES] = got_ref[...]
+    along_x, along_y = lax.axis_index(ALONG_X), lax.axis_index(ALONG_Y)
+
+    def block_of(place):
+        from_x, from_y = along_x ^ (place // SIDES), along_y ^ (place % SIDES)
+        return left_ref[from_y * SIDES + from_x]
+
     for step in range(PEERS // 2):
-        left = left_ref[2 * step : 2 * step + 2].reshape(2 * LANES, LANES)
+        left = jnp.concatenate([block_of(2 * step), block_of(2 * step + 1)], axis=0)
         rows = slice(step * 2 * LANES, (step + 1) * 2 * LANES)
         parts = jnp.zeros((2 * LANES, LANES), F32)
         for chunk in range(PEERS // 2):
@@ -90,9 +104,9 @@
 
 
 def scale_of(got_ref):
-    total = got_ref[0]
+    total = got_ref[0].astype(F32)
     for peer in range(1, PEERS):
-        total += got_ref[peer]
+        total += got_ref[peer].astype(F32)
     return 1.0 / total
 
 
@@ -158,52 +172,54 @@
     return lax.all_to_all(array, axes, 0, 0)
 
 
-def embed(feats, w_first, w_second, copies, unit):
-    flops = 2 * feats.shape[0] * w_first.shape[0] * w_first.shape[1]
-    return call(
-        functools.partial(embed_kernel, unit=unit),
-        pltpu.VMEM((copies, LANES, LANES), BF16),
-        feats,
+def turned(array, axes):
+    swaps = [[(place, place ^ turn) for place in range(SIDES)] for turn in range(1, SIDES)]
+    return [array] + [lax.ppermute(array, axes, swap) for swap in swaps]
+
+
+def on_device(feats_one, feats_two, w_first, w_second):
+    short = pltpu.VMEM((PEERS, PEERS, LANES), BF16)
+    wide = pltpu.VMEM((PEERS, PEERS, LANES), F32)
+    lines = pltpu.VMEM((PEERS, LANES), F32)
+    block = pltpu.VMEM((SIDE, LANES), BF16)
+    unit_one, plain_two = call(
+        embed_kernel,
+        (pltpu.VMEM((LANES, LANES), BF16), pltpu.VMEM((PEERS // 2, LANES, LANES), BF16)),
+        feats_one,
+        feats_two,
         w_first,
         w_second,
-        in_specs=[pl.BlockSpec(memory_space=pltpu.HBM)] * 3,
+        in_specs=[pl.BlockSpec(memory_space=pltpu.HBM)] * 4,
         limit=60 * 2**20,
         scratch=(
-            pltpu.VMEM(feats.shape, BF16),
+            pltpu.VMEM((2 * LANES, feats_one.shape[1]), BF16),
             pltpu.VMEM(w_first.shape, BF16),
             pltpu.VMEM(w_second.shape, BF16),
-            pltpu.SemaphoreType.DMA((PIECES + 2,)),
+            pltpu.SemaphoreType.DMA((PIECES + 3,)),
         ),
-        flops=flops,
+        flops=4 * LANES * w_first.shape[0] * w_first.shape[1],
     )
-
-
-def on_device(feats_one, feats_two, w_first, w_second):
-    vectors = pltpu.VMEM((PEERS, PEERS, LANES), F32)
-    lines = pltpu.VMEM((PEERS, LANES), F32)
-    block = pltpu.VMEM((SIDE, LANES), BF16)
-    plain_two = embed(feats_two, w_first, w_second, PEERS // 2, False)
     mine = exchange(plain_two, RING)
-    unit_one = embed(feats_one, w_first, w_second, PEERS, True)
-    mine, unit_one = lax.optimization_barrier((mine, unit_one))
     other = lax.ppermute(mine, "c", SWAP)
-    units_left = exchange(unit_one, SAME_ROWS)
+    strip = jnp.stack(turned(unit_one, ALONG_X))
+    units_left = [near(part) for part in turned(strip, ALONG_Y)]
     plains, units_right = call(unit_kernel, (block, block), near(mine), near(other), flops=SIDE * LANES * 8)
     tile, sums = call(
         tile_kernel,
-        (pltpu.VMEM((SIDE, SIDE), F32), vectors),
-        near(units_left),
+        (pltpu.VMEM((SIDE, SIDE), F32), short),
+        *units_left,
         near(units_right),
-        scratch=(lines,),
+        scratch=(pltpu.VMEM((PEERS, LANES, LANES), BF16), lines),
         flops=2 * SIDE * SIDE * LANES,
         exps=SIDE * SIDE,
     )
     tile = near(tile)
     for sweep in range(SWEEPS):
         if sweep:
-            sums = call(rows_kernel, vectors, sums, tile, scratch=(lines,))
+            sums = call(rows_kernel, short, sums, tile, scratch=(lines,))
         sums = near(exchange(sums, SAME_ROWS))
-        sums, row_scale = call(cols_kernel, (vectors, lines), sums, tile, scratch=(lines,))
+        totals = wide if sweep == SWEEPS - 1 else short
+        sums, row_scale = call(cols_kernel, (totals, lines), sums, tile, scratch=(lines,))
         sums = near(exchange(sums, SAME_COLS))
     parts = call(map_kernel, pltpu.VMEM((PEERS, LANES, LANES), BF16), sums, tile, near(plains))
     parts = near(exchange(parts, SAME_ROWS))

time: 137 us -> 130 us (0.949)
  blocking collectives: 86.4 us -> 83.4 us
  Pallas kernels: 17.8 us -> 15.3 us
    ppermute x0 -> x6, starting transfers between devices: none -> 6.75 us  [turned(): return [array] + [lax.ppermute(array, axes, swap) for swap in swaps]]
    all_to_all x2 -> x1, starting transfers between devices: 15.8 us -> 9.03 us  [exchange(): return lax.all_to_all(array, axes, 0, 0)]
    ppermute x0 -> x6, waiting for transfers between devices: none -> 5.75 us  [turned(): return [array] + [lax.ppermute(array, axes, swap) for swap in swaps]]
    all_to_all x2 -> x1, waiting for transfers between devices: 11.9 us -> 7.14 us  [exchange(): return lax.all_to_all(array, axes, 0, 0)]
    all_to_all x7, blocking collectives: 86.4 us -> 83.4 us  [exchange(): return lax.all_to_all(array, axes, 0, 0)]
    pallas_call x11 -> x10, Pallas kernels: 17.8 us -> 15.3 us  [call(): pl.pallas_call(kernel, out_shape=outs, **specs, scratch_shapes=scratch, c...]
  transfers between devices with their start and end apart: 3 -> 8, of which waited for: 3 -> 4; matrix products, arithmetic and copies ran while one was open for 0% -> 0% of each run, Pallas kernels for 3% -> 0%
where the time goes in v5:
time: 130 us
  blocking collectives  83.4 us (64%)
  starting transfers between devices  18.2 us (14%)
  Pallas kernels  15.3 us (12%)
  waiting for transfers between devices  12.9 us (10%)
    all_to_all x7, blocking collectives, exchange(): return lax.all_to_all(array, axes, 0, 0)  83.4 us
    pallas_call x10, Pallas kernels, call(): pl.pallas_call(kernel, out_shape=outs, **specs, scratch_shapes=scratch, c...  15.3 us
    all_to_all x1, starting transfers between devices, exchange(): return lax.all_to_all(array, axes, 0, 0)  9.03 us
    all_to_all x1, waiting for transfers between devices, exchange(): return lax.all_to_all(array, axes, 0, 0)  7.14 us
    ppermute x6, starting transfers between devices, turned(): return [array] + [lax.ppermute(array, axes, swap) for swap in swaps]  6.75 us
    ppermute x6, waiting for transfers between devices, turned(): return [array] + [lax.ppermute(array, axes, swap) for swap in swaps]  5.75 us
  transfers between devices with their start and end apart: 8, of which 4 were waited for; matrix products, arithmetic and copies ran while one was open for 0% of the time, Pallas kernels for 0%

profile of v5, /device:TPU:1, one launch (start us, length us, event | category | flops | bytes accessed | tf_op | source)
XLA Modules:
  0.0 129.9 jit_solution(15719090454033694002)
XLA Ops:
  0.0 3.0 %shard_map.46 = (bf16[128,128]{1,0:T(8,128)(2,1)S(1)}, bf16[8,128,128]{2,1,0:T(8,128)(2,1)}) custom-call(bf16[128,1536]{1,0:T(8,128)(2,1)} %one_hbm.1, bf16[128,1536]{1,0:T(8,128)(2,1)} %two_hbm.1, bf16[1536,512]{1,0:T(8,128)(2,1)} %first_hbm.1, bf16[512,128]{1,0:T(8,128)(2,1)} %second_hbm.1), custom_call_target="tpu_custom_call" | custom-call | flops 402653184 | bytes 2490368 | tf_op jit(solution)/shard_map/pallas_call | solution.py:157
  3.0 9.0 %all-to-all-start = ((bf16[8,128,128]{2,1,0:T(8,128)(2,1)}), bf16[8,128,128]{2,1,0:T(8,128)(2,1)S(1)}, u32[]{:S(2)}, u32[]{:S(2)}) async-start(bf16[8,128,128]{2,1,0:T(8,128)(2,1)} %get-tuple-element.16), calls=%async_computation | async-start | bytes 524288 | tf_op jit(solution)/shard_map/all_to_all | solution.py:172
  12.1 2.5 %collective-permute-start.2 = (bf16[128,128]{1,0:T(8,128)(2,1)S(1)}, bf16[128,128]{1,0:T(8,128)(2,1)S(1)}, u32[]{:S(2)}, u32[]{:S(2)}) collective-permute-start(bf16[128,128]{1,0:T(8,128)(2,1)S(1)} %get-tuple-element.15), channel_id=1, source_target_pairs={{0,192},{64,128},{128,64},{192,0},{1,193},{65,129},{129,65},{193,1... | collective-permute-start | bytes 98312 | tf_op jit(solution)/shard_map/ppermute | solution.py:177
  14.5 0.5 collective-permute-start.1
  15.0 0.3 collective-permute-start
  15.3 7.1 %all-to-all-done.mine_ref = bf16[8,128,128]{2,1,0:T(8,128)(2,1)S(1)} async-done(((bf16[8,128,128]{2,1,0:T(8,128)(2,1)}), bf16[8,128,128]{2,1,0:T(8,128)(2,1)S(1)}, u32[]{:S(2)}, u32[]{:S(2)}) %all-to-all-start) | async-done | bytes 262176 | tf_op jit(solution)/shard_map/all_to_all | solution.py:172
  22.5 2.4 %collective-permute-start.6 = (bf16[8,128,128]{2,1,0:T(8,128)(2,1)S(1)}, bf16[8,128,128]{2,1,0:T(8,128)(2,1)S(1)}, u32[]{:S(2)}, u32[]{:S(2)}) collective-permute-start(bf16[8,128,128]{2,1,0:T(8,128)(2,1)S(1)} %all-to-all-done.mine_ref), channel_id=1, source_target_pairs={{0,16},{16,0},{1,17},{17,1},{2,18},{18,2},{3,19},{19,3},{4,20},{20... | collective-permute-start | bytes 786440 | tf_op jit(solution)/shard_map/ppermute | solution.py:203
  24.9 0.0 collective-permute-done.2
  24.9 0.0 collective-permute-done.1
  24.9 0.0 collective-permute-done
  24.9 2.8 %collective-permute-start.5 = (bf16[4,128,128]{2,1,0:T(8,128)(2,1)S(1)}, bf16[4,128,128]{2,1,0:T(8,128)(2,1)S(1)}, u32[]{:S(2)}, u32[]{:S(2)}) collective-permute-start(bf16[4,128,128]{2,1,0:T(8,128)(2,1)S(1)} %pad_maximum_fusion.refs_0_), channel_id=1, source_target_pairs={{0,12},{4,8},{8,4},{12,0},{1,13},{5,9},{9,5},{13,1},{2,14},{6,10},... | collective-permute-start | bytes 393224 | tf_op jit(solution)/shard_map/ppermute | solution.py:177
  27.7 0.4 collective-permute-start.4
  28.1 0.3 collective-permute-start.3
  28.4 0.0 collective-permute-done.6.other_ref
  28.4 0.6 shard_map.47
  29.0 4.5 %collective-permute-done.5.refs_3_ = bf16[4,128,128]{2,1,0:T(8,128)(2,1)S(1)} collective-permute-done((bf16[4,128,128]{2,1,0:T(8,128)(2,1)S(1)}, bf16[4,128,128]{2,1,0:T(8,128)(2,1)S(1)}, u32[]{:S(2)}, u32[]{:S(2)}) %collective-permute-start.5) | collective-permute-done | bytes 131104 | tf_op jit(solution)/shard_map/ppermute | solution.py:177
  33.5 0.6 collective-permute-done.4.refs_2_
  34.1 0.7 collective-permute-done.3.refs_1_
  34.8 2.5 %shard_map.48 = (f32[2048,2048]{1,0:T(8,128)S(1)}, bf16[16,16,128]{2,1,0:T(8,128)(2,1)S(1)}) custom-call(bf16[4,128,128]{2,1,0:T(8,128)(2,1)S(1)} %pad_maximum_fusion.refs_0_, bf16[4,128,128]{2,1,0:T(8,128)(2,1)S(1)} %collective-permute-done.3.refs_1_, bf16[4,128,128]{2,1,0:T(8,128)(2,1)S(1)} %collective-permute-done.4.refs_2_, ...), custom_call_target="tpu_custom_call" | custom-call | flops 1073741824 | bytes 1048576 | tf_op jit(solution)/shard_map/pallas_call | solution.py:157
  37.3 12.7 %all_to_all.40.got_ref = bf16[16,16,128]{2,1,0:T(8,128)(2,1)S(1)} all-to-all(bf16[16,16,128]{2,1,0:T(8,128)(2,1)S(1)} %get-tuple-element.18), channel_id=1, replica_groups=mesh['xh'=2,'xl'=2,'zh'=2,'c'=2,'yh'=2,'yl'=2,'zm'=2,'zl'=2] {'xh','xl',..., dimensions={0} | all-to-all | bytes 131072 | tf_op jit(solution)/shard_map/all_to_all | solution.py:172
  50.0 1.2 shard_map.49
  51.2 12.8 %all_to_all.41.got_ref = bf16[16,16,128]{2,1,0:T(8,128)(2,1)S(1)} all-to-all(bf16[16,16,128]{2,1,0:T(8,128)(2,1)S(1)} %get-tuple-element.20), channel_id=1, replica_groups=mesh['xh'=2,'xl'=2,'zh'=2,'c'=2,'yh'=2,'yl'=2,'zm'=2,'zl'=2] {'zh','zm',..., dimensions={0} | all-to-all | bytes 131072 | tf_op jit(solution)/shard_map/all_to_all | solution.py:172
  64.0 1.2 shard_map.50
  65.2 9.5 %all_to_all.42.got_ref = bf16[16,16,128]{2,1,0:T(8,128)(2,1)S(1)} all-to-all(bf16[16,16,128]{2,1,0:T(8,128)(2,1)S(1)} %shard_map.50), channel_id=1, replica_groups=mesh['xh'=2,'xl'=2,'zh'=2,'c'=2,'yh'=2,'yl'=2,'zm'=2,'zl'=2] {'xh','xl',..., dimensions={0} | all-to-all | bytes 131072 | tf_op jit(solution)/shard_map/all_to_all | solution.py:172
  74.6 1.2 shard_map.51
  75.8 11.8 %all_to_all.43.got_ref = bf16[16,16,128]{2,1,0:T(8,128)(2,1)S(1)} all-to-all(bf16[16,16,128]{2,1,0:T(8,128)(2,1)S(1)} %get-tuple-element.21), channel_id=1, replica_groups=mesh['xh'=2,'xl'=2,'zh'=2,'c'=2,'yh'=2,'yl'=2,'zm'=2,'zl'=2] {'zh','zm',..., dimensions={0} | all-to-all | bytes 131072 | tf_op jit(solution)/shard_map/all_to_all | solution.py:172
  87.7 1.2 shard_map.52
  88.9 9.5 %all_to_all.44.got_ref = bf16[16,16,128]{2,1,0:T(8,128)(2,1)S(1)} all-to-all(bf16[16,16,128]{2,1,0:T(8,128)(2,1)S(1)} %shard_map.52), channel_id=1, replica_groups=mesh['xh'=2,'xl'=2,'zh'=2,'c'=2,'yh'=2,'yl'=2,'zm'=2,'zl'=2] {'xh','xl',..., dimensions={0} | all-to-all | bytes 131072 | tf_op jit(solution)/shard_map/all_to_all | solution.py:172
  98.3 1.2 shard_map.53
  99.6 13.2 %all_to_all.45.got_ref = f32[16,16,128]{2,1,0:T(8,128)S(1)} all-to-all(f32[16,16,128]{2,1,0:T(8,128)S(1)} %get-tuple-element.22), channel_id=1, replica_groups=mesh['xh'=2,'xl'=2,'zh'=2,'c'=2,'yh'=2,'yl'=2,'zm'=2,'zl'=2] {'zh','zm',..., dimensions={0} | all-to-all | bytes 262144 | tf_op jit(solution)/shard_map/all_to_all | solution.py:172
  112.8 2.4 %shard_map.54 = bf16[16,128,128]{2,1,0:T(8,128)(2,1)S(1)} custom-call(f32[16,16,128]{2,1,0:T(8,128)S(1)} %all_to_all.45.got_ref, f32[2048,2048]{1,0:T(8,128)S(1)} %get-tuple-element.19.tile_ref, bf16[2048,128]{1,0:T(8,128)(2,1)S(1)} %get-tuple-element.23.plain_ref), custom_call_target="tpu_custom_call" | custom-call | bytes 17432576 | tf_op jit(solution)/shard_map/pallas_call | solution.py:157
  115.1 14.0 %all_to_all.46.got_ref = bf16[16,128,128]{2,1,0:T(8,128)(2,1)S(1)} all-to-all(bf16[16,128,128]{2,1,0:T(8,128)(2,1)S(1)} %shard_map.54), channel_id=1, replica_groups=mesh['xh'=2,'xl'=2,'zh'=2,'c'=2,'yh'=2,'yl'=2,'zm'=2,'zl'=2] {'xh','xl',..., dimensions={0} | all-to-all | bytes 1048576 | tf_op jit(solution)/shard_map/all_to_all | solution.py:172
  129.1 0.7 shard_map.55
  (1 shorter events, 0.0 us)
Async XLA Ops:
  3.0 19.4 %all-to-all-start = ((bf16[8,128,128]{2,1,0:T(8,128)(2,1)}), bf16[8,128,128]{2,1,0:T(8,128)(2,1)S(1)}, u32[]{:S(2)}, u32[]{:S(2)}) async-start(bf16[8,128,128]{2,1,0:T(8,128)(2,1)} %get-tuple-element.16), calls=%async_computation | async-start | bytes 524288 | tf_op jit(solution)/shard_map/all_to_all | solution.py:172
  12.1 12.8 %collective-permute-start.2 = (bf16[128,128]{1,0:T(8,128)(2,1)S(1)}, bf16[128,128]{1,0:T(8,128)(2,1)S(1)}, u32[]{:S(2)}, u32[]{:S(2)}) collective-permute-start(bf16[128,128]{1,0:T(8,128)(2,1)S(1)} %get-tuple-element.15), channel_id=1, source_target_pairs={{0,192},{64,128},{128,64},{192,0},{1,193},{65,129},{129,65},{193,1... | collective-permute-start | bytes 98312 | tf_op jit(solution)/shard_map/ppermute | solution.py:177
  14.5 10.4 %collective-permute-start.1 = (bf16[128,128]{1,0:T(8,128)(2,1)S(1)}, bf16[128,128]{1,0:T(8,128)(2,1)S(1)}, u32[]{:S(2)}, u32[]{:S(2)}) collective-permute-start(bf16[128,128]{1,0:T(8,128)(2,1)S(1)} %get-tuple-element.15), channel_id=1, source_target_pairs={{0,128},{64,192},{128,0},{192,64},{1,129},{65,193},{129,1},{193,65... | collective-permute-start | bytes 98312 | tf_op jit(solution)/shard_map/ppermute | solution.py:177
  15.0 9.9 %collective-permute-start = (bf16[128,128]{1,0:T(8,128)(2,1)S(1)}, bf16[128,128]{1,0:T(8,128)(2,1)S(1)}, u32[]{:S(2)}, u32[]{:S(2)}) collective-permute-start(bf16[128,128]{1,0:T(8,128)(2,1)S(1)} %get-tuple-element.15), channel_id=1, source_target_pairs={{0,64},{64,0},{128,192},{192,128},{1,65},{65,1},{129,193},{193,129... | collective-permute-start | bytes 98312 | tf_op jit(solution)/shard_map/ppermute | solution.py:177
  22.5 6.0 %collective-permute-start.6 = (bf16[8,128,128]{2,1,0:T(8,128)(2,1)S(1)}, bf16[8,128,128]{2,1,0:T(8,128)(2,1)S(1)}, u32[]{:S(2)}, u32[]{:S(2)}) collective-permute-start(bf16[8,128,128]{2,1,0:T(8,128)(2,1)S(1)} %all-to-all-done.mine_ref), channel_id=1, source_target_pairs={{0,16},{16,0},{1,17},{17,1},{2,18},{18,2},{3,19},{19,3},{4,20},{20... | collective-permute-start | bytes 786440 | tf_op jit(solution)/shard_map/ppermute | solution.py:203
  24.9 8.6 %collective-permute-start.5 = (bf16[4,128,128]{2,1,0:T(8,128)(2,1)S(1)}, bf16[4,128,128]{2,1,0:T(8,128)(2,1)S(1)}, u32[]{:S(2)}, u32[]{:S(2)}) collective-permute-start(bf16[4,128,128]{2,1,0:T(8,128)(2,1)S(1)} %pad_maximum_fusion.refs_0_), channel_id=1, source_target_pairs={{0,12},{4,8},{8,4},{12,0},{1,13},{5,9},{9,5},{13,1},{2,14},{6,10},... | collective-permute-start | bytes 393224 | tf_op jit(solution)/shard_map/ppermute | solution.py:177
  27.7 6.3 %collective-permute-start.4 = (bf16[4,128,128]{2,1,0:T(8,128)(2,1)S(1)}, bf16[4,128,128]{2,1,0:T(8,128)(2,1)S(1)}, u32[]{:S(2)}, u32[]{:S(2)}) collective-permute-start(bf16[4,128,128]{2,1,0:T(8,128)(2,1)S(1)} %pad_maximum_fusion.refs_0_), channel_id=1, source_target_pairs={{0,8},{4,12},{8,0},{12,4},{1,9},{5,13},{9,1},{13,5},{2,10},{6,14},... | collective-permute-start | bytes 393224 | tf_op jit(solution)/shard_map/ppermute | solution.py:177
  28.1 6.7 %collective-permute-start.3 = (bf16[4,128,128]{2,1,0:T(8,128)(2,1)S(1)}, bf16[4,128,128]{2,1,0:T(8,128)(2,1)S(1)}, u32[]{:S(2)}, u32[]{:S(2)}) collective-permute-start(bf16[4,128,128]{2,1,0:T(8,128)(2,1)S(1)} %pad_maximum_fusion.refs_0_), channel_id=1, source_target_pairs={{0,4},{4,0},{8,12},{12,8},{1,5},{5,1},{9,13},{13,9},{2,6},{6,2},{1... | collective-permute-start | bytes 393224 | tf_op jit(solution)/shard_map/ppermute | solution.py:177

commit v6 on v5

--- a/solution.py
+++ b/solution.py
@@ -59,15 +59,6 @@
         plain_ref[peer] = plain[LANES:]
 
 
-def unit_kernel(mine_ref, other_ref, plain_ref, unit_ref):
-    core = lax.axis_index("c")
-    for half, got_ref in ((core, mine_ref), (1 - core, other_ref)):
-        place = pl.ds(pl.multiple_of(half * HALF, HALF), HALF)
-        plain = got_ref[...].reshape(HALF, LANES)
-        plain_ref[place, :] = plain
-        unit_ref[place, :] = unit_of(plain)
-
-
 def row_totals(parts):
     return jnp.sum(parts.T, axis=0, keepdims=True)
 
@@ -78,29 +69,42 @@
         out_ref[peer] = lines
 
 
-def tile_kernel(*refs):
-    *got_refs, right_ref, tile_ref, sums_ref, left_ref, lines_ref = refs
-    for turn, got_ref in enumerate(got_refs):
-        left_ref[turn * SIDES : (turn + 1) * SIDES] = got_ref[...]
-    along_x, along_y = lax.axis_index(ALONG_X), lax.axis_index(ALONG_Y)
-
-    def block_of(place):
-        from_x, from_y = along_x ^ (place // SIDES), along_y ^ (place % SIDES)
-        return left_ref[from_y * SIDES + from_x]
-
+def half_tile(left_ref, plain_ref, tile_ref, units_ref, lines_ref):
+    units_ref[...] = unit_of(plain_ref[...].reshape(HALF, LANES))
     for step in range(PEERS // 2):
-        left = jnp.concatenate([block_of(2 * step), block_of(2 * step + 1)], axis=0)
+        left = left_ref[2 * step : 2 * step + 2].reshape(2 * LANES, LANES)
         rows = slice(step * 2 * LANES, (step + 1) * 2 * LANES)
         parts = jnp.zeros((2 * LANES, LANES), F32)
-        for chunk in range(PEERS // 2):
+        for chunk in range(PEERS // 4):
             cols = slice(chunk * 2 * LANES, (chunk + 1) * 2 * LANES)
-            dots = lax.dot_general(left, right_ref[cols], (((1,), (1,)), ((), ())), preferred_element_type=F32)
+            dots = lax.dot_general(left, units_ref[cols], (((1,), (1,)), ((), ())), preferred_element_type=F32)
             block = jnp.exp2(dots * EXPONENT)
             tile_ref[rows, cols] = block
             parts += block[:, :LANES] + block[:, LANES:]
         lines_ref[2 * step : 2 * step + 1] = row_totals(parts[:LANES])
         lines_ref[2 * step + 1 : 2 * step + 2] = row_totals(parts[LANES:])
+
+
+def mine_kernel(*refs):
+    *got_refs, plain_ref, tile_ref, left_ref, lines_ref, held_ref, units_ref = refs
+    for turn, got_ref in enumerate(got_refs):
+        held_ref[turn * SIDES : (turn + 1) * SIDES] = got_ref[...]
+    along_x, along_y = lax.axis_index(ALONG_X), lax.axis_index(ALONG_Y)
+    for place in range(PEERS):
+        from_x, from_y = along_x ^ (place // SIDES), along_y ^ (place % SIDES)
+        left_ref[place] = held_ref[from_y * SIDES + from_x]
+    half_tile(left_ref, plain_ref, tile_ref, units_ref, lines_ref)
+
+
+def other_kernel(left_ref, plain_ref, first_ref, tile_ref, sums_ref, units_ref, lines_ref):
+    half_tile(left_ref, plain_ref, tile_ref, units_ref, lines_ref)
+    lines_ref[...] += first_ref[...]
     fill(sums_ref, lines_ref)
+
+
+def core_lines():
+    core = lax.axis_index("c")
+    return [pl.ds(pl.multiple_of(half * (PEERS // 2), PEERS // 2), PEERS // 2) for half in (core, 1 - core)]
 
 
 def scale_of(got_ref):
@@ -110,37 +114,52 @@
     return 1.0 / total
 
 
-def cols_kernel(got_ref, tile_ref, sums_ref, scale_ref, lines_ref):
+def cols_kernel(got_ref, mine_ref, other_ref, sums_ref, scale_ref, lines_ref):
     scale = scale_of(got_ref)
     scale_ref[...] = scale
+    chunks = PEERS // 2
     parts = [jnp.zeros((8, LANES), F32) for _ in range(PEERS)]
     for block in range(PEERS):
         rows = slice(block * LANES, (block + 1) * LANES)
         factor = jnp.broadcast_to(scale[block : block + 1], (LANES, LANES)).T
         for chunk in range(PEERS):
-            product = tile_ref[rows, chunk * LANES : (chunk + 1) * LANES] * factor
+            half_ref, at = (mine_ref, other_ref)[chunk // chunks], chunk % chunks
+            product = half_ref[rows, at * LANES : (at + 1) * LANES] * factor
             parts[chunk] += jnp.sum(product.reshape(LANES // 8, 8, LANES), axis=0)
-    for chunk in range(PEERS):
-        lines_ref[chunk : chunk + 1] = jnp.sum(parts[chunk], axis=0, keepdims=True)
+    lines = [jnp.sum(part, axis=0, keepdims=True) for part in parts]
+    for half, place in enumerate(core_lines()):
+        lines_ref[place] = jnp.concatenate(lines[half * chunks : (half + 1) * chunks], axis=0)
     fill(sums_ref, lines_ref)
 
 
-def rows_kernel(got_ref, tile_ref, sums_ref, lines_ref):
-    scale = scale_of(got_ref)
+def local_scale(got_ref, lines_ref):
+    lines_ref[...] = scale_of(got_ref)
+    halves = [lines_ref[place] for place in core_lines()]
+    return [half[row : row + 1] for half in halves for row in range(PEERS // 2)]
+
+
+def rows_kernel(got_ref, mine_ref, other_ref, sums_ref, lines_ref):
+    scale = local_scale(got_ref, lines_ref)
     for block in range(PEERS):
         rows = slice(block * LANES, (block + 1) * LANES)
-        parts = tile_ref[rows, :LANES] * scale[:1]
-        for chunk in range(1, PEERS):
-            parts += tile_ref[rows, chunk * LANES : (chunk + 1) * LANES] * scale[chunk : chunk + 1]
+        parts = None
+        for chunk in range(PEERS):
+            half_ref, at = (mine_ref, other_ref)[2 * chunk // PEERS], chunk % (PEERS // 2)
+            product = half_ref[rows, at * LANES : (at + 1) * LANES] * scale[chunk]
+            parts = product if parts is None else parts + product
         lines_ref[block : block + 1] = row_totals(parts)
     fill(sums_ref, lines_ref)
 
 
-def map_kernel(got_ref, tile_ref, plain_ref, out_ref):
-    scale = scale_of(got_ref)
-    wide = jnp.concatenate([scale[chunk : chunk + 1] for chunk in range(PEERS)], axis=1)
-    scaled = (tile_ref[...] * wide).astype(BF16)
-    part = jnp.dot(scaled, plain_ref[...], preferred_element_type=F32)
+def map_kernel(got_ref, mine_ref, other_ref, plain_mine_ref, plain_other_ref, out_ref, lines_ref):
+    scale = local_scale(got_ref, lines_ref)
+    part = None
+    for half, (tile_ref, plain_ref) in enumerate(((mine_ref, plain_mine_ref), (other_ref, plain_other_ref))):
+        wide = jnp.concatenate(scale[half * PEERS // 2 : (half + 1) * PEERS // 2], axis=1)
+        scaled = (tile_ref[...] * wide).astype(BF16)
+        plain = plain_ref[...].reshape(HALF, LANES)
+        product = jnp.dot(scaled, plain, preferred_element_type=F32)
+        part = product if part is None else part + product
     out_ref[...] = part.reshape(PEERS, LANES, LANES).astype(BF16)
 
 
@@ -181,7 +200,6 @@
     short = pltpu.VMEM((PEERS, PEERS, LANES), BF16)
     wide = pltpu.VMEM((PEERS, PEERS, LANES), F32)
     lines = pltpu.VMEM((PEERS, LANES), F32)
-    block = pltpu.VMEM((SIDE, LANES), BF16)
     unit_one, plain_two = call(
         embed_kernel,
         (pltpu.VMEM((LANES, LANES), BF16), pltpu.VMEM((PEERS // 2, LANES, LANES), BF16)),
@@ -200,28 +218,25 @@
         flops=4 * LANES * w_first.shape[0] * w_first.shape[1],
     )
     mine = exchange(plain_two, RING)
+    strip = jnp.stack(turned(unit_one, ALONG_X))
+    mine, *units_left = lax.optimization_barrier((mine, *turned(strip, ALONG_Y)))
+    units_left = [near(part) for part in units_left]
     other = lax.ppermute(mine, "c", SWAP)
-    strip = jnp.stack(turned(unit_one, ALONG_X))
-    units_left = [near(part) for part in turned(strip, ALONG_Y)]
-    plains, units_right = call(unit_kernel, (block, block), near(mine), near(other), flops=SIDE * LANES * 8)
-    tile, sums = call(
-        tile_kernel,
-        (pltpu.VMEM((SIDE, SIDE), F32), short),
-        *units_left,
-        near(units_right),
-        scratch=(pltpu.VMEM((PEERS, LANES, LANES), BF16), lines),
-        flops=2 * SIDE * SIDE * LANES,
-        exps=SIDE * SIDE,
-    )
-    tile = near(tile)
+    half, units = pltpu.VMEM((SIDE, HALF), F32), pltpu.VMEM((HALF, LANES), BF16)
+    blocks = pltpu.VMEM((PEERS, LANES, LANES), BF16)
+    work = dict(flops=2 * SIDE * HALF * LANES, exps=SIDE * HALF)
+    mine, other = near(mine), near(other)
+    tile_mine, left, first = call(mine_kernel, (half, blocks, lines), *units_left, mine, scratch=(blocks, units), **work)
+    tile_other, sums = call(other_kernel, (half, short), near(left), other, near(first), scratch=(units, lines), **work)
+    tile = (near(tile_mine), near(tile_other))
     for sweep in range(SWEEPS):
         if sweep:
-            sums = call(rows_kernel, short, sums, tile, scratch=(lines,))
+            sums = call(rows_kernel, short, sums, *tile, scratch=(lines,))
         sums = near(exchange(sums, SAME_ROWS))
         totals = wide if sweep == SWEEPS - 1 else short
-        sums, row_scale = call(cols_kernel, (totals, lines), sums, tile, scratch=(lines,))
+        sums, row_scale = call(cols_kernel, (totals, lines), sums, *tile, scratch=(lines,))
         sums = near(exchange(sums, SAME_COLS))
-    parts = call(map_kernel, pltpu.VMEM((PEERS, LANES, LANES), BF16), sums, tile, near(plains))
+    parts = call(map_kernel, blocks, sums, *tile, mine, other, scratch=(lines,))
     parts = near(exchange(parts, SAME_ROWS))
     return call(finish_kernel, jax.ShapeDtypeStruct((LANES, LANES), F32), parts, row_scale)
 

time: 130 us -> 129 us (level)
  waiting for transfers between devices: 12.9 us -> 8.4 us
  blocking collectives: 83.4 us -> 85.2 us
    all_to_all x1, waiting for transfers between devices: 7.14 us -> 0.01 us  [exchange(): return lax.all_to_all(array, axes, 0, 0)]
    ppermute x6, waiting for transfers between devices: 5.75 us -> 8.39 us  [turned(): return [array] + [lax.ppermute(array, axes, swap) for swap in swaps]]
    all_to_all x7, blocking collectives: 83.4 us -> 85.2 us  [exchange(): return lax.all_to_all(array, axes, 0, 0)]
  transfers between devices with their start and end apart: 8 -> 8, of which waited for: 4 -> 4; matrix products, arithmetic and copies ran while one was open for 0% -> 0% of each run, Pallas kernels for 0% -> 1%
where the time goes in v6:
time: 129 us
  blocking collectives  85.2 us (66%)
  starting transfers between devices  19.3 us (15%)
  Pallas kernels  15.5 us (12%)
  waiting for transfers between devices  8.4 us (7%)
    all_to_all x7, blocking collectives, exchange(): return lax.all_to_all(array, axes, 0, 0)  85.2 us
    pallas_call x10, Pallas kernels, call(): pl.pallas_call(kernel, out_shape=outs, **specs, scratch_shapes=scratch, c...  15.5 us
    all_to_all x1, starting transfers between devices, exchange(): return lax.all_to_all(array, axes, 0, 0)  9.03 us
    ppermute x6, waiting for transfers between devices, turned(): return [array] + [lax.ppermute(array, axes, swap) for swap in swaps]  8.39 us
    ppermute x6, starting transfers between devices, turned(): return [array] + [lax.ppermute(array, axes, swap) for swap in swaps]  6.74 us
    ppermute x1, starting transfers between devices, on_device(): other = lax.ppermute(mine, 'c', SWAP)  3.58 us
  transfers between devices with their start and end apart: 8, of which 4 were waited for; matrix products, arithmetic and copies ran while one was open for 0% of the time, Pallas kernels for 1%

profile of v6, /device:TPU:1, one launch (start us, length us, event | category | flops | bytes accessed | tf_op | source)
XLA Modules:
  0.0 128.6 jit_solution(11710382876144724917)
XLA Ops:
  0.0 3.0 %shard_map.46 = (bf16[128,128]{1,0:T(8,128)(2,1)S(1)}, bf16[8,128,128]{2,1,0:T(8,128)(2,1)}) custom-call(bf16[128,1536]{1,0:T(8,128)(2,1)} %one_hbm.1, bf16[128,1536]{1,0:T(8,128)(2,1)} %two_hbm.1, bf16[1536,512]{1,0:T(8,128)(2,1)} %first_hbm.1, bf16[512,128]{1,0:T(8,128)(2,1)} %second_hbm.1), custom_call_target="tpu_custom_call" | custom-call | flops 402653184 | bytes 2490368 | tf_op jit(solution)/shard_map/pallas_call | solution.py:176
  3.0 9.0 %all-to-all-start = ((bf16[8,128,128]{2,1,0:T(8,128)(2,1)}), bf16[8,128,128]{2,1,0:T(8,128)(2,1)S(1)}, u32[]{:S(2)}, u32[]{:S(2)}) async-start(bf16[8,128,128]{2,1,0:T(8,128)(2,1)} %get-tuple-element.21), calls=%async_computation | async-start | bytes 524288 | tf_op jit(solution)/shard_map/all_to_all | solution.py:191
  12.1 2.5 %collective-permute-start.2 = (bf16[128,128]{1,0:T(8,128)(2,1)S(1)}, bf16[128,128]{1,0:T(8,128)(2,1)S(1)}, u32[]{:S(2)}, u32[]{:S(2)}) collective-permute-start(bf16[128,128]{1,0:T(8,128)(2,1)S(1)} %get-tuple-element.22), channel_id=1, source_target_pairs={{0,192},{64,128},{128,64},{192,0},{1,193},{65,129},{129,65},{193,1... | collective-permute-start | bytes 98312 | tf_op jit(solution)/shard_map/ppermute | solution.py:196
  14.5 0.5 collective-permute-start.1
  15.0 0.3 collective-permute-start
  15.3 0.7 collective-permute-done.2
  16.0 2.9 %collective-permute-done.1 = bf16[128,128]{1,0:T(8,128)(2,1)S(1)} collective-permute-done((bf16[128,128]{1,0:T(8,128)(2,1)S(1)}, bf16[128,128]{1,0:T(8,128)(2,1)S(1)}, u32[]{:S(2)}, u32[]{:S(2)}) %collective-permute-start.1) | collective-permute-done | bytes 32800 | tf_op jit(solution)/shard_map/ppermute | solution.py:196
  18.9 0.0 collective-permute-done
  19.0 2.8 %collective-permute-start.5 = (bf16[4,128,128]{2,1,0:T(8,128)(2,1)S(1)}, bf16[4,128,128]{2,1,0:T(8,128)(2,1)S(1)}, u32[]{:S(2)}, u32[]{:S(2)}) collective-permute-start(bf16[4,128,128]{2,1,0:T(8,128)(2,1)S(1)} %pad_maximum_fusion.refs_0_), channel_id=1, source_target_pairs={{0,12},{4,8},{8,4},{12,0},{1,13},{5,9},{9,5},{13,1},{2,14},{6,10},... | collective-permute-start | bytes 393224 | tf_op jit(solution)/shard_map/ppermute | solution.py:196
  21.8 0.4 collective-permute-start.4
  22.1 0.3 collective-permute-start.3
  22.5 2.6 %collective-permute-done.5.refs_3_ = bf16[4,128,128]{2,1,0:T(8,128)(2,1)S(1)} collective-permute-done((bf16[4,128,128]{2,1,0:T(8,128)(2,1)S(1)}, bf16[4,128,128]{2,1,0:T(8,128)(2,1)S(1)}, u32[]{:S(2)}, u32[]{:S(2)}) %collective-permute-start.5) | collective-permute-done | bytes 131104 | tf_op jit(solution)/shard_map/ppermute | solution.py:196
  25.1 2.1 %collective-permute-done.4.refs_2_ = bf16[4,128,128]{2,1,0:T(8,128)(2,1)S(1)} collective-permute-done((bf16[4,128,128]{2,1,0:T(8,128)(2,1)S(1)}, bf16[4,128,128]{2,1,0:T(8,128)(2,1)S(1)}, u32[]{:S(2)}, u32[]{:S(2)}) %collective-permute-start.4) | collective-permute-done | bytes 131104 | tf_op jit(solution)/shard_map/ppermute | solution.py:196
  27.2 0.0 collective-permute-done.3.refs_1_
  27.2 0.0 all-to-all-done.refs_4_.plain_mine_ref
  27.2 3.6 %collective-permute-start.6 = (bf16[8,128,128]{2,1,0:T(8,128)(2,1)S(1)}, bf16[8,128,128]{2,1,0:T(8,128)(2,1)S(1)}, u32[]{:S(2)}, u32[]{:S(2)}) collective-permute-start(bf16[8,128,128]{2,1,0:T(8,128)(2,1)S(1)} %all-to-all-done.refs_4_.plain_mine_ref), channel_id=1, source_target_pairs={{0,16},{16,0},{1,17},{17,1},{2,18},{18,2},{3,19},{19,3},{4,20},{20... | collective-permute-start | bytes 786440 | tf_op jit(solution)/shard_map/ppermute | solution.py:224
  30.8 1.6 %shard_map.47 = (f32[2048,1024]{1,0:T(8,128)S(1)}, bf16[16,128,128]{2,1,0:T(8,128)(2,1)S(1)}, f32[16,128]{1,0:T(8,128)S(1)}) custom-call(bf16[4,128,128]{2,1,0:T(8,128)(2,1)S(1)} %pad_maximum_fusion.refs_0_, bf16[4,128,128]{2,1,0:T(8,128)(2,1)S(1)} %collective-permute-done.3.refs_1_, bf16[4,128,128]{2,1,0:T(8,128)(2,1)S(1)} %collective-permute-done.4.refs_2_, ...), custom_call_target="tpu_custom_call" | custom-call | flops 536870912 | bytes 786432 | tf_op jit(solution)/shard_map/pallas_call | solution.py:176
  32.4 0.0 collective-permute-done.6.plain_ref.plain_other_ref
  32.4 1.7 %shard_map.48 = (f32[2048,1024]{1,0:T(8,128)S(1)}, bf16[16,16,128]{2,1,0:T(8,128)(2,1)S(1)}) custom-call(bf16[16,128,128]{2,1,0:T(8,128)(2,1)S(1)} %get-tuple-element.28.left_ref, bf16[8,128,128]{2,1,0:T(8,128)(2,1)S(1)} %collective-permute-done.6.plain_ref.plain_other_ref, f32[16,128]{1,0:T(8,128)S(1)} %get-tuple-element.29.first_ref), custom_call_target="tpu_custom_call" | custom-call | flops 536870912 | bytes 794624 | tf_op jit(solution)/shard_map/pallas_call | solution.py:176
  34.1 11.0 %all_to_all.40.got_ref = bf16[16,16,128]{2,1,0:T(8,128)(2,1)S(1)} all-to-all(bf16[16,16,128]{2,1,0:T(8,128)(2,1)S(1)} %get-tuple-element.30), channel_id=1, replica_groups=mesh['xh'=2,'xl'=2,'zh'=2,'c'=2,'yh'=2,'yl'=2,'zm'=2,'zl'=2] {'xh','xl',..., dimensions={0} | all-to-all | bytes 131072 | tf_op jit(solution)/shard_map/all_to_all | solution.py:191
  45.1 1.2 shard_map.49
  46.4 16.3 %all_to_all.41.got_ref = bf16[16,16,128]{2,1,0:T(8,128)(2,1)S(1)} all-to-all(bf16[16,16,128]{2,1,0:T(8,128)(2,1)S(1)} %get-tuple-element.33), channel_id=1, replica_groups=mesh['xh'=2,'xl'=2,'zh'=2,'c'=2,'yh'=2,'yl'=2,'zm'=2,'zl'=2] {'zh','zm',..., dimensions={0} | all-to-all | bytes 131072 | tf_op jit(solution)/shard_map/all_to_all | solution.py:191
  62.6 1.2 shard_map.50
  63.8 9.5 %all_to_all.42.got_ref = bf16[16,16,128]{2,1,0:T(8,128)(2,1)S(1)} all-to-all(bf16[16,16,128]{2,1,0:T(8,128)(2,1)S(1)} %shard_map.50), channel_id=1, replica_groups=mesh['xh'=2,'xl'=2,'zh'=2,'c'=2,'yh'=2,'yl'=2,'zm'=2,'zl'=2] {'xh','xl',..., dimensions={0} | all-to-all | bytes 131072 | tf_op jit(solution)/shard_map/all_to_all | solution.py:191
  73.3 1.2 shard_map.51
  74.5 11.8 %all_to_all.43.got_ref = bf16[16,16,128]{2,1,0:T(8,128)(2,1)S(1)} all-to-all(bf16[16,16,128]{2,1,0:T(8,128)(2,1)S(1)} %get-tuple-element.34), channel_id=1, replica_groups=mesh['xh'=2,'xl'=2,'zh'=2,'c'=2,'yh'=2,'yl'=2,'zm'=2,'zl'=2] {'zh','zm',..., dimensions={0} | all-to-all | bytes 131072 | tf_op jit(solution)/shard_map/all_to_all | solution.py:191
  86.4 1.2 shard_map.52
  87.6 9.5 %all_to_all.44.got_ref = bf16[16,16,128]{2,1,0:T(8,128)(2,1)S(1)} all-to-all(bf16[16,16,128]{2,1,0:T(8,128)(2,1)S(1)} %shard_map.52), channel_id=1, replica_groups=mesh['xh'=2,'xl'=2,'zh'=2,'c'=2,'yh'=2,'yl'=2,'zm'=2,'zl'=2] {'xh','xl',..., dimensions={0} | all-to-all | bytes 131072 | tf_op jit(solution)/shard_map/all_to_all | solution.py:191
  97.0 1.2 shard_map.53
  98.3 13.2 %all_to_all.45.got_ref = f32[16,16,128]{2,1,0:T(8,128)S(1)} all-to-all(f32[16,16,128]{2,1,0:T(8,128)S(1)} %get-tuple-element.35), channel_id=1, replica_groups=mesh['xh'=2,'xl'=2,'zh'=2,'c'=2,'yh'=2,'yl'=2,'zm'=2,'zl'=2] {'zh','zm',..., dimensions={0} | all-to-all | bytes 262144 | tf_op jit(solution)/shard_map/all_to_all | solution.py:191
  111.5 2.4 %shard_map.54 = bf16[16,128,128]{2,1,0:T(8,128)(2,1)S(1)} custom-call(f32[16,16,128]{2,1,0:T(8,128)S(1)} %all_to_all.45.got_ref, f32[2048,1024]{1,0:T(8,128)S(1)} %get-tuple-element.31.mine_ref, f32[2048,1024]{1,0:T(8,128)S(1)} %get-tuple-element.32.other_ref, bf16[8,128,128]{2,1,0:T(8,128)(2,1)S(1)} %all-to-all-done.refs_4_.plain_mine_ref, ...), custom_call_target="tpu_custom_call" | custom-call | bytes 17432576 | tf_op jit(solution)/shard_map/pallas_call | solution.py:176
  113.8 14.0 %all_to_all.46.got_ref = bf16[16,128,128]{2,1,0:T(8,128)(2,1)S(1)} all-to-all(bf16[16,128,128]{2,1,0:T(8,128)(2,1)S(1)} %shard_map.54), channel_id=1, replica_groups=mesh['xh'=2,'xl'=2,'zh'=2,'c'=2,'yh'=2,'yl'=2,'zm'=2,'zl'=2] {'xh','xl',..., dimensions={0} | all-to-all | bytes 1048576 | tf_op jit(solution)/shard_map/all_to_all | solution.py:191
  127.9 0.7 shard_map.55
  (1 shorter events, 0.0 us)
Async XLA Ops:
  3.0 24.2 %all-to-all-start = ((bf16[8,128,128]{2,1,0:T(8,128)(2,1)}), bf16[8,128,128]{2,1,0:T(8,128)(2,1)S(1)}, u32[]{:S(2)}, u32[]{:S(2)}) async-start(bf16[8,128,128]{2,1,0:T(8,128)(2,1)} %get-tuple-element.21), calls=%async_computation | async-start | bytes 524288 | tf_op jit(solution)/shard_map/all_to_all | solution.py:191
  12.1 4.0 %collective-permute-start.2 = (bf16[128,128]{1,0:T(8,128)(2,1)S(1)}, bf16[128,128]{1,0:T(8,128)(2,1)S(1)}, u32[]{:S(2)}, u32[]{:S(2)}) collective-permute-start(bf16[128,128]{1,0:T(8,128)(2,1)S(1)} %get-tuple-element.22), channel_id=1, source_target_pairs={{0,192},{64,128},{128,64},{192,0},{1,193},{65,129},{129,65},{193,1... | collective-permute-start | bytes 98312 | tf_op jit(solution)/shard_map/ppermute | solution.py:196
  14.5 4.4 %collective-permute-start.1 = (bf16[128,128]{1,0:T(8,128)(2,1)S(1)}, bf16[128,128]{1,0:T(8,128)(2,1)S(1)}, u32[]{:S(2)}, u32[]{:S(2)}) collective-permute-start(bf16[128,128]{1,0:T(8,128)(2,1)S(1)} %get-tuple-element.22), channel_id=1, source_target_pairs={{0,128},{64,192},{128,0},{192,64},{1,129},{65,193},{129,1},{193,65... | collective-permute-start | bytes 98312 | tf_op jit(solution)/shard_map/ppermute | solution.py:196
  15.0 3.9 %collective-permute-start = (bf16[128,128]{1,0:T(8,128)(2,1)S(1)}, bf16[128,128]{1,0:T(8,128)(2,1)S(1)}, u32[]{:S(2)}, u32[]{:S(2)}) collective-permute-start(bf16[128,128]{1,0:T(8,128)(2,1)S(1)} %get-tuple-element.22), channel_id=1, source_target_pairs={{0,64},{64,0},{128,192},{192,128},{1,65},{65,1},{129,193},{193,129... | collective-permute-start | bytes 98312 | tf_op jit(solution)/shard_map/ppermute | solution.py:196
  19.0 6.1 %collective-permute-start.5 = (bf16[4,128,128]{2,1,0:T(8,128)(2,1)S(1)}, bf16[4,128,128]{2,1,0:T(8,128)(2,1)S(1)}, u32[]{:S(2)}, u32[]{:S(2)}) collective-permute-start(bf16[4,128,128]{2,1,0:T(8,128)(2,1)S(1)} %pad_maximum_fusion.refs_0_), channel_id=1, source_target_pairs={{0,12},{4,8},{8,4},{12,0},{1,13},{5,9},{9,5},{13,1},{2,14},{6,10},... | collective-permute-start | bytes 393224 | tf_op jit(solution)/shard_map/ppermute | solution.py:196
  21.8 5.4 %collective-permute-start.4 = (bf16[4,128,128]{2,1,0:T(8,128)(2,1)S(1)}, bf16[4,128,128]{2,1,0:T(8,128)(2,1)S(1)}, u32[]{:S(2)}, u32[]{:S(2)}) collective-permute-start(bf16[4,128,128]{2,1,0:T(8,128)(2,1)S(1)} %pad_maximum_fusion.refs_0_), channel_id=1, source_target_pairs={{0,8},{4,12},{8,0},{12,4},{1,9},{5,13},{9,1},{13,5},{2,10},{6,14},... | collective-permute-start | bytes 393224 | tf_op jit(solution)/shard_map/ppermute | solution.py:196
  22.1 5.1 %collective-permute-start.3 = (bf16[4,128,128]{2,1,0:T(8,128)(2,1)S(1)}, bf16[4,128,128]{2,1,0:T(8,128)(2,1)S(1)}, u32[]{:S(2)}, u32[]{:S(2)}) collective-permute-start(bf16[4,128,128]{2,1,0:T(8,128)(2,1)S(1)} %pad_maximum_fusion.refs_0_), channel_id=1, source_target_pairs={{0,4},{4,0},{8,12},{12,8},{1,5},{5,1},{9,13},{13,9},{2,6},{6,2},{1... | collective-permute-start | bytes 393224 | tf_op jit(solution)/shard_map/ppermute | solution.py:196
  27.2 5.2 %collective-permute-start.6 = (bf16[8,128,128]{2,1,0:T(8,128)(2,1)S(1)}, bf16[8,128,128]{2,1,0:T(8,128)(2,1)S(1)}, u32[]{:S(2)}, u32[]{:S(2)}) collective-permute-start(bf16[8,128,128]{2,1,0:T(8,128)(2,1)S(1)} %all-to-all-done.refs_4_.plain_mine_ref), channel_id=1, source_target_pairs={{0,16},{16,0},{1,17},{17,1},{2,18},{18,2},{3,19},{19,3},{4,20},{20... | collective-permute-start | bytes 786440 | tf_op jit(solution)/shard_map/ppermute | solution.py:224

commit v7 on v6

--- a/solution.py
+++ b/solution.py
@@ -10,6 +10,7 @@
 
 SWEEPS = 3
 PIECES = 6
+FLOPS_HINT = 10**9
 PEERS = 16
 LANES = 128
 SIDE = PEERS * LANES
@@ -69,15 +70,14 @@
         out_ref[peer] = lines
 
 
-def half_tile(left_ref, plain_ref, tile_ref, units_ref, lines_ref):
-    units_ref[...] = unit_of(plain_ref[...].reshape(HALF, LANES))
+def half_tile(left_ref, rows_ref, tile_ref, lines_ref):
     for step in range(PEERS // 2):
         left = left_ref[2 * step : 2 * step + 2].reshape(2 * LANES, LANES)
         rows = slice(step * 2 * LANES, (step + 1) * 2 * LANES)
         parts = jnp.zeros((2 * LANES, LANES), F32)
         for chunk in range(PEERS // 4):
             cols = slice(chunk * 2 * LANES, (chunk + 1) * 2 * LANES)
-            dots = lax.dot_general(left, units_ref[cols], (((1,), (1,)), ((), ())), preferred_element_type=F32)
+            dots = lax.dot_general(left, rows_ref[0, cols], (((1,), (1,)), ((), ())), preferred_element_type=F32)
             block = jnp.exp2(dots * EXPONENT)
             tile_ref[rows, cols] = block
             parts += block[:, :LANES] + block[:, LANES:]
@@ -85,19 +85,25 @@
         lines_ref[2 * step + 1 : 2 * step + 2] = row_totals(parts[LANES:])
 
 
+def unit_kernel(plain_ref, rows_ref):
+    plain = plain_ref[...].reshape(HALF, LANES)
+    rows_ref[0] = unit_of(plain)
+    rows_ref[1] = plain
+
+
 def mine_kernel(*refs):
-    *got_refs, plain_ref, tile_ref, left_ref, lines_ref, held_ref, units_ref = refs
+    *got_refs, rows_ref, tile_ref, left_ref, lines_ref, held_ref = refs
     for turn, got_ref in enumerate(got_refs):
         held_ref[turn * SIDES : (turn + 1) * SIDES] = got_ref[...]
     along_x, along_y = lax.axis_index(ALONG_X), lax.axis_index(ALONG_Y)
     for place in range(PEERS):
         from_x, from_y = along_x ^ (place // SIDES), along_y ^ (place % SIDES)
         left_ref[place] = held_ref[from_y * SIDES + from_x]
-    half_tile(left_ref, plain_ref, tile_ref, units_ref, lines_ref)
-
-
-def other_kernel(left_ref, plain_ref, first_ref, tile_ref, sums_ref, units_ref, lines_ref):
-    half_tile(left_ref, plain_ref, tile_ref, units_ref, lines_ref)
+    half_tile(left_ref, rows_ref, tile_ref, lines_ref)
+
+
+def other_kernel(left_ref, rows_ref, first_ref, tile_ref, sums_ref, lines_ref):
+    half_tile(left_ref, rows_ref, tile_ref, lines_ref)
     lines_ref[...] += first_ref[...]
     fill(sums_ref, lines_ref)
 
@@ -157,8 +163,7 @@
     for half, (tile_ref, plain_ref) in enumerate(((mine_ref, plain_mine_ref), (other_ref, plain_other_ref))):
         wide = jnp.concatenate(scale[half * PEERS // 2 : (half + 1) * PEERS // 2], axis=1)
         scaled = (tile_ref[...] * wide).astype(BF16)
-        plain = plain_ref[...].reshape(HALF, LANES)
-        product = jnp.dot(scaled, plain, preferred_element_type=F32)
+        product = jnp.dot(scaled, plain_ref[1], preferred_element_type=F32)
         part = product if part is None else part + product
     out_ref[...] = part.reshape(PEERS, LANES, LANES).astype(BF16)
 
@@ -219,15 +224,16 @@
     )
     mine = exchange(plain_two, RING)
     strip = jnp.stack(turned(unit_one, ALONG_X))
+    half = pltpu.VMEM((SIDE, HALF), F32)
+    blocks = pltpu.VMEM((PEERS, LANES, LANES), BF16)
+    work = dict(flops=2 * SIDE * HALF * LANES, exps=SIDE * HALF)
+    mine = call(unit_kernel, pltpu.VMEM((2, HALF, LANES), BF16), near(mine), flops=FLOPS_HINT)
     mine, *units_left = lax.optimization_barrier((mine, *turned(strip, ALONG_Y)))
     units_left = [near(part) for part in units_left]
-    other = lax.ppermute(mine, "c", SWAP)
-    half, units = pltpu.VMEM((SIDE, HALF), F32), pltpu.VMEM((HALF, LANES), BF16)
-    blocks = pltpu.VMEM((PEERS, LANES, LANES), BF16)
-    work = dict(flops=2 * SIDE * HALF * LANES, exps=SIDE * HALF)
-    mine, other = near(mine), near(other)
-    tile_mine, left, first = call(mine_kernel, (half, blocks, lines), *units_left, mine, scratch=(blocks, units), **work)
-    tile_other, sums = call(other_kernel, (half, short), near(left), other, near(first), scratch=(units, lines), **work)
+    other = near(lax.ppermute(mine, "c", SWAP))
+    mine = near(mine)
+    tile_mine, left, first = call(mine_kernel, (half, blocks, lines), *units_left, mine, scratch=(blocks,), **work)
+    tile_other, sums = call(other_kernel, (half, short), near(left), other, near(first), scratch=(lines,), **work)
     tile = (near(tile_mine), near(tile_other))
     for sweep in range(SWEEPS):
         if sweep:

time: 129 us -> 129 us (level)
    pallas_call x10 -> x11, Pallas kernels: 15.5 us -> 15.3 us  [call(): pl.pallas_call(kernel, out_shape=outs, **specs, scratch_shapes=scratch, c...]
  transfers between devices with their start and end apart: 8 -> 8, of which waited for: 4 -> 5; matrix products, arithmetic and copies ran while one was open for 0% -> 0% of each run, Pallas kernels for 1% -> 1%
where the time goes in v7:
time: 129 us
  blocking collectives  85.6 us (66%)
  starting transfers between devices  19.3 us (15%)
  Pallas kernels  15.3 us (12%)
  waiting for transfers between devices  8.24 us (6%)
    all_to_all x7, blocking collectives, exchange(): return lax.all_to_all(array, axes, 0, 0)  85.6 us
    pallas_call x11, Pallas kernels, call(): pl.pallas_call(kernel, out_shape=outs, **specs, scratch_shapes=scratch, c...  15.3 us
    all_to_all x1, starting transfers between devices, exchange(): return lax.all_to_all(array, axes, 0, 0)  9.03 us
    ppermute x6, waiting for transfers between devices, turned(): return [array] + [lax.ppermute(array, axes, swap) for swap in swaps]  8.1 us
    ppermute x6, starting transfers between devices, turned(): return [array] + [lax.ppermute(array, axes, swap) for swap in swaps]  6.74 us
    ppermute x1, starting transfers between devices, on_device(): other = near(lax.ppermute(mine, 'c', SWAP))  3.58 us
  transfers between devices with their start and end apart: 8, of which 5 were waited for; matrix products, arithmetic and copies ran while one was open for 0% of the time, Pallas kernels for 1%

profile of v7, /device:TPU:1, one launch (start us, length us, event | category | flops | bytes accessed | tf_op | source)
XLA Modules:
  0.0 128.6 jit_solution(12986633063451574342)
XLA Ops:
  0.0 3.0 %shard_map.46 = (bf16[128,128]{1,0:T(8,128)(2,1)S(1)}, bf16[8,128,128]{2,1,0:T(8,128)(2,1)}) custom-call(bf16[128,1536]{1,0:T(8,128)(2,1)} %one_hbm.1, bf16[128,1536]{1,0:T(8,128)(2,1)} %two_hbm.1, bf16[1536,512]{1,0:T(8,128)(2,1)} %first_hbm.1, bf16[512,128]{1,0:T(8,128)(2,1)} %second_hbm.1), custom_call_target="tpu_custom_call" | custom-call | flops 402653184 | bytes 2490368 | tf_op jit(solution)/shard_map/pallas_call | solution.py:181
  3.0 9.0 %all-to-all-start = ((bf16[8,128,128]{2,1,0:T(8,128)(2,1)}), bf16[8,128,128]{2,1,0:T(8,128)(2,1)S(1)}, u32[]{:S(2)}, u32[]{:S(2)}) async-start(bf16[8,128,128]{2,1,0:T(8,128)(2,1)} %get-tuple-element.21), calls=%async_computation | async-start | bytes 524288 | tf_op jit(solution)/shard_map/all_to_all | solution.py:196
  12.1 2.5 %collective-permute-start.2 = (bf16[128,128]{1,0:T(8,128)(2,1)S(1)}, bf16[128,128]{1,0:T(8,128)(2,1)S(1)}, u32[]{:S(2)}, u32[]{:S(2)}) collective-permute-start(bf16[128,128]{1,0:T(8,128)(2,1)S(1)} %get-tuple-element.22), channel_id=1, source_target_pairs={{0,192},{64,128},{128,64},{192,0},{1,193},{65,129},{129,65},{193,1... | collective-permute-start | bytes 98312 | tf_op jit(solution)/shard_map/ppermute | solution.py:201
  14.5 0.5 collective-permute-start.1
  15.0 0.3 collective-permute-start
  15.3 0.7 collective-permute-done.2
  16.0 2.9 %collective-permute-done.1 = bf16[128,128]{1,0:T(8,128)(2,1)S(1)} collective-permute-done((bf16[128,128]{1,0:T(8,128)(2,1)S(1)}, bf16[128,128]{1,0:T(8,128)(2,1)S(1)}, u32[]{:S(2)}, u32[]{:S(2)}) %collective-permute-start.1) | collective-permute-done | bytes 32800 | tf_op jit(solution)/shard_map/ppermute | solution.py:201
  18.9 0.0 collective-permute-done
  19.0 2.8 %collective-permute-start.5 = (bf16[4,128,128]{2,1,0:T(8,128)(2,1)S(1)}, bf16[4,128,128]{2,1,0:T(8,128)(2,1)S(1)}, u32[]{:S(2)}, u32[]{:S(2)}) collective-permute-start(bf16[4,128,128]{2,1,0:T(8,128)(2,1)S(1)} %pad_maximum_fusion.refs_0_), channel_id=1, source_target_pairs={{0,12},{4,8},{8,4},{12,0},{1,13},{5,9},{9,5},{13,1},{2,14},{6,10},... | collective-permute-start | bytes 393224 | tf_op jit(solution)/shard_map/ppermute | solution.py:201
  21.8 0.4 collective-permute-start.4
  22.1 0.3 collective-permute-start.3
  22.5 0.0 all-to-all-done.plain_ref
  22.5 0.3 shard_map.47.refs_4_.plain_mine_ref
  22.8 2.3 %collective-permute-done.5.refs_3_ = bf16[4,128,128]{2,1,0:T(8,128)(2,1)S(1)} collective-permute-done((bf16[4,128,128]{2,1,0:T(8,128)(2,1)S(1)}, bf16[4,128,128]{2,1,0:T(8,128)(2,1)S(1)}, u32[]{:S(2)}, u32[]{:S(2)}) %collective-permute-start.5) | collective-permute-done | bytes 131104 | tf_op jit(solution)/shard_map/ppermute | solution.py:201
  25.1 2.1 %collective-permute-done.4.refs_2_ = bf16[4,128,128]{2,1,0:T(8,128)(2,1)S(1)} collective-permute-done((bf16[4,128,128]{2,1,0:T(8,128)(2,1)S(1)}, bf16[4,128,128]{2,1,0:T(8,128)(2,1)S(1)}, u32[]{:S(2)}, u32[]{:S(2)}) %collective-permute-start.4) | collective-permute-done | bytes 131104 | tf_op jit(solution)/shard_map/ppermute | solution.py:201
  27.2 0.0 collective-permute-done.3.refs_1_
  27.2 3.6 %collective-permute-start.6 = (bf16[2,1024,128]{2,1,0:T(8,128)(2,1)S(1)}, bf16[2,1024,128]{2,1,0:T(8,128)(2,1)S(1)}, u32[]{:S(2)}, u32[]{:S(2)}) collective-permute-start(bf16[2,1024,128]{2,1,0:T(8,128)(2,1)S(1)} %shard_map.47.refs_4_.plain_mine_ref), channel_id=1, source_target_pairs={{0,16},{16,0},{1,17},{17,1},{2,18},{18,2},{3,19},{19,3},{4,20},{20... | collective-permute-start | bytes 1572872 | tf_op jit(solution)/shard_map/ppermute | solution.py:233
  30.8 1.4 %shard_map.48 = (f32[2048,1024]{1,0:T(8,128)S(1)}, bf16[16,128,128]{2,1,0:T(8,128)(2,1)S(1)}, f32[16,128]{1,0:T(8,128)S(1)}) custom-call(bf16[4,128,128]{2,1,0:T(8,128)(2,1)S(1)} %pad_maximum_fusion.refs_0_, bf16[4,128,128]{2,1,0:T(8,128)(2,1)S(1)} %collective-permute-done.3.refs_1_, bf16[4,128,128]{2,1,0:T(8,128)(2,1)S(1)} %collective-permute-done.4.refs_2_, ...), custom_call_target="tpu_custom_call" | custom-call | flops 536870912 | bytes 1048576 | tf_op jit(solution)/shard_map/pallas_call | solution.py:181
  32.2 0.1 collective-permute-done.6.rows_ref.plain_other_ref
  32.3 1.4 %shard_map.49 = (f32[2048,1024]{1,0:T(8,128)S(1)}, bf16[16,16,128]{2,1,0:T(8,128)(2,1)S(1)}) custom-call(bf16[16,128,128]{2,1,0:T(8,128)(2,1)S(1)} %get-tuple-element.28.left_ref, bf16[2,1024,128]{2,1,0:T(8,128)(2,1)S(1)} %collective-permute-done.6.rows_ref.plain_other_ref, f32[16,128]{1,0:T(8,128)S(1)} %get-tuple-element.29.first_ref), custom_call_target="tpu_custom_call" | custom-call | flops 536870912 | bytes 1056768 | tf_op jit(solution)/shard_map/pallas_call | solution.py:181
  33.7 11.0 %all_to_all.40.got_ref = bf16[16,16,128]{2,1,0:T(8,128)(2,1)S(1)} all-to-all(bf16[16,16,128]{2,1,0:T(8,128)(2,1)S(1)} %get-tuple-element.30), channel_id=1, replica_groups=mesh['xh'=2,'xl'=2,'zh'=2,'c'=2,'yh'=2,'yl'=2,'zm'=2,'zl'=2] {'xh','xl',..., dimensions={0} | all-to-all | bytes 131072 | tf_op jit(solution)/shard_map/all_to_all | solution.py:196
  44.8 1.2 shard_map.50
  46.0 16.6 %all_to_all.41.got_ref = bf16[16,16,128]{2,1,0:T(8,128)(2,1)S(1)} all-to-all(bf16[16,16,128]{2,1,0:T(8,128)(2,1)S(1)} %get-tuple-element.33), channel_id=1, replica_groups=mesh['xh'=2,'xl'=2,'zh'=2,'c'=2,'yh'=2,'yl'=2,'zm'=2,'zl'=2] {'zh','zm',..., dimensions={0} | all-to-all | bytes 131072 | tf_op jit(solution)/shard_map/all_to_all | solution.py:196
  62.6 1.2 shard_map.51
  63.8 9.5 %all_to_all.42.got_ref = bf16[16,16,128]{2,1,0:T(8,128)(2,1)S(1)} all-to-all(bf16[16,16,128]{2,1,0:T(8,128)(2,1)S(1)} %shard_map.51), channel_id=1, replica_groups=mesh['xh'=2,'xl'=2,'zh'=2,'c'=2,'yh'=2,'yl'=2,'zm'=2,'zl'=2] {'xh','xl',..., dimensions={0} | all-to-all | bytes 131072 | tf_op jit(solution)/shard_map/all_to_all | solution.py:196
  73.3 1.2 shard_map.52
  74.5 11.8 %all_to_all.43.got_ref = bf16[16,16,128]{2,1,0:T(8,128)(2,1)S(1)} all-to-all(bf16[16,16,128]{2,1,0:T(8,128)(2,1)S(1)} %get-tuple-element.34), channel_id=1, replica_groups=mesh['xh'=2,'xl'=2,'zh'=2,'c'=2,'yh'=2,'yl'=2,'zm'=2,'zl'=2] {'zh','zm',..., dimensions={0} | all-to-all | bytes 131072 | tf_op jit(solution)/shard_map/all_to_all | solution.py:196
  86.4 1.2 shard_map.53
  87.6 9.5 %all_to_all.44.got_ref = bf16[16,16,128]{2,1,0:T(8,128)(2,1)S(1)} all-to-all(bf16[16,16,128]{2,1,0:T(8,128)(2,1)S(1)} %shard_map.53), channel_id=1, replica_groups=mesh['xh'=2,'xl'=2,'zh'=2,'c'=2,'yh'=2,'yl'=2,'zm'=2,'zl'=2] {'xh','xl',..., dimensions={0} | all-to-all | bytes 131072 | tf_op jit(solution)/shard_map/all_to_all | solution.py:196
  97.0 1.2 shard_map.54
  98.3 13.2 %all_to_all.45.got_ref = f32[16,16,128]{2,1,0:T(8,128)S(1)} all-to-all(f32[16,16,128]{2,1,0:T(8,128)S(1)} %get-tuple-element.35), channel_id=1, replica_groups=mesh['xh'=2,'xl'=2,'zh'=2,'c'=2,'yh'=2,'yl'=2,'zm'=2,'zl'=2] {'zh','zm',..., dimensions={0} | all-to-all | bytes 262144 | tf_op jit(solution)/shard_map/all_to_all | solution.py:196
  111.5 2.4 %shard_map.55 = bf16[16,128,128]{2,1,0:T(8,128)(2,1)S(1)} custom-call(f32[16,16,128]{2,1,0:T(8,128)S(1)} %all_to_all.45.got_ref, f32[2048,1024]{1,0:T(8,128)S(1)} %get-tuple-element.31.mine_ref, f32[2048,1024]{1,0:T(8,128)S(1)} %get-tuple-element.32.other_ref, bf16[2,1024,128]{2,1,0:T(8,128)(2,1)S(1)} %shard_map.47.refs_4_.plain_mine_ref, ...), custom_call_target="tpu_custom_call" | custom-call | bytes 17956864 | tf_op jit(solution)/shard_map/pallas_call | solution.py:181
  113.8 14.0 %all_to_all.46.got_ref = bf16[16,128,128]{2,1,0:T(8,128)(2,1)S(1)} all-to-all(bf16[16,128,128]{2,1,0:T(8,128)(2,1)S(1)} %shard_map.55), channel_id=1, replica_groups=mesh['xh'=2,'xl'=2,'zh'=2,'c'=2,'yh'=2,'yl'=2,'zm'=2,'zl'=2] {'xh','xl',..., dimensions={0} | all-to-all | bytes 1048576 | tf_op jit(solution)/shard_map/all_to_all | solution.py:196
  127.9 0.7 shard_map.56
  (1 shorter events, 0.0 us)
Async XLA Ops:
  3.0 19.4 %all-to-all-start = ((bf16[8,128,128]{2,1,0:T(8,128)(2,1)}), bf16[8,128,128]{2,1,0:T(8,128)(2,1)S(1)}, u32[]{:S(2)}, u32[]{:S(2)}) async-start(bf16[8,128,128]{2,1,0:T(8,128)(2,1)} %get-tuple-element.21), calls=%async_computation | async-start | bytes 524288 | tf_op jit(solution)/shard_map/all_to_all | solution.py:196
  12.1 4.0 %collective-permute-start.2 = (bf16[128,128]{1,0:T(8,128)(2,1)S(1)}, bf16[128,128]{1,0:T(8,128)(2,1)S(1)}, u32[]{:S(2)}, u32[]{:S(2)}) collective-permute-start(bf16[128,128]{1,0:T(8,128)(2,1)S(1)} %get-tuple-element.22), channel_id=1, source_target_pairs={{0,192},{64,128},{128,64},{192,0},{1,193},{65,129},{129,65},{193,1... | collective-permute-start | bytes 98312 | tf_op jit(solution)/shard_map/ppermute | solution.py:201
  14.5 4.4 %collective-permute-start.1 = (bf16[128,128]{1,0:T(8,128)(2,1)S(1)}, bf16[128,128]{1,0:T(8,128)(2,1)S(1)}, u32[]{:S(2)}, u32[]{:S(2)}) collective-permute-start(bf16[128,128]{1,0:T(8,128)(2,1)S(1)} %get-tuple-element.22), channel_id=1, source_target_pairs={{0,128},{64,192},{128,0},{192,64},{1,129},{65,193},{129,1},{193,65... | collective-permute-start | bytes 98312 | tf_op jit(solution)/shard_map/ppermute | solution.py:201
  15.0 3.9 %collective-permute-start = (bf16[128,128]{1,0:T(8,128)(2,1)S(1)}, bf16[128,128]{1,0:T(8,128)(2,1)S(1)}, u32[]{:S(2)}, u32[]{:S(2)}) collective-permute-start(bf16[128,128]{1,0:T(8,128)(2,1)S(1)} %get-tuple-element.22), channel_id=1, source_target_pairs={{0,64},{64,0},{128,192},{192,128},{1,65},{65,1},{129,193},{193,129... | collective-permute-start | bytes 98312 | tf_op jit(solution)/shard_map/ppermute | solution.py:201
  19.0 6.1 %collective-permute-start.5 = (bf16[4,128,128]{2,1,0:T(8,128)(2,1)S(1)}, bf16[4,128,128]{2,1,0:T(8,128)(2,1)S(1)}, u32[]{:S(2)}, u32[]{:S(2)}) collective-permute-start(bf16[4,128,128]{2,1,0:T(8,128)(2,1)S(1)} %pad_maximum_fusion.refs_0_), channel_id=1, source_target_pairs={{0,12},{4,8},{8,4},{12,0},{1,13},{5,9},{9,5},{13,1},{2,14},{6,10},... | collective-permute-start | bytes 393224 | tf_op jit(solution)/shard_map/ppermute | solution.py:201
  21.8 5.4 %collective-permute-start.4 = (bf16[4,128,128]{2,1,0:T(8,128)(2,1)S(1)}, bf16[4,128,128]{2,1,0:T(8,128)(2,1)S(1)}, u32[]{:S(2)}, u32[]{:S(2)}) collective-permute-start(bf16[4,128,128]{2,1,0:T(8,128)(2,1)S(1)} %pad_maximum_fusion.refs_0_), channel_id=1, source_target_pairs={{0,8},{4,12},{8,0},{12,4},{1,9},{5,13},{9,1},{13,5},{2,10},{6,14},... | collective-permute-start | bytes 393224 | tf_op jit(solution)/shard_map/ppermute | solution.py:201
  22.1 5.1 %collective-permute-start.3 = (bf16[4,128,128]{2,1,0:T(8,128)(2,1)S(1)}, bf16[4,128,128]{2,1,0:T(8,128)(2,1)S(1)}, u32[]{:S(2)}, u32[]{:S(2)}) collective-permute-start(bf16[4,128,128]{2,1,0:T(8,128)(2,1)S(1)} %pad_maximum_fusion.refs_0_), channel_id=1, source_target_pairs={{0,4},{4,0},{8,12},{12,8},{1,5},{5,1},{9,13},{13,9},{2,6},{6,2},{1... | collective-permute-start | bytes 393224 | tf_op jit(solution)/shard_map/ppermute | solution.py:201
  27.2 5.1 %collective-permute-start.6 = (bf16[2,1024,128]{2,1,0:T(8,128)(2,1)S(1)}, bf16[2,1024,128]{2,1,0:T(8,128)(2,1)S(1)}, u32[]{:S(2)}, u32[]{:S(2)}) collective-permute-start(bf16[2,1024,128]{2,1,0:T(8,128)(2,1)S(1)} %shard_map.47.refs_4_.plain_mine_ref), channel_id=1, source_target_pairs={{0,16},{16,0},{1,17},{17,1},{2,18},{18,2},{3,19},{19,3},{4,20},{20... | collective-permute-start | bytes 1572872 | tf_op jit(solution)/shard_map/ppermute | solution.py:233

commit v8 on v7

--- a/solution.py
+++ b/solution.py
@@ -19,8 +19,8 @@
 SAME_ROWS = ("xh", "xl", "yh", "yl")
 ALONG_X, ALONG_Y = SAME_ROWS[:2], SAME_ROWS[2:]
 SIDES = 4
-SAME_COLS = ("zh", "zm", "zl", "c")
-RING = SAME_COLS[:3]
+SAME_COLS = ("c", "zh", "zm", "zl")
+RING = SAME_COLS[1:]
 HALF = SIDE // 2
 SWAP = [(0, 1), (1, 0)]
 F32, BF16 = jnp.float32, jnp.bfloat16

time: 129 us -> 127 us (0.984); the launches traced: 129 us -> 125 us
  blocking collectives: 85.6 us -> 81.8 us
    all_to_all x7, blocking collectives: 85.6 us -> 81.8 us  [exchange(): return lax.all_to_all(array, axes, 0, 0)]
where the time goes in v8:
time: 127 us; the launch traced here: 125 us
  blocking collectives  81.8 us (64%)
  starting transfers between devices  19.3 us (15%)
  Pallas kernels  15.3 us (12%)
  waiting for transfers between devices  8.24 us (6%)
    all_to_all x7, blocking collectives, exchange(): return lax.all_to_all(array, axes, 0, 0)  81.8 us
    pallas_call x11, Pallas kernels, call(): pl.pallas_call(kernel, out_shape=outs, **specs, scratch_shapes=scratch, c...  15.3 us
    all_to_all x1, starting transfers between devices, exchange(): return lax.all_to_all(array, axes, 0, 0)  9.03 us
    ppermute x6, waiting for transfers between devices, turned(): return [array] + [lax.ppermute(array, axes, swap) for swap in swaps]  8.1 us
    ppermute x6, starting transfers between devices, turned(): return [array] + [lax.ppermute(array, axes, swap) for swap in swaps]  6.74 us
    ppermute x1, starting transfers between devices, on_device(): other = near(lax.ppermute(mine, 'c', SWAP))  3.58 us
  transfers between devices with their start and end apart: 8, of which 5 were waited for; matrix products, arithmetic and copies ran while one was open for 0% of the time, Pallas kernels for 1%

profile of v8, /device:TPU:1, one launch (start us, length us, event | category | flops | bytes accessed | tf_op | source)
XLA Modules:
  0.0 124.8 jit_solution(13014484699569432159)
XLA Ops:
  0.0 3.0 %shard_map.46 = (bf16[128,128]{1,0:T(8,128)(2,1)S(1)}, bf16[8,128,128]{2,1,0:T(8,128)(2,1)}) custom-call(bf16[128,1536]{1,0:T(8,128)(2,1)} %one_hbm.1, bf16[128,1536]{1,0:T(8,128)(2,1)} %two_hbm.1, bf16[1536,512]{1,0:T(8,128)(2,1)} %first_hbm.1, bf16[512,128]{1,0:T(8,128)(2,1)} %second_hbm.1), custom_call_target="tpu_custom_call" | custom-call | flops 402653184 | bytes 2490368 | tf_op jit(solution)/shard_map/pallas_call | solution.py:181
  3.0 9.0 %all-to-all-start = ((bf16[8,128,128]{2,1,0:T(8,128)(2,1)}), bf16[8,128,128]{2,1,0:T(8,128)(2,1)S(1)}, u32[]{:S(2)}, u32[]{:S(2)}) async-start(bf16[8,128,128]{2,1,0:T(8,128)(2,1)} %get-tuple-element.21), calls=%async_computation | async-start | bytes 524288 | tf_op jit(solution)/shard_map/all_to_all | solution.py:196
  12.1 2.5 %collective-permute-start.2 = (bf16[128,128]{1,0:T(8,128)(2,1)S(1)}, bf16[128,128]{1,0:T(8,128)(2,1)S(1)}, u32[]{:S(2)}, u32[]{:S(2)}) collective-permute-start(bf16[128,128]{1,0:T(8,128)(2,1)S(1)} %get-tuple-element.22), channel_id=1, source_target_pairs={{0,192},{64,128},{128,64},{192,0},{1,193},{65,129},{129,65},{193,1... | collective-permute-start | bytes 98312 | tf_op jit(solution)/shard_map/ppermute | solution.py:201
  14.5 0.5 collective-permute-start.1
  15.0 0.3 collective-permute-start
  15.3 0.7 collective-permute-done.2
  16.0 2.9 %collective-permute-done.1 = bf16[128,128]{1,0:T(8,128)(2,1)S(1)} collective-permute-done((bf16[128,128]{1,0:T(8,128)(2,1)S(1)}, bf16[128,128]{1,0:T(8,128)(2,1)S(1)}, u32[]{:S(2)}, u32[]{:S(2)}) %collective-permute-start.1) | collective-permute-done | bytes 32800 | tf_op jit(solution)/shard_map/ppermute | solution.py:201
  18.9 0.0 collective-permute-done
  19.0 2.8 %collective-permute-start.5 = (bf16[4,128,128]{2,1,0:T(8,128)(2,1)S(1)}, bf16[4,128,128]{2,1,0:T(8,128)(2,1)S(1)}, u32[]{:S(2)}, u32[]{:S(2)}) collective-permute-start(bf16[4,128,128]{2,1,0:T(8,128)(2,1)S(1)} %pad_maximum_fusion.refs_0_), channel_id=1, source_target_pairs={{0,12},{4,8},{8,4},{12,0},{1,13},{5,9},{9,5},{13,1},{2,14},{6,10},... | collective-permute-start | bytes 393224 | tf_op jit(solution)/shard_map/ppermute | solution.py:201
  21.8 0.4 collective-permute-start.4
  22.1 0.3 collective-permute-start.3
  22.5 0.0 all-to-all-done.plain_ref
  22.5 0.3 shard_map.47.refs_4_.plain_mine_ref
  22.8 2.3 %collective-permute-done.5.refs_3_ = bf16[4,128,128]{2,1,0:T(8,128)(2,1)S(1)} collective-permute-done((bf16[4,128,128]{2,1,0:T(8,128)(2,1)S(1)}, bf16[4,128,128]{2,1,0:T(8,128)(2,1)S(1)}, u32[]{:S(2)}, u32[]{:S(2)}) %collective-permute-start.5) | collective-permute-done | bytes 131104 | tf_op jit(solution)/shard_map/ppermute | solution.py:201
  25.1 2.1 %collective-permute-done.4.refs_2_ = bf16[4,128,128]{2,1,0:T(8,128)(2,1)S(1)} collective-permute-done((bf16[4,128,128]{2,1,0:T(8,128)(2,1)S(1)}, bf16[4,128,128]{2,1,0:T(8,128)(2,1)S(1)}, u32[]{:S(2)}, u32[]{:S(2)}) %collective-permute-start.4) | collective-permute-done | bytes 131104 | tf_op jit(solution)/shard_map/ppermute | solution.py:201
  27.2 0.0 collective-permute-done.3.refs_1_
  27.2 3.6 %collective-permute-start.6 = (bf16[2,1024,128]{2,1,0:T(8,128)(2,1)S(1)}, bf16[2,1024,128]{2,1,0:T(8,128)(2,1)S(1)}, u32[]{:S(2)}, u32[]{:S(2)}) collective-permute-start(bf16[2,1024,128]{2,1,0:T(8,128)(2,1)S(1)} %shard_map.47.refs_4_.plain_mine_ref), channel_id=1, source_target_pairs={{0,16},{16,0},{1,17},{17,1},{2,18},{18,2},{3,19},{19,3},{4,20},{20... | collective-permute-start | bytes 1572872 | tf_op jit(solution)/shard_map/ppermute | solution.py:233
  30.8 1.4 %shard_map.48 = (f32[2048,1024]{1,0:T(8,128)S(1)}, bf16[16,128,128]{2,1,0:T(8,128)(2,1)S(1)}, f32[16,128]{1,0:T(8,128)S(1)}) custom-call(bf16[4,128,128]{2,1,0:T(8,128)(2,1)S(1)} %pad_maximum_fusion.refs_0_, bf16[4,128,128]{2,1,0:T(8,128)(2,1)S(1)} %collective-permute-done.3.refs_1_, bf16[4,128,128]{2,1,0:T(8,128)(2,1)S(1)} %collective-permute-done.4.refs_2_, ...), custom_call_target="tpu_custom_call" | custom-call | flops 536870912 | bytes 1048576 | tf_op jit(solution)/shard_map/pallas_call | solution.py:181
  32.2 0.1 collective-permute-done.6.rows_ref.plain_other_ref
  32.3 1.4 %shard_map.49 = (f32[2048,1024]{1,0:T(8,128)S(1)}, bf16[16,16,128]{2,1,0:T(8,128)(2,1)S(1)}) custom-call(bf16[16,128,128]{2,1,0:T(8,128)(2,1)S(1)} %get-tuple-element.28.left_ref, bf16[2,1024,128]{2,1,0:T(8,128)(2,1)S(1)} %collective-permute-done.6.rows_ref.plain_other_ref, f32[16,128]{1,0:T(8,128)S(1)} %get-tuple-element.29.first_ref), custom_call_target="tpu_custom_call" | custom-call | flops 536870912 | bytes 1056768 | tf_op jit(solution)/shard_map/pallas_call | solution.py:181
  33.7 11.0 %all_to_all.40.got_ref = bf16[16,16,128]{2,1,0:T(8,128)(2,1)S(1)} all-to-all(bf16[16,16,128]{2,1,0:T(8,128)(2,1)S(1)} %get-tuple-element.30), channel_id=1, replica_groups=mesh['xh'=2,'xl'=2,'zh'=2,'c'=2,'yh'=2,'yl'=2,'zm'=2,'zl'=2] {'xh','xl',..., dimensions={0} | all-to-all | bytes 131072 | tf_op jit(solution)/shard_map/all_to_all | solution.py:196
  44.8 1.2 shard_map.50
  46.0 16.0 %all_to_all.41.got_ref = bf16[16,16,128]{2,1,0:T(8,128)(2,1)S(1)} all-to-all(bf16[16,16,128]{2,1,0:T(8,128)(2,1)S(1)} %get-tuple-element.33), channel_id=1, replica_groups=mesh['xh'=2,'xl'=2,'zh'=2,'c'=2,'yh'=2,'yl'=2,'zm'=2,'zl'=2] {'c','zh','..., dimensions={0} | all-to-all | bytes 131072 | tf_op jit(solution)/shard_map/all_to_all | solution.py:196
  62.0 1.2 shard_map.51
  63.2 9.5 %all_to_all.42.got_ref = bf16[16,16,128]{2,1,0:T(8,128)(2,1)S(1)} all-to-all(bf16[16,16,128]{2,1,0:T(8,128)(2,1)S(1)} %shard_map.51), channel_id=1, replica_groups=mesh['xh'=2,'xl'=2,'zh'=2,'c'=2,'yh'=2,'yl'=2,'zm'=2,'zl'=2] {'xh','xl',..., dimensions={0} | all-to-all | bytes 131072 | tf_op jit(solution)/shard_map/all_to_all | solution.py:196
  72.6 1.2 shard_map.52
  73.9 11.9 %all_to_all.43.got_ref = bf16[16,16,128]{2,1,0:T(8,128)(2,1)S(1)} all-to-all(bf16[16,16,128]{2,1,0:T(8,128)(2,1)S(1)} %get-tuple-element.34), channel_id=1, replica_groups=mesh['xh'=2,'xl'=2,'zh'=2,'c'=2,'yh'=2,'yl'=2,'zm'=2,'zl'=2] {'c','zh','..., dimensions={0} | all-to-all | bytes 131072 | tf_op jit(solution)/shard_map/all_to_all | solution.py:196
  85.8 1.2 shard_map.53
  87.0 9.5 %all_to_all.44.got_ref = bf16[16,16,128]{2,1,0:T(8,128)(2,1)S(1)} all-to-all(bf16[16,16,128]{2,1,0:T(8,128)(2,1)S(1)} %shard_map.53), channel_id=1, replica_groups=mesh['xh'=2,'xl'=2,'zh'=2,'c'=2,'yh'=2,'yl'=2,'zm'=2,'zl'=2] {'xh','xl',..., dimensions={0} | all-to-all | bytes 131072 | tf_op jit(solution)/shard_map/all_to_all | solution.py:196
  96.5 1.2 shard_map.54
  97.8 12.1 %all_to_all.45.got_ref = f32[16,16,128]{2,1,0:T(8,128)S(1)} all-to-all(f32[16,16,128]{2,1,0:T(8,128)S(1)} %get-tuple-element.35), channel_id=1, replica_groups=mesh['xh'=2,'xl'=2,'zh'=2,'c'=2,'yh'=2,'yl'=2,'zm'=2,'zl'=2] {'c','zh','..., dimensions={0} | all-to-all | bytes 262144 | tf_op jit(solution)/shard_map/all_to_all | solution.py:196
  109.9 2.4 %shard_map.55 = bf16[16,128,128]{2,1,0:T(8,128)(2,1)S(1)} custom-call(f32[16,16,128]{2,1,0:T(8,128)S(1)} %all_to_all.45.got_ref, f32[2048,1024]{1,0:T(8,128)S(1)} %get-tuple-element.31.mine_ref, f32[2048,1024]{1,0:T(8,128)S(1)} %get-tuple-element.32.other_ref, bf16[2,1024,128]{2,1,0:T(8,128)(2,1)S(1)} %shard_map.47.refs_4_.plain_mine_ref, ...), custom_call_target="tpu_custom_call" | custom-call | bytes 17956864 | tf_op jit(solution)/shard_map/pallas_call | solution.py:181
  112.2 11.9 %all_to_all.46.got_ref = bf16[16,128,128]{2,1,0:T(8,128)(2,1)S(1)} all-to-all(bf16[16,128,128]{2,1,0:T(8,128)(2,1)S(1)} %shard_map.55), channel_id=1, replica_groups=mesh['xh'=2,'xl'=2,'zh'=2,'c'=2,'yh'=2,'yl'=2,'zm'=2,'zl'=2] {'xh','xl',..., dimensions={0} | all-to-all | bytes 1048576 | tf_op jit(solution)/shard_map/all_to_all | solution.py:196
  124.1 0.7 shard_map.56
  (1 shorter events, 0.0 us)
Async XLA Ops:
  3.0 19.4 %all-to-all-start = ((bf16[8,128,128]{2,1,0:T(8,128)(2,1)}), bf16[8,128,128]{2,1,0:T(8,128)(2,1)S(1)}, u32[]{:S(2)}, u32[]{:S(2)}) async-start(bf16[8,128,128]{2,1,0:T(8,128)(2,1)} %get-tuple-element.21), calls=%async_computation | async-start | bytes 524288 | tf_op jit(solution)/shard_map/all_to_all | solution.py:196
  12.1 4.0 %collective-permute-start.2 = (bf16[128,128]{1,0:T(8,128)(2,1)S(1)}, bf16[128,128]{1,0:T(8,128)(2,1)S(1)}, u32[]{:S(2)}, u32[]{:S(2)}) collective-permute-start(bf16[128,128]{1,0:T(8,128)(2,1)S(1)} %get-tuple-element.22), channel_id=1, source_target_pairs={{0,192},{64,128},{128,64},{192,0},{1,193},{65,129},{129,65},{193,1... | collective-permute-start | bytes 98312 | tf_op jit(solution)/shard_map/ppermute | solution.py:201
  14.5 4.4 %collective-permute-start.1 = (bf16[128,128]{1,0:T(8,128)(2,1)S(1)}, bf16[128,128]{1,0:T(8,128)(2,1)S(1)}, u32[]{:S(2)}, u32[]{:S(2)}) collective-permute-start(bf16[128,128]{1,0:T(8,128)(2,1)S(1)} %get-tuple-element.22), channel_id=1, source_target_pairs={{0,128},{64,192},{128,0},{192,64},{1,129},{65,193},{129,1},{193,65... | collective-permute-start | bytes 98312 | tf_op jit(solution)/shard_map/ppermute | solution.py:201
  15.0 3.9 %collective-permute-start = (bf16[128,128]{1,0:T(8,128)(2,1)S(1)}, bf16[128,128]{1,0:T(8,128)(2,1)S(1)}, u32[]{:S(2)}, u32[]{:S(2)}) collective-permute-start(bf16[128,128]{1,0:T(8,128)(2,1)S(1)} %get-tuple-element.22), channel_id=1, source_target_pairs={{0,64},{64,0},{128,192},{192,128},{1,65},{65,1},{129,193},{193,129... | collective-permute-start | bytes 98312 | tf_op jit(solution)/shard_map/ppermute | solution.py:201
  19.0 6.1 %collective-permute-start.5 = (bf16[4,128,128]{2,1,0:T(8,128)(2,1)S(1)}, bf16[4,128,128]{2,1,0:T(8,128)(2,1)S(1)}, u32[]{:S(2)}, u32[]{:S(2)}) collective-permute-start(bf16[4,128,128]{2,1,0:T(8,128)(2,1)S(1)} %pad_maximum_fusion.refs_0_), channel_id=1, source_target_pairs={{0,12},{4,8},{8,4},{12,0},{1,13},{5,9},{9,5},{13,1},{2,14},{6,10},... | collective-permute-start | bytes 393224 | tf_op jit(solution)/shard_map/ppermute | solution.py:201
  21.8 5.4 %collective-permute-start.4 = (bf16[4,128,128]{2,1,0:T(8,128)(2,1)S(1)}, bf16[4,128,128]{2,1,0:T(8,128)(2,1)S(1)}, u32[]{:S(2)}, u32[]{:S(2)}) collective-permute-start(bf16[4,128,128]{2,1,0:T(8,128)(2,1)S(1)} %pad_maximum_fusion.refs_0_), channel_id=1, source_target_pairs={{0,8},{4,12},{8,0},{12,4},{1,9},{5,13},{9,1},{13,5},{2,10},{6,14},... | collective-permute-start | bytes 393224 | tf_op jit(solution)/shard_map/ppermute | solution.py:201
  22.1 5.1 %collective-permute-start.3 = (bf16[4,128,128]{2,1,0:T(8,128)(2,1)S(1)}, bf16[4,128,128]{2,1,0:T(8,128)(2,1)S(1)}, u32[]{:S(2)}, u32[]{:S(2)}) collective-permute-start(bf16[4,128,128]{2,1,0:T(8,128)(2,1)S(1)} %pad_maximum_fusion.refs_0_), channel_id=1, source_target_pairs={{0,4},{4,0},{8,12},{12,8},{1,5},{5,1},{9,13},{13,9},{2,6},{6,2},{1... | collective-permute-start | bytes 393224 | tf_op jit(solution)/shard_map/ppermute | solution.py:201
  27.2 5.1 %collective-permute-start.6 = (bf16[2,1024,128]{2,1,0:T(8,128)(2,1)S(1)}, bf16[2,1024,128]{2,1,0:T(8,128)(2,1)S(1)}, u32[]{:S(2)}, u32[]{:S(2)}) collective-permute-start(bf16[2,1024,128]{2,1,0:T(8,128)(2,1)S(1)} %shard_map.47.refs_4_.plain_mine_ref), channel_id=1, source_target_pairs={{0,16},{16,0},{1,17},{17,1},{2,18},{18,2},{3,19},{19,3},{4,20},{20... | collective-permute-start | bytes 1572872 | tf_op jit(solution)/shard_map/ppermute | solution.py:233

commit v9 on v8

--- a/solution.py
+++ b/solution.py
@@ -238,10 +238,10 @@
     for sweep in range(SWEEPS):
         if sweep:
             sums = call(rows_kernel, short, sums, *tile, scratch=(lines,))
-        sums = near(exchange(sums, SAME_ROWS))
+        sums = near(exchange(sums, ALONG_Y + ALONG_X))
         totals = wide if sweep == SWEEPS - 1 else short
         sums, row_scale = call(cols_kernel, (totals, lines), sums, *tile, scratch=(lines,))
-        sums = near(exchange(sums, SAME_COLS))
+        sums = near(exchange(sums, ("c", "zm", "zh", "zl")))
     parts = call(map_kernel, blocks, sums, *tile, mine, other, scratch=(lines,))
     parts = near(exchange(parts, SAME_ROWS))
     return call(finish_kernel, jax.ShapeDtypeStruct((LANES, LANES), F32), parts, row_scale)

time: 127 us -> 127 us (level)
  no operation moved by 1% of the time
where the time goes in v9:
time: 127 us; the launch traced here: 125 us
  blocking collectives  81.8 us (64%)
  starting transfers between devices  19.3 us (15%)
  Pallas kernels  15.3 us (12%)
  waiting for transfers between devices  8.24 us (6%)
    all_to_all x7, blocking collectives, exchange(): return lax.all_to_all(array, axes, 0, 0)  81.8 us
    pallas_call x11, Pallas kernels, call(): pl.pallas_call(kernel, out_shape=outs, **specs, scratch_shapes=scratch, c...  15.3 us
    all_to_all x1, starting transfers between devices, exchange(): return lax.all_to_all(array, axes, 0, 0)  9.03 us
    ppermute x6, waiting for transfers between devices, turned(): return [array] + [lax.ppermute(array, axes, swap) for swap in swaps]  8.1 us
    ppermute x6, starting transfers between devices, turned(): return [array] + [lax.ppermute(array, axes, swap) for swap in swaps]  6.74 us
    ppermute x1, starting transfers between devices, on_device(): other = near(lax.ppermute(mine, 'c', SWAP))  3.58 us
  transfers between devices with their start and end apart: 8, of which 5 were waited for; matrix products, arithmetic and copies ran while one was open for 0% of the time, Pallas kernels for 1%

profile of v9, /device:TPU:1, one launch (start us, length us, event | category | flops | bytes accessed | tf_op | source)
XLA Modules:
  0.0 124.8 jit_solution(14225192967569895956)
XLA Ops:
  0.0 3.0 %shard_map.46 = (bf16[128,128]{1,0:T(8,128)(2,1)S(1)}, bf16[8,128,128]{2,1,0:T(8,128)(2,1)}) custom-call(bf16[128,1536]{1,0:T(8,128)(2,1)} %one_hbm.1, bf16[128,1536]{1,0:T(8,128)(2,1)} %two_hbm.1, bf16[1536,512]{1,0:T(8,128)(2,1)} %first_hbm.1, bf16[512,128]{1,0:T(8,128)(2,1)} %second_hbm.1), custom_call_target="tpu_custom_call" | custom-call | flops 402653184 | bytes 2490368 | tf_op jit(solution)/shard_map/pallas_call | solution.py:181
  3.0 9.0 %all-to-all-start = ((bf16[8,128,128]{2,1,0:T(8,128)(2,1)}), bf16[8,128,128]{2,1,0:T(8,128)(2,1)S(1)}, u32[]{:S(2)}, u32[]{:S(2)}) async-start(bf16[8,128,128]{2,1,0:T(8,128)(2,1)} %get-tuple-element.21), calls=%async_computation | async-start | bytes 524288 | tf_op jit(solution)/shard_map/all_to_all | solution.py:196
  12.1 2.5 %collective-permute-start.2 = (bf16[128,128]{1,0:T(8,128)(2,1)S(1)}, bf16[128,128]{1,0:T(8,128)(2,1)S(1)}, u32[]{:S(2)}, u32[]{:S(2)}) collective-permute-start(bf16[128,128]{1,0:T(8,128)(2,1)S(1)} %get-tuple-element.22), channel_id=1, source_target_pairs={{0,192},{64,128},{128,64},{192,0},{1,193},{65,129},{129,65},{193,1... | collective-permute-start | bytes 98312 | tf_op jit(solution)/shard_map/ppermute | solution.py:201
  14.5 0.5 collective-permute-start.1
  15.0 0.3 collective-permute-start
  15.3 0.7 collective-permute-done.2
  16.0 2.9 %collective-permute-done.1 = bf16[128,128]{1,0:T(8,128)(2,1)S(1)} collective-permute-done((bf16[128,128]{1,0:T(8,128)(2,1)S(1)}, bf16[128,128]{1,0:T(8,128)(2,1)S(1)}, u32[]{:S(2)}, u32[]{:S(2)}) %collective-permute-start.1) | collective-permute-done | bytes 32800 | tf_op jit(solution)/shard_map/ppermute | solution.py:201
  18.9 0.0 collective-permute-done
  19.0 2.8 %collective-permute-start.5 = (bf16[4,128,128]{2,1,0:T(8,128)(2,1)S(1)}, bf16[4,128,128]{2,1,0:T(8,128)(2,1)S(1)}, u32[]{:S(2)}, u32[]{:S(2)}) collective-permute-start(bf16[4,128,128]{2,1,0:T(8,128)(2,1)S(1)} %pad_maximum_fusion.refs_0_), channel_id=1, source_target_pairs={{0,12},{4,8},{8,4},{12,0},{1,13},{5,9},{9,5},{13,1},{2,14},{6,10},... | collective-permute-start | bytes 393224 | tf_op jit(solution)/shard_map/ppermute | solution.py:201
  21.8 0.4 collective-permute-start.4
  22.1 0.3 collective-permute-start.3
  22.5 0.0 all-to-all-done.plain_ref
  22.5 0.3 shard_map.47.refs_4_.plain_mine_ref
  22.8 2.3 %collective-permute-done.5.refs_3_ = bf16[4,128,128]{2,1,0:T(8,128)(2,1)S(1)} collective-permute-done((bf16[4,128,128]{2,1,0:T(8,128)(2,1)S(1)}, bf16[4,128,128]{2,1,0:T(8,128)(2,1)S(1)}, u32[]{:S(2)}, u32[]{:S(2)}) %collective-permute-start.5) | collective-permute-done | bytes 131104 | tf_op jit(solution)/shard_map/ppermute | solution.py:201
  25.1 2.1 %collective-permute-done.4.refs_2_ = bf16[4,128,128]{2,1,0:T(8,128)(2,1)S(1)} collective-permute-done((bf16[4,128,128]{2,1,0:T(8,128)(2,1)S(1)}, bf16[4,128,128]{2,1,0:T(8,128)(2,1)S(1)}, u32[]{:S(2)}, u32[]{:S(2)}) %collective-permute-start.4) | collective-permute-done | bytes 131104 | tf_op jit(solution)/shard_map/ppermute | solution.py:201
  27.2 0.0 collective-permute-done.3.refs_1_
  27.2 3.6 %collective-permute-start.6 = (bf16[2,1024,128]{2,1,0:T(8,128)(2,1)S(1)}, bf16[2,1024,128]{2,1,0:T(8,128)(2,1)S(1)}, u32[]{:S(2)}, u32[]{:S(2)}) collective-permute-start(bf16[2,1024,128]{2,1,0:T(8,128)(2,1)S(1)} %shard_map.47.refs_4_.plain_mine_ref), channel_id=1, source_target_pairs={{0,16},{16,0},{1,17},{17,1},{2,18},{18,2},{3,19},{19,3},{4,20},{20... | collective-permute-start | bytes 1572872 | tf_op jit(solution)/shard_map/ppermute | solution.py:233
  30.8 1.4 %shard_map.48 = (f32[2048,1024]{1,0:T(8,128)S(1)}, bf16[16,128,128]{2,1,0:T(8,128)(2,1)S(1)}, f32[16,128]{1,0:T(8,128)S(1)}) custom-call(bf16[4,128,128]{2,1,0:T(8,128)(2,1)S(1)} %pad_maximum_fusion.refs_0_, bf16[4,128,128]{2,1,0:T(8,128)(2,1)S(1)} %collective-permute-done.3.refs_1_, bf16[4,128,128]{2,1,0:T(8,128)(2,1)S(1)} %collective-permute-done.4.refs_2_, ...), custom_call_target="tpu_custom_call" | custom-call | flops 536870912 | bytes 1048576 | tf_op jit(solution)/shard_map/pallas_call | solution.py:181
  32.2 0.1 collective-permute-done.6.rows_ref.plain_other_ref
  32.3 1.4 %shard_map.49 = (f32[2048,1024]{1,0:T(8,128)S(1)}, bf16[16,16,128]{2,1,0:T(8,128)(2,1)S(1)}) custom-call(bf16[16,128,128]{2,1,0:T(8,128)(2,1)S(1)} %get-tuple-element.28.left_ref, bf16[2,1024,128]{2,1,0:T(8,128)(2,1)S(1)} %collective-permute-done.6.rows_ref.plain_other_ref, f32[16,128]{1,0:T(8,128)S(1)} %get-tuple-element.29.first_ref), custom_call_target="tpu_custom_call" | custom-call | flops 536870912 | bytes 1056768 | tf_op jit(solution)/shard_map/pallas_call | solution.py:181
  33.7 11.0 %all_to_all.40.got_ref = bf16[16,16,128]{2,1,0:T(8,128)(2,1)S(1)} all-to-all(bf16[16,16,128]{2,1,0:T(8,128)(2,1)S(1)} %get-tuple-element.30), channel_id=1, replica_groups=mesh['xh'=2,'xl'=2,'zh'=2,'c'=2,'yh'=2,'yl'=2,'zm'=2,'zl'=2] {'yh','yl',..., dimensions={0} | all-to-all | bytes 131072 | tf_op jit(solution)/shard_map/all_to_all | solution.py:196
  44.8 1.2 shard_map.50
  46.0 16.0 %all_to_all.41.got_ref = bf16[16,16,128]{2,1,0:T(8,128)(2,1)S(1)} all-to-all(bf16[16,16,128]{2,1,0:T(8,128)(2,1)S(1)} %get-tuple-element.33), channel_id=1, replica_groups=mesh['xh'=2,'xl'=2,'zh'=2,'c'=2,'yh'=2,'yl'=2,'zm'=2,'zl'=2] {'c','zm','..., dimensions={0} | all-to-all | bytes 131072 | tf_op jit(solution)/shard_map/all_to_all | solution.py:196
  62.0 1.2 shard_map.51
  63.2 9.4 %all_to_all.42.got_ref = bf16[16,16,128]{2,1,0:T(8,128)(2,1)S(1)} all-to-all(bf16[16,16,128]{2,1,0:T(8,128)(2,1)S(1)} %shard_map.51), channel_id=1, replica_groups=mesh['xh'=2,'xl'=2,'zh'=2,'c'=2,'yh'=2,'yl'=2,'zm'=2,'zl'=2] {'yh','yl',..., dimensions={0} | all-to-all | bytes 131072 | tf_op jit(solution)/shard_map/all_to_all | solution.py:196
  72.6 1.2 shard_map.52
  73.8 11.8 %all_to_all.43.got_ref = bf16[16,16,128]{2,1,0:T(8,128)(2,1)S(1)} all-to-all(bf16[16,16,128]{2,1,0:T(8,128)(2,1)S(1)} %get-tuple-element.34), channel_id=1, replica_groups=mesh['xh'=2,'xl'=2,'zh'=2,'c'=2,'yh'=2,'yl'=2,'zm'=2,'zl'=2] {'c','zm','..., dimensions={0} | all-to-all | bytes 131072 | tf_op jit(solution)/shard_map/all_to_all | solution.py:196
  85.6 1.2 shard_map.53
  86.9 9.4 %all_to_all.44.got_ref = bf16[16,16,128]{2,1,0:T(8,128)(2,1)S(1)} all-to-all(bf16[16,16,128]{2,1,0:T(8,128)(2,1)S(1)} %shard_map.53), channel_id=1, replica_groups=mesh['xh'=2,'xl'=2,'zh'=2,'c'=2,'yh'=2,'yl'=2,'zm'=2,'zl'=2] {'yh','yl',..., dimensions={0} | all-to-all | bytes 131072 | tf_op jit(solution)/shard_map/all_to_all | solution.py:196
  96.2 1.2 shard_map.54
  97.5 12.4 %all_to_all.45.got_ref = f32[16,16,128]{2,1,0:T(8,128)S(1)} all-to-all(f32[16,16,128]{2,1,0:T(8,128)S(1)} %get-tuple-element.35), channel_id=1, replica_groups=mesh['xh'=2,'xl'=2,'zh'=2,'c'=2,'yh'=2,'yl'=2,'zm'=2,'zl'=2] {'c','zm','..., dimensions={0} | all-to-all | bytes 262144 | tf_op jit(solution)/shard_map/all_to_all | solution.py:196
  109.9 2.4 %shard_map.55 = bf16[16,128,128]{2,1,0:T(8,128)(2,1)S(1)} custom-call(f32[16,16,128]{2,1,0:T(8,128)S(1)} %all_to_all.45.got_ref, f32[2048,1024]{1,0:T(8,128)S(1)} %get-tuple-element.31.mine_ref, f32[2048,1024]{1,0:T(8,128)S(1)} %get-tuple-element.32.other_ref, bf16[2,1024,128]{2,1,0:T(8,128)(2,1)S(1)} %shard_map.47.refs_4_.plain_mine_ref, ...), custom_call_target="tpu_custom_call" | custom-call | bytes 17956864 | tf_op jit(solution)/shard_map/pallas_call | solution.py:181
  112.2 11.8 %all_to_all.46.got_ref = bf16[16,128,128]{2,1,0:T(8,128)(2,1)S(1)} all-to-all(bf16[16,128,128]{2,1,0:T(8,128)(2,1)S(1)} %shard_map.55), channel_id=1, replica_groups=mesh['xh'=2,'xl'=2,'zh'=2,'c'=2,'yh'=2,'yl'=2,'zm'=2,'zl'=2] {'xh','xl',..., dimensions={0} | all-to-all | bytes 1048576 | tf_op jit(solution)/shard_map/all_to_all | solution.py:196
  124.1 0.7 shard_map.56
  (1 shorter events, 0.0 us)
Async XLA Ops:
  3.0 19.4 %all-to-all-start = ((bf16[8,128,128]{2,1,0:T(8,128)(2,1)}), bf16[8,128,128]{2,1,0:T(8,128)(2,1)S(1)}, u32[]{:S(2)}, u32[]{:S(2)}) async-start(bf16[8,128,128]{2,1,0:T(8,128)(2,1)} %get-tuple-element.21), calls=%async_computation | async-start | bytes 524288 | tf_op jit(solution)/shard_map/all_to_all | solution.py:196
  12.1 4.0 %collective-permute-start.2 = (bf16[128,128]{1,0:T(8,128)(2,1)S(1)}, bf16[128,128]{1,0:T(8,128)(2,1)S(1)}, u32[]{:S(2)}, u32[]{:S(2)}) collective-permute-start(bf16[128,128]{1,0:T(8,128)(2,1)S(1)} %get-tuple-element.22), channel_id=1, source_target_pairs={{0,192},{64,128},{128,64},{192,0},{1,193},{65,129},{129,65},{193,1... | collective-permute-start | bytes 98312 | tf_op jit(solution)/shard_map/ppermute | solution.py:201
  14.5 4.4 %collective-permute-start.1 = (bf16[128,128]{1,0:T(8,128)(2,1)S(1)}, bf16[128,128]{1,0:T(8,128)(2,1)S(1)}, u32[]{:S(2)}, u32[]{:S(2)}) collective-permute-start(bf16[128,128]{1,0:T(8,128)(2,1)S(1)} %get-tuple-element.22), channel_id=1, source_target_pairs={{0,128},{64,192},{128,0},{192,64},{1,129},{65,193},{129,1},{193,65... | collective-permute-start | bytes 98312 | tf_op jit(solution)/shard_map/ppermute | solution.py:201
  15.0 3.9 %collective-permute-start = (bf16[128,128]{1,0:T(8,128)(2,1)S(1)}, bf16[128,128]{1,0:T(8,128)(2,1)S(1)}, u32[]{:S(2)}, u32[]{:S(2)}) collective-permute-start(bf16[128,128]{1,0:T(8,128)(2,1)S(1)} %get-tuple-element.22), channel_id=1, source_target_pairs={{0,64},{64,0},{128,192},{192,128},{1,65},{65,1},{129,193},{193,129... | collective-permute-start | bytes 98312 | tf_op jit(solution)/shard_map/ppermute | solution.py:201
  19.0 6.1 %collective-permute-start.5 = (bf16[4,128,128]{2,1,0:T(8,128)(2,1)S(1)}, bf16[4,128,128]{2,1,0:T(8,128)(2,1)S(1)}, u32[]{:S(2)}, u32[]{:S(2)}) collective-permute-start(bf16[4,128,128]{2,1,0:T(8,128)(2,1)S(1)} %pad_maximum_fusion.refs_0_), channel_id=1, source_target_pairs={{0,12},{4,8},{8,4},{12,0},{1,13},{5,9},{9,5},{13,1},{2,14},{6,10},... | collective-permute-start | bytes 393224 | tf_op jit(solution)/shard_map/ppermute | solution.py:201
  21.8 5.4 %collective-permute-start.4 = (bf16[4,128,128]{2,1,0:T(8,128)(2,1)S(1)}, bf16[4,128,128]{2,1,0:T(8,128)(2,1)S(1)}, u32[]{:S(2)}, u32[]{:S(2)}) collective-permute-start(bf16[4,128,128]{2,1,0:T(8,128)(2,1)S(1)} %pad_maximum_fusion.refs_0_), channel_id=1, source_target_pairs={{0,8},{4,12},{8,0},{12,4},{1,9},{5,13},{9,1},{13,5},{2,10},{6,14},... | collective-permute-start | bytes 393224 | tf_op jit(solution)/shard_map/ppermute | solution.py:201
  22.1 5.1 %collective-permute-start.3 = (bf16[4,128,128]{2,1,0:T(8,128)(2,1)S(1)}, bf16[4,128,128]{2,1,0:T(8,128)(2,1)S(1)}, u32[]{:S(2)}, u32[]{:S(2)}) collective-permute-start(bf16[4,128,128]{2,1,0:T(8,128)(2,1)S(1)} %pad_maximum_fusion.refs_0_), channel_id=1, source_target_pairs={{0,4},{4,0},{8,12},{12,8},{1,5},{5,1},{9,13},{13,9},{2,6},{6,2},{1... | collective-permute-start | bytes 393224 | tf_op jit(solution)/shard_map/ppermute | solution.py:201
  27.2 5.1 %collective-permute-start.6 = (bf16[2,1024,128]{2,1,0:T(8,128)(2,1)S(1)}, bf16[2,1024,128]{2,1,0:T(8,128)(2,1)S(1)}, u32[]{:S(2)}, u32[]{:S(2)}) collective-permute-start(bf16[2,1024,128]{2,1,0:T(8,128)(2,1)S(1)} %shard_map.47.refs_4_.plain_mine_ref), channel_id=1, source_target_pairs={{0,16},{16,0},{1,17},{17,1},{2,18},{18,2},{3,19},{19,3},{4,20},{20... | collective-permute-start | bytes 1572872 | tf_op jit(solution)/shard_map/ppermute | solution.py:233
